TPU v7x, 32 devices: a whole 2x2x4 slice. The times are simulated.
32 devices in a mesh: dp: 4 (over z), row: 2 (over y), col: 4 (over x, core).
Axes of the slice: x: 2, y: 2, z: 4, core: 2. Of those that a mesh axis runs over, the one named last changes fastest.
Arguments:
- tokens: bfloat16 [16384, 2048], P(('dp', 'col'), 'row'), may hold values from -6 to 6
- norm1_gain: float32 [2048], P('row'), may hold values from 0.25 to 1.75
- w_query: bfloat16 [2048, 1280], P('row', 'col'), may hold values from -0.125 to 0.125
- w_key: bfloat16 [2048, 320], P('row', 'col'), may hold values from -0.125 to 0.125
- w_value: bfloat16 [2048, 320], P('row', 'col'), may hold values from -0.125 to 0.125
- query_gain: float32 [64], replicated, may hold values from 0.25 to 1.75
- key_gain: float32 [64], replicated, may hold values from 0.25 to 1.75
- w_out: bfloat16 [1280, 2048], P('col', 'row'), may hold values from -0.625 to 0.625
- norm2_gain: float32 [2048], P('row'), may hold values from 0.25 to 1.75
- w_gate: bfloat16 [2048, 5120], P('row', 'col'), may hold values from -0.125 to 0.125
- w_up: bfloat16 [2048, 5120], P('row', 'col'), may hold values from -0.125 to 0.125
- w_down: bfloat16 [5120, 2048], P('col', 'row'), may hold values from -0.078125 to 0.078125
- teacher: bfloat16 [16384, 2048], P(('dp', 'col'), 'row'), may hold values from -6 to 6
- positions: int32 [16384], P('dp'), may hold values from 0 to 3453, as said below
- token_count: int32 [1], replicated, may hold values from 8192 to 16384
Outputs:
- block_out: bfloat16 [16384, 2048], P(('dp', 'col'), 'row')
- grad_input: float32 [16384, 2048], P(('dp', 'col'), 'row')
- grad_norm1: float32 [2048], P('row')
- grad_query: float32 [2048, 1280], P('row', 'col')
- grad_key: float32 [2048, 320], P('row', 'col')
- grad_value: float32 [2048, 320], P('row', 'col')
- grad_query_gain: float32 [64], replicated
- grad_key_gain: float32 [64], replicated
- grad_out: float32 [1280, 2048], P('col', 'row')
- grad_norm2: float32 [2048], P('row')
- grad_gate: float32 [2048, 5120], P('row', 'col')
- grad_up: float32 [2048, 5120], P('row', 'col')
- grad_down: float32 [5120, 2048], P('col', 'row')
Inputs may be any that keep to these rules, and one draw needn't show every extreme that they name: Within each group of 2048 tokens the prompt's 1024 positions count up by one from a start of the group; each continuation's 128 positions count up by one from a start at or after the prompt's last position plus one.
All inputs are finite; a program needn't handle non-finite values.
Results may differ from a plain program's by a relative error of at most 0.015.
Values may be sent and summed in bfloat16 or wider, within the bound.
A program may use at most 320 MiB of HBM per device.

v0:
```python
import math

import jax
import jax.numpy as jnp
from jax import lax
from jax.sharding import PartitionSpec as P

D = 2048
QH = 20
KVH = 5
HD = 64
PROMPT = 1024
CONT = 128
NCONT = 8


EPSILON = 1e-06
NEG_FILL = -1e30


def head_norm(values, gain):
    return values * lax.rsqrt(jnp.mean(values * values, axis=-1, keepdims=True) + EPSILON) * gain


def rotate(values, places):
    half = values.shape[-1] // 2
    freq = jnp.exp(
        jnp.arange(half, dtype=jnp.float32) * (-2.0 * math.log(10000.0) / values.shape[-1])
    )
    angle = places.astype(jnp.float32)[:, None] * freq[None, :]
    cosine = jnp.cos(angle)[:, None, :]
    sine = jnp.sin(angle)[:, None, :]
    first = values[..., :half]
    second = values[..., half:]
    return jnp.concatenate(
        [first * cosine - second * sine, second * cosine + first * sine], axis=-1
    )


def allowed_keys(query_index, key_index):
    query_seg = jnp.where(query_index < PROMPT, -1, (query_index - PROMPT) // CONT)
    key_seg = jnp.where(key_index < PROMPT, -1, (key_index - PROMPT) // CONT)
    causal = key_index[None, :] <= query_index[:, None]
    visible = (key_index[None, :] < PROMPT) | (key_seg[None, :] == query_seg[:, None])
    return causal & visible


def width_mean(values):
    return lax.psum(jnp.sum(values, axis=1), "row") / D


def norm_back(states, inverse, gain, d_normed):
    return (
        inverse * gain * d_normed
        - states * inverse**3 * width_mean(states * gain * d_normed)[:, None]
    )


def col_to_row(local, weight):
    whole = lax.all_gather(local, "col", axis=0, tiled=True)
    mine = lax.all_to_all(whole, "row", split_axis=0, concat_axis=1, tiled=True)
    full_weight = lax.all_gather(weight, "row", axis=0, tiled=True)
    return (whole, jnp.dot(mine, full_weight, preferred_element_type=jnp.float32))


def row_to_col(local, weight, contract):
    whole = lax.all_gather(local, "row", axis=0, tiled=True)
    return (
        whole,
        lax.psum_scatter(
            lax.dot_general(
                whole, weight, (((1,), (contract,)), ((), ())), preferred_element_type=jnp.float32
            ),
            "col",
            scatter_dimension=0,
            tiled=True,
        ),
    )


def add_rows(accum, part, first):
    current = lax.dynamic_slice_in_dim(accum, first, part.shape[0], 0)
    return lax.dynamic_update_slice_in_dim(accum, current + part, first, 0)


def body(
    tokens,
    norm1_gain,
    w_query,
    w_key,
    w_value,
    query_gain,
    key_gain,
    w_out,
    norm2_gain,
    w_gate,
    w_up,
    w_down,
    teacher,
    positions,
    token_count,
):
    row_count = lax.axis_size("row")
    col_count = lax.axis_size("col")
    row_index = lax.axis_index("row")
    col_index = lax.axis_index("col")
    token_values = tokens.astype(jnp.float32)
    inverse_one = lax.rsqrt(width_mean(token_values * token_values) + EPSILON)[:, None]
    normed_one = (token_values * inverse_one * norm1_gain).astype(jnp.bfloat16)
    w_project = jnp.concatenate([w_query, w_key, w_value], axis=1)
    whole_first, projected = col_to_row(normed_one, w_project)
    query_width = w_query.shape[1]
    key_width = w_key.shape[1]
    query_raw = projected[:, :query_width]
    key_raw = projected[:, query_width : query_width + key_width]
    value_raw = projected[:, query_width + key_width :]
    my_rows = query_raw.shape[0]
    keys_all, values_all = (
        lax.all_gather(key_raw.astype(jnp.bfloat16)[None], ("row", "col"), axis=0, tiled=True),
        lax.all_gather(value_raw.astype(jnp.bfloat16)[None], ("row", "col"), axis=0, tiled=True),
    )

    def regroup(stacked):
        return (
            stacked.reshape(row_count, col_count, my_rows, key_width)
            .transpose(0, 2, 1, 3)
            .reshape(row_count * my_rows, col_count * key_width)
        )

    def spread(full):
        return (
            full.reshape(row_count, my_rows, col_count, key_width)
            .transpose(0, 2, 1, 3)
            .reshape(row_count * col_count, my_rows, key_width)
        )

    keys_all = regroup(keys_all)
    values_all = regroup(values_all)
    group_rows = keys_all.shape[0]
    local_heads = query_width // HD
    my_places = lax.dynamic_slice_in_dim(positions, row_index * my_rows, my_rows, 0)

    def prepare_query(raw, gain):
        return rotate(head_norm(raw.reshape(my_rows, local_heads, HD), gain), my_places)

    def prepare_key(raw, gain):
        return rotate(head_norm(raw.reshape(group_rows, KVH, HD), gain), positions)

    query_rot, query_back = jax.vjp(prepare_query, query_raw, query_gain)
    query_use = query_rot.astype(jnp.bfloat16)
    key_rot, key_back = jax.vjp(prepare_key, keys_all.astype(jnp.float32), key_gain)
    key_use = key_rot.astype(jnp.bfloat16)
    heads_global = col_index * local_heads + jnp.arange(local_heads)
    selector = (heads_global[:, None] // (QH // KVH) == jnp.arange(KVH)[None, :]).astype(
        jnp.bfloat16
    )
    key_heads = jnp.einsum(
        "tkd,hk->thd", key_use, selector, preferred_element_type=jnp.float32
    ).astype(jnp.bfloat16)
    value_heads = jnp.einsum(
        "tkd,hk->thd",
        values_all.reshape(group_rows, KVH, HD),
        selector,
        preferred_element_type=jnp.float32,
    ).astype(jnp.bfloat16)
    block = min(512, my_rows)
    block_count = my_rows // block
    group_len = PROMPT + NCONT * CONT
    scale = 1.0 / math.sqrt(HD)

    def scores_for(index):
        first = index * block
        query_block = lax.dynamic_slice_in_dim(query_use, first, block, 0)
        global_first = row_index * my_rows + first
        group_first = global_first // group_len * group_len
        local_first = global_first - group_first
        tail_first = jnp.maximum(local_first, PROMPT)
        key_block = jnp.concatenate(
            [
                lax.dynamic_slice_in_dim(key_heads, group_first, PROMPT, 0),
                lax.dynamic_slice_in_dim(key_heads, group_first + tail_first, block, 0),
            ],
            axis=0,
        )
        value_block = jnp.concatenate(
            [
                lax.dynamic_slice_in_dim(value_heads, group_first, PROMPT, 0),
                lax.dynamic_slice_in_dim(value_heads, group_first + tail_first, block, 0),
            ],
            axis=0,
        )
        key_index = jnp.concatenate([jnp.arange(PROMPT), tail_first + jnp.arange(block)])
        query_index = local_first + jnp.arange(block)
        raw = (
            jnp.einsum("qhd,khd->hqk", query_block, key_block, preferred_element_type=jnp.float32)
            * scale
        )
        scores = jnp.where(allowed_keys(query_index, key_index)[None], raw, NEG_FILL)
        return (query_block, key_block, value_block, group_first, tail_first, scores)

    def attend(index):
        query_block, key_block, value_block, group_first, tail_first, scores = scores_for(index)
        top = jnp.max(scores, axis=-1, keepdims=True)
        expo = jnp.exp(scores - top)
        total = jnp.sum(expo, axis=-1, keepdims=True)
        weights = (expo / total).astype(jnp.bfloat16)
        mixed = jnp.einsum("hqk,khd->qhd", weights, value_block, preferred_element_type=jnp.float32)
        return (mixed, top[..., 0] + jnp.log(total[..., 0]))

    mixed_blocks, log_totals = lax.map(attend, jnp.arange(block_count))
    attn_values = mixed_blocks.reshape(my_rows, query_width).astype(jnp.bfloat16)
    whole_attn, attn_out = row_to_col(attn_values, w_out, 0)
    hidden_state = token_values + attn_out
    inverse_two = lax.rsqrt(width_mean(hidden_state * hidden_state) + EPSILON)[:, None]
    normed_two = (hidden_state * inverse_two * norm2_gain).astype(jnp.bfloat16)
    w_gate_up = jnp.concatenate([w_gate, w_up], axis=1)
    whole_second, gate_up = col_to_row(normed_two, w_gate_up)
    ff_width = w_gate.shape[1]

    def swiglu(gate, up):
        return jax.nn.silu(gate) * up

    activated, swiglu_back = jax.vjp(swiglu, gate_up[:, :ff_width], gate_up[:, ff_width:])
    whole_act, ffn_out = row_to_col(activated.astype(jnp.bfloat16), w_down, 0)
    result = hidden_state + ffn_out
    block_out = result.astype(jnp.bfloat16)
    total_tokens = tokens.shape[0] * col_count * lax.axis_size("dp")
    loss_scale = total_tokens / token_count[0].astype(jnp.float32)
    d_result = loss_scale * (result - teacher.astype(jnp.float32))
    whole_dres, d_act = col_to_row(d_result.astype(jnp.bfloat16), w_down.T)
    grad_down = jnp.einsum("tf,td->fd", whole_act, whole_dres, preferred_element_type=jnp.float32)
    d_gate, d_up = swiglu_back(d_act)
    d_gate_up = jnp.concatenate([d_gate, d_up], axis=1).astype(jnp.bfloat16)
    whole_dgu, d_normed_two = row_to_col(d_gate_up, w_gate_up, 1)
    grad_gate_up = jnp.einsum(
        "td,tf->df", whole_second, whole_dgu, preferred_element_type=jnp.float32
    )
    d_hidden = d_result + norm_back(hidden_state, inverse_two, norm2_gain, d_normed_two)
    norm_two_part = jnp.sum(d_normed_two * hidden_state * inverse_two, axis=0)
    whole_dhid, d_attn = col_to_row(d_hidden.astype(jnp.bfloat16), w_out.T)
    grad_out = jnp.einsum("tf,td->fd", whole_attn, whole_dhid, preferred_element_type=jnp.float32)
    d_mixed = d_attn.astype(jnp.bfloat16).reshape(my_rows, local_heads, HD)

    def attend_back(carry, index):
        key_accum, value_accum = carry
        query_block, key_block, value_block, group_first, tail_first, scores = scores_for(index)
        probs = jnp.exp(scores - log_totals[index][..., None])
        d_block = lax.dynamic_slice_in_dim(d_mixed, index * block, block, 0)
        d_probs = jnp.einsum(
            "qhd,khd->hqk", d_block, value_block, preferred_element_type=jnp.float32
        )
        d_scores = (probs * (d_probs - jnp.sum(probs * d_probs, axis=-1, keepdims=True))).astype(
            jnp.bfloat16
        )
        value_part = jnp.einsum(
            "hqk,qhd->khd", probs.astype(jnp.bfloat16), d_block, preferred_element_type=jnp.float32
        )
        key_part = (
            jnp.einsum("hqk,qhd->khd", d_scores, query_block, preferred_element_type=jnp.float32)
            * scale
        )
        query_part = (
            jnp.einsum("hqk,khd->qhd", d_scores, key_block, preferred_element_type=jnp.float32)
            * scale
        )
        key_accum = add_rows(key_accum, key_part[:PROMPT], group_first)
        key_accum = add_rows(key_accum, key_part[PROMPT:], group_first + tail_first)
        value_accum = add_rows(value_accum, value_part[:PROMPT], group_first)
        value_accum = add_rows(value_accum, value_part[PROMPT:], group_first + tail_first)
        return ((key_accum, value_accum), query_part)

    zeros_heads = jnp.zeros((group_rows, local_heads, HD), jnp.float32)
    (d_key_heads, d_value_heads), d_query_blocks = lax.scan(
        attend_back, (zeros_heads, zeros_heads), jnp.arange(block_count)
    )
    d_query_raw, query_gain_part = query_back(d_query_blocks.reshape(my_rows, local_heads, HD))
    selector_wide = selector.astype(jnp.float32)
    d_key_use = jnp.einsum(
        "thd,hk->tkd", d_key_heads, selector_wide, precision=lax.Precision.HIGHEST
    )
    d_value_use = jnp.einsum(
        "thd,hk->tkd", d_value_heads, selector_wide, precision=lax.Precision.HIGHEST
    )
    d_keys_all, key_gain_part = key_back(d_key_use)
    d_key_mine, d_value_mine = (
        lax.psum_scatter(
            spread(d_keys_all).astype(jnp.bfloat16), ("row", "col"), scatter_dimension=0, tiled=True
        ).astype(jnp.float32),
        lax.psum_scatter(
            spread(d_value_use.reshape(group_rows, KVH * HD)).astype(jnp.bfloat16),
            ("row", "col"),
            scatter_dimension=0,
            tiled=True,
        ).astype(jnp.float32),
    )
    d_projected = jnp.concatenate([d_query_raw, d_key_mine[0], d_value_mine[0]], axis=1).astype(
        jnp.bfloat16
    )
    whole_dproj, d_normed_one = row_to_col(d_projected, w_project, 1)
    grad_project = jnp.einsum(
        "td,tf->df", whole_first, whole_dproj, preferred_element_type=jnp.float32
    )
    grad_input = d_hidden + norm_back(token_values, inverse_one, norm1_gain, d_normed_one)
    norm_one_part = jnp.sum(d_normed_one * token_values * inverse_one, axis=0)
    summed = (
        lax.psum(grad_project.astype(jnp.bfloat16), "dp").astype(jnp.float32),
        lax.psum(grad_out.astype(jnp.bfloat16), "dp").astype(jnp.float32),
        lax.psum(grad_gate_up.astype(jnp.bfloat16), "dp").astype(jnp.float32),
        lax.psum(grad_down.astype(jnp.bfloat16), "dp").astype(jnp.float32),
    )
    gains = lax.psum((norm_one_part, norm_two_part), ("dp", "col"))
    head_sums = lax.psum((query_gain_part, key_gain_part), ("dp", "row", "col"))
    grad_proj_all = summed[0]
    grad_gu_all = summed[2]
    return (
        block_out,
        grad_input,
        gains[0],
        grad_proj_all[:, :query_width],
        grad_proj_all[:, query_width : query_width + key_width],
        grad_proj_all[:, query_width + key_width :],
        head_sums[0],
        head_sums[1],
        summed[1],
        gains[1],
        grad_gu_all[:, :ff_width],
        grad_gu_all[:, ff_width:],
        summed[3],
    )


def solution(mesh):
    return jax.shard_map(
        body,
        mesh=mesh,
        in_specs=(
            P(("dp", "col"), "row"),
            P("row"),
            P("row", "col"),
            P("row", "col"),
            P("row", "col"),
            P(),
            P(),
            P("col", "row"),
            P("row"),
            P("row", "col"),
            P("row", "col"),
            P("col", "row"),
            P(("dp", "col"), "row"),
            P("dp"),
            P(),
        ),
        out_specs=(
            P(("dp", "col"), "row"),
            P(("dp", "col"), "row"),
            P("row"),
            P("row", "col"),
            P("row", "col"),
            P("row", "col"),
            P(),
            P(),
            P("col", "row"),
            P("row"),
            P("row", "col"),
            P("row", "col"),
            P("col", "row"),
        ),
        check_vma=False,
    )
```

profile of v0, /device:TPU:0, one launch (start us, length us, event | category | flops | bytes accessed | tf_op | source)
XLA Modules:
  0.0 2932.1 jit_solution(17457016474699235943)
XLA Ops:
  20.7 60.2 %all-gather.17.cloned.1.call-done = bf16[4096,1024]{1,0:T(8,128)(2,1)} async-done(((bf16[1024,1024]{1,0:T(8,128)(2,1)}), bf16[4096,1024]{1,0:T(8,128)(2,1)}) %all-gather.17.cloned.1.call-update) | async-done | bytes 8388624 | tf_op jit(solution)/shard_map/all_gather | solution.py:60
  101.0 54.0 %all-gather.19.cloned.1.call-done = bf16[2048,480]{0,1:T(8,128)(2,1)} async-done(((bf16[1024,480]{0,1:T(8,128)(2,1)}), bf16[2048,480]{0,1:T(8,128)(2,1)}) %all-gather.19.cloned.1.call-update) | async-done | bytes 1966096 | tf_op jit(solution)/shard_map/all_gather | solution.py:62
  155.1 58.9 %all-to-all-done = bf16[2,2048,1024]{1,2,0:T(8,128)(2,1)} async-done(((bf16[2,2048,1024]{1,2,0:T(8,128)(2,1)}), bf16[2,2048,1024]{1,2,0:T(8,128)(2,1)}, u32[]{:S(2)}, u32[]{:S(2)}) %all-to-all-start) | async-done | bytes 8388640 | tf_op jit(solution)/shard_map/all_to_all | solution.py:61
  325.3 75.4 %while.32 = (s32[]{:T(128)}, bf16[4,512,5,64]{1,3,2,0:T(8,128)(2,1)S(1)}, f32[4,5,512]{2,1,0:T(8,128)}, s32[4]{0:T(128)S(1)}, s32[]{:T(128)}, /*index=5*/bf16[40...) while((s32[]{:T(128)}, ...), condition=%wide.region_7.8_spmd, body=%wide.region_4.7_spmd.sunk | while | flops 1060936704 | bytes 57368080 | solution.py:210
  403.2 38.9 %all-gather.21.cloned.1.call-done = bf16[4096,320]{0,1:T(8,128)(2,1)} async-done(((bf16[2048,320]{0,1:T(8,128)(2,1)}), bf16[4096,320]{0,1:T(8,128)(2,1)}) %all-gather.21.cloned.1.call-update) | async-done | bytes 2621456 | tf_op jit(solution)/shard_map/all_gather | solution.py:67
  452.2 126.2 %reduce-scatter.7.cloned.1.call-done = f32[1024,1024]{1,0:T(8,128)} async-done(((f32[4096,1024]{1,0:T(8,128)}), f32[1024,1024]{1,0:T(8,128)}) %reduce-scatter.7.cloned.1.call-update) | async-done | bytes 4194320 | tf_op jit(solution)/shard_map/reduce_scatter | solution.py:70
  597.8 54.0 %all-gather.23.cloned.1.call-done = bf16[4096,1024]{1,0:T(8,128)(2,1)} async-done(((bf16[1024,1024]{1,0:T(8,128)(2,1)}), bf16[4096,1024]{1,0:T(8,128)(2,1)}) %all-gather.23.cloned.1.call-update) | async-done | bytes 8388624 | tf_op jit(solution)/shard_map/all_gather | solution.py:60
  671.4 201.9 %all-gather.25.cloned.1.call-done = bf16[2048,2560]{1,0:T(8,128)(2,1)} async-done(((bf16[1024,2560]{1,0:T(8,128)(2,1)}), bf16[2048,2560]{1,0:T(8,128)(2,1)}) %all-gather.25.cloned.1.call-update) | async-done | bytes 10485776 | tf_op jit(solution)/shard_map/all_gather | solution.py:62
  912.6 129.4 %all-gather.27.cloned.1.call-done = bf16[4096,1280]{1,0:T(8,128)(2,1)} async-done(((bf16[2048,1280]{1,0:T(8,128)(2,1)}), bf16[4096,1280]{1,0:T(8,128)(2,1)}) %all-gather.27.cloned.1.call-update) | async-done | bytes 10485776 | tf_op jit(solution)/shard_map/all_gather | solution.py:67
  1060.0 125.2 %reduce-scatter.9.cloned.1.call-done = f32[1024,1024]{1,0:T(8,128)} async-done(((f32[4096,1024]{1,0:T(8,128)}), f32[1024,1024]{1,0:T(8,128)}) %reduce-scatter.9.cloned.1.call-update) | async-done | bytes 4194320 | tf_op jit(solution)/shard_map/reduce_scatter | solution.py:70
  1192.0 57.7 %all-gather.29.cloned.1.call-done = bf16[4096,1024]{1,0:T(8,128)(2,1)} async-done(((bf16[1024,1024]{1,0:T(8,128)(2,1)}), bf16[4096,1024]{1,0:T(8,128)(2,1)}) %all-gather.29.cloned.1.call-update) | async-done | bytes 8388624 | tf_op jit(solution)/shard_map/all_gather | solution.py:60
  1269.1 98.3 %all-gather.31.cloned.1.call-done = bf16[2048,1280]{0,1:T(8,128)(2,1)} async-done(((bf16[1024,1280]{0,1:T(8,128)(2,1)}), bf16[2048,1280]{0,1:T(8,128)(2,1)}) %all-gather.31.cloned.1.call-update) | async-done | bytes 5242896 | tf_op jit(solution)/shard_map/all_gather | solution.py:62
  1367.4 42.2 %all-to-all-done.2 = bf16[2,2048,1024]{1,2,0:T(8,128)(2,1)} async-done(((bf16[2,2048,1024]{1,2,0:T(8,128)(2,1)}), bf16[2,2048,1024]{1,2,0:T(8,128)(2,1)}, u32[]{:S(2)}, u32[]{:S(2)}) %all-to-all-start.2) | async-done | bytes 8388640 | tf_op jit(solution)/shard_map/all_to_all | solution.py:61
  1444.9 247.3 %all-gather.33.cloned.1.call-done = bf16[4096,2560]{1,0:T(8,128)(2,1)} async-done(((bf16[2048,2560]{1,0:T(8,128)(2,1)}), bf16[4096,2560]{1,0:T(8,128)(2,1)}) %all-gather.33.cloned.1.call-update) | async-done | bytes 20971536 | tf_op jit(solution)/shard_map/all_gather | solution.py:67
  1720.7 126.2 %reduce-scatter.11.cloned.1.call-done = f32[1024,1024]{1,0:T(8,128)} async-done(((f32[4096,1024]{1,0:T(8,128)}), f32[1024,1024]{1,0:T(8,128)}) %reduce-scatter.11.cloned.1.call-update) | async-done | bytes 4194320 | tf_op jit(solution)/shard_map/reduce_scatter | solution.py:70
  1864.3 58.5 %all-gather.35.cloned.1.call-done = bf16[4096,1024]{1,0:T(8,128)(2,1)} async-done(((bf16[1024,1024]{1,0:T(8,128)(2,1)}), bf16[4096,1024]{1,0:T(8,128)(2,1)}) %all-gather.35.cloned.1.call-update) | async-done | bytes 8388624 | tf_op jit(solution)/shard_map/all_gather | solution.py:60
  1942.1 40.3 %all-gather.37.cloned.1.call-done = bf16[2048,320]{0,1:T(8,128)(2,1)} async-done(((bf16[1024,320]{0,1:T(8,128)(2,1)}), bf16[2048,320]{0,1:T(8,128)(2,1)}) %all-gather.37.cloned.1.call-update) | async-done | bytes 1310736 | tf_op jit(solution)/shard_map/all_gather | solution.py:62
  1982.4 66.2 %all-to-all-done.3 = bf16[2,2048,1024]{1,2,0:T(8,128)(2,1)} async-done(((bf16[2,2048,1024]{1,2,0:T(8,128)(2,1)}), bf16[2,2048,1024]{1,2,0:T(8,128)(2,1)}, u32[]{:S(2)}, u32[]{:S(2)}) %all-to-all-start.3) | async-done | bytes 8388640 | tf_op jit(solution)/shard_map/all_to_all | solution.py:61
  2062.2 298.3 %while.33 = (s32[]{:T(128)}, f32[4096,5,64]{0,2,1:T(8,128)}, f32[4096,5,64]{0,2,1:T(8,128)}, f32[4,512,5,64]{1,0,3,2:T(4,128)}, s32[4]{0:T(128)S(1)}, /*index=5*...) while((s32[]{:T(128)}, f32[4096,5,64]{0,2,1:T(8,128)}, ...), condition=%wide.region_17.18_spmd, body=%wide.region_15.17_spmd.sunk | while | flops 2586287616 | bytes 151103120 | solution.py:273
  2424.0 45.8 %reduce-scatter.13.cloned.1.call-done = bf16[1,2048,80]{1,2,0:T(8,128)(2,1)} async-done(((bf16[8,2048,80]{1,2,0:T(8,128)(2,1)}), bf16[1,2048,80]{1,2,0:T(8,128)(2,1)}) %reduce-scatter.13.cloned.1.call-update) | async-done | bytes 327696 | tf_op jit(solution)/shard_map/reduce_scatter | solution.py:286
  2490.1 28.7 convolution_convert_fusion.2
  2547.4 46.2 %all-reduce.4 = (f32[64]{0:T(128)}, f32[64]{0:T(128)}) all-reduce(f32[64]{0:T(128)S(1)} %get-tuple-element.406, f32[64]{0:T(128)S(1)} %get-tuple-element.400), channel_id=1, replica_groups=mesh['dp'=4,'row'=2,'col'=4] {'dp','row','col'}, use_global_device_ids=true, to_apply=%region_29.30 | all-reduce | flops 128 | bytes 1024 | tf_op jit(solution)/shard_map/psum | solution.py:312
  2593.6 271.9 %all-reduce.9.cloned.1.call-done = (bf16[1024,480]{0,1:T(8,128)(2,1)}, bf16[320,1024]{1,0:T(8,128)(2,1)}, bf16[1024,2560]{1,0:T(8,128)(2,1)}, bf16[1280,1024]{1,0:T(8,128)(2,1)}) async-done(((bf16[1024,480]{0,1:T(8,128)(2,1)}, bf16[320,1024]{1,0:T(8,128)(2,1)}, bf16[1024,2560]{1,0:T(8,128)(2,1)}, bf16[1280,1024]{1,0:T(8,128)(2,1)}), (bf16[1024,480]{0,1:T(8,128)(2,1)}, bf16[320,1024]{1,0:T(8,128)(2,1)}, ...) | async-done | bytes 9502736 | tf_op jit(solution)/shard_map/psum | solution.py:306
  2887.6 31.3 %all-reduce.5 = (f32[1024]{0:T(1024)}, f32[1024]{0:T(1024)}) all-reduce(f32[1024]{0:T(1024)S(1)} %get-tuple-element.404, f32[1024]{0:T(1024)S(1)} %copy-done.46), channel_id=1, replica_groups=mesh['dp'=4,'row'=2,'col'=4] {'dp','col'}, use_global_device_ids=true, to_apply=%region_26.27 | all-reduce | flops 2048 | bytes 16384 | tf_op jit(solution)/shard_map/psum | solution.py:311
  (435 shorter events, 890.5 us)
Async XLA Ops:
  8.0 72.9 %all-gather.17.cloned.1.call-start = ((), (), s32[]{:S(2)}) async-start(), calls=%async_computation.10 | async-start | bytes 10485760 | tf_op jit(solution)/shard_map/all_gather | solution.py:60
  92.6 121.3 %all-to-all-start = ((bf16[2,2048,1024]{1,2,0:T(8,128)(2,1)}), bf16[2,2048,1024]{1,2,0:T(8,128)(2,1)}, u32[]{:S(2)}, u32[]{:S(2)}) async-start(bf16[2,2048,1024]{1,2,0:T(8,128)(2,1)} %copy.62), calls=%async_computation | async-start | bytes 16777216 | tf_op jit(solution)/shard_map/all_to_all | solution.py:61
  99.8 55.2 %all-gather.19.cloned.1.call-start = ((), (), s32[]{:S(2)}) async-start(), calls=%async_computation.11 | async-start | bytes 2949120 | tf_op jit(solution)/shard_map/all_gather | solution.py:62
  101.0 153.2 %all-gather.41.cloned.1.call-start = ((), (), s32[]{:S(2)}) async-start(), calls=%async_computation.28 | async-start | bytes 2949120 | tf_op jit(solution)/shard_map/all_gather | solution.py:120
  225.0 61.5 %all-gather.43.cloned.1.call-start = ((), (), s32[]{:S(2)}) async-start(), calls=%async_computation.29 | async-start | bytes 2949120 | tf_op jit(solution)/shard_map/all_gather | solution.py:119
  225.6 216.5 %all-gather.21.cloned.1.call-start = ((), (), s32[]{:S(2)}) async-start(), calls=%async_computation.12 | async-start | bytes 3932160 | tf_op jit(solution)/shard_map/all_gather | solution.py:67
  403.1 175.2 %reduce-scatter.7.cloned.1.call-start = ((), (), s32[]{:S(2)}) async-start(), calls=%async_computation.13 | async-start | bytes 20971520 | tf_op jit(solution)/shard_map/reduce_scatter | solution.py:70
  452.1 199.7 %all-gather.23.cloned.1.call-start = ((), (), s32[]{:S(2)}) async-start(), calls=%async_computation.14 | async-start | bytes 10485760 | tf_op jit(solution)/shard_map/all_gather | solution.py:60
  593.3 280.0 %all-gather.25.cloned.1.call-start = ((), (), s32[]{:S(2)}) async-start(), calls=%async_computation.15 | async-start | bytes 15728640 | tf_op jit(solution)/shard_map/all_gather | solution.py:62
  663.8 209.5 %all-to-all-start.1 = ((bf16[2,2048,1024]{1,2,0:T(8,128)(2,1)}), bf16[2,2048,1024]{1,2,0:T(8,128)(2,1)}, u32[]{:S(2)}, u32[]{:S(2)}) async-start(bf16[2,2048,1024]{1,2,0:T(8,128)(2,1)} %copy.72), calls=%async_computation.2 | async-start | bytes 16777216 | tf_op jit(solution)/shard_map/all_to_all | solution.py:61
  671.3 370.7 %all-gather.27.cloned.1.call-start = ((), (), s32[]{:S(2)}) async-start(), calls=%async_computation.16 | async-start | bytes 15728640 | tf_op jit(solution)/shard_map/all_gather | solution.py:67
  912.6 272.6 %reduce-scatter.9.cloned.1.call-start = ((), (), s32[]{:S(2)}) async-start(), calls=%async_computation.17 | async-start | bytes 20971520 | tf_op jit(solution)/shard_map/reduce_scatter | solution.py:70
  1059.0 190.8 %all-gather.29.cloned.1.call-start = ((), (), s32[]{:S(2)}) async-start(), calls=%async_computation.18 | async-start | bytes 10485760 | tf_op jit(solution)/shard_map/all_gather | solution.py:60
  1191.3 176.1 %all-gather.31.cloned.1.call-start = ((), (), s32[]{:S(2)}) async-start(), calls=%async_computation.19 | async-start | bytes 7864320 | tf_op jit(solution)/shard_map/all_gather | solution.py:62
  1261.7 147.9 %all-to-all-start.2 = ((bf16[2,2048,1024]{1,2,0:T(8,128)(2,1)}), bf16[2,2048,1024]{1,2,0:T(8,128)(2,1)}, u32[]{:S(2)}, u32[]{:S(2)}) async-start(bf16[2,2048,1024]{1,2,0:T(8,128)(2,1)} %copy.73), calls=%async_computation.4 | async-start | bytes 16777216 | tf_op jit(solution)/shard_map/all_to_all | solution.py:61
  1269.1 423.1 %all-gather.33.cloned.1.call-start = ((), (), s32[]{:S(2)}) async-start(), calls=%async_computation.20 | async-start | bytes 31457280 | tf_op jit(solution)/shard_map/all_gather | solution.py:67
  1444.8 402.0 %reduce-scatter.11.cloned.1.call-start = ((), (), s32[]{:S(2)}) async-start(), calls=%async_computation.21 | async-start | bytes 20971520 | tf_op jit(solution)/shard_map/reduce_scatter | solution.py:70
  1720.6 202.2 %all-gather.35.cloned.1.call-start = ((), (), s32[]{:S(2)}) async-start(), calls=%async_computation.22 | async-start | bytes 10485760 | tf_op jit(solution)/shard_map/all_gather | solution.py:60
  1934.5 114.1 %all-to-all-start.3 = ((bf16[2,2048,1024]{1,2,0:T(8,128)(2,1)}), bf16[2,2048,1024]{1,2,0:T(8,128)(2,1)}, u32[]{:S(2)}, u32[]{:S(2)}) async-start(bf16[2,2048,1024]{1,2,0:T(8,128)(2,1)} %copy.76), calls=%async_computation.6 | async-start | bytes 16777216 | tf_op jit(solution)/shard_map/all_to_all | solution.py:61
  1942.1 482.0 %reduce-scatter.15.cloned.1.call-start = ((), (), s32[]{:S(2)}) async-start(), calls=%async_computation.25 | async-start | bytes 2949120 | tf_op jit(solution)/shard_map/reduce_scatter | solution.py:289
  2379.5 90.4 %reduce-scatter.13.cloned.1.call-start = ((), (), s32[]{:S(2)}) async-start(), calls=%async_computation.24 | async-start | bytes 2949120 | tf_op jit(solution)/shard_map/reduce_scatter | solution.py:286
  2416.9 109.2 %all-gather.39.cloned.1.call-start = ((), (), s32[]{:S(2)}) async-start(), calls=%async_computation.26 | async-start | bytes 5898240 | tf_op jit(solution)/shard_map/all_gather | solution.py:67
  2472.4 393.1 %all-reduce.9.cloned.1.call-start = ((), (), s32[]{:S(2)}) async-start(), calls=%async_computation.30 | async-start | bytes 19005440 | tf_op jit(solution)/shard_map/psum | solution.py:306
  2535.9 343.2 %reduce-scatter.17.cloned.1.call-start = ((), (), s32[]{:S(2)}) async-start(), calls=%async_computation.27 | async-start | bytes 20971520 | tf_op jit(solution)/shard_map/reduce_scatter | solution.py:70
  (64 other events, 1847.5 us)
Sparse Core Ops, SparseCore 0:
  20.8 60.0 all-gather.16
  452.2 126.0 reduce-scatter.6
  593.4 58.2 all-gather.22
  653.9 219.3 all-gather.24
  1059.1 126.0 reduce-scatter.8
  1191.4 58.2 all-gather.28
  1251.3 116.0 all-gather.30
  1720.7 126.0 reduce-scatter.10
  1864.5 58.2 all-gather.34
  2547.5 127.1 reduce-scatter.16
Sparse Core Ops, SparseCore 1:
  101.8 53.2 all-gather.18
  225.1 29.0 all-gather.40
  256.5 29.9 all-gather.42
  403.2 38.8 all-gather.20
  912.7 129.3 all-gather.26
  1444.9 247.2 all-gather.32
  1943.6 38.8 all-gather.36
  2379.6 42.6 reduce-scatter.14
  2426.3 43.5 reduce-scatter.12
  2472.5 53.6 all-gather.38
  2536.0 329.5 all-reduce.8
where the time goes:
time: 2940 us; the launch traced here: 2930 us
  waiting for transfers between devices  1940 us (66%)
  matrix products  360 us (12%)
  local copies, waits for them, and re-layouts  285 us (10%)
  other arithmetic  186 us (6%)
  blocking collectives  98.2 us (3%)
  starting transfers between devices  30.3 us (1%)
    all_gather x4, waiting for transfers between devices, row_to_col(): whole = lax.all_gather(local, 'row', axis=0, tiled=True)  419 us
    all_gather x4, waiting for transfers between devices, col_to_row(): full_weight = lax.all_gather(weight, 'row', axis=0, tiled=True)  394 us
    reduce_scatter x4, waiting for transfers between devices, row_to_col(): lax.psum_scatter(lax.dot_general(whole, weight, (((1,), (contract,)), (()...  378 us
    psum x1, waiting for transfers between devices, body(): lax.psum(grad_project.astype(jnp.bfloat16), 'dp').astype(jnp.float32)  272 us
    all_gather x4, waiting for transfers between devices, col_to_row(): whole = lax.all_gather(local, 'col', axis=0, tiled=True)  230 us
    all_to_all x4, waiting for transfers between devices, col_to_row(): mine = lax.all_to_all(whole, 'row', split_axis=0, concat_axis=1, tiled=True)  167 us
    dot_general x4, matrix products, col_to_row(): jnp.dot(mine, full_weight, preferred_element_type=jnp.float32)  71.1 us
    dot_general x4, matrix products, row_to_col(): lax.dot_general(whole, weight, (((1,), (contract,)), ((), ())), preferred...  65.6 us
  transfers between devices with their start and end apart: 25, of which 22 were waited for; matrix products, arithmetic and copies ran while one was open for 6% of the time, Pallas kernels for 0%

commit v1 on v0

v1 whole, which is shorter than its diff:
```python
import functools
import math

import jax
import jax.numpy as jnp
from jax import lax
from jax.experimental import pallas as pl
from jax.experimental.pallas import tpu as pltpu
from jax.sharding import Mesh
from jax.sharding import PartitionSpec as P

D = 2048
QH = 20
KVH = 5
HD = 64
PROMPT = 1024
CONT = 128
NCONT = 8
GROUP = PROMPT + NCONT * CONT
REP = QH // KVH
KEYS = 256

EPSILON = 1e-06
BF = jnp.bfloat16
F32 = jnp.float32


def dot(left, right, dims=((1,), (0,))):
    return lax.dot_general(left, right, (dims, ((), ())), preferred_element_type=F32)


def rms(values):
    return lax.rsqrt(jnp.mean(values * values, axis=1, keepdims=True) + EPSILON)


def norm_back(states, inverse, gain, d_normed):
    mean = jnp.mean(states * gain * d_normed, axis=1, keepdims=True)
    return inverse * gain * d_normed - states * inverse**3 * mean


def prepare(raw, gain, cosine, sine):
    values = raw * lax.rsqrt(jnp.mean(raw * raw, axis=1, keepdims=True) + EPSILON)
    values = values * gain[None, :, None]
    half = HD // 2
    first, second = values[:, :half], values[:, half:]
    return jnp.concatenate(
        [first * cosine - second * sine, second * cosine + first * sine], axis=1
    )


def allowed(first_query, first_key, span, rows):
    key = first_key + lax.broadcasted_iota(jnp.int32, (KEYS, rows), 0)
    query = first_query + lax.broadcasted_iota(jnp.int32, (KEYS, rows), 1) % span
    return (key <= query) & ((key < PROMPT) | (key // CONT == query // CONT))


def side_by_side(ref, index, span):
    return jnp.concatenate(
        [ref[0, head, :, index * span : (index + 1) * span] for head in range(REP)], axis=1
    )


def tiles_of(first_query):
    last = first_query // KEYS
    return jnp.minimum(last, PROMPT // KEYS), last


def attend_kernel(chunks, span, first_ref, query_ref, key_ref, value_ref, out_ref, log_ref):
    rows = REP * span
    for index in range(chunks):
        query = side_by_side(query_ref, index, span)
        first_query = first_ref[index]
        full, last = tiles_of(first_query)

        def tile(where, accum, masked):
            first_key = pl.multiple_of(where * KEYS, KEYS)
            scores = dot(key_ref[0, pl.ds(first_key, KEYS), :], query)
            expo = jnp.exp(scores)
            if masked:
                expo = jnp.where(allowed(first_query, first_key, span, rows), expo, 0.0)
            return accum + dot(value_ref[0, :, pl.ds(first_key, KEYS)], expo.astype(BF))

        accum = tile(last, jnp.zeros((value_ref.shape[1], rows), F32), True)
        accum = lax.fori_loop(0, full, lambda where, total: tile(where, total, False), accum)
        total = accum[HD : HD + 1]
        mixed = accum[:HD] / total
        logs = jnp.log(total)
        for head in range(REP):
            cut = slice(head * span, (head + 1) * span)
            out_ref[0, head, :, index * span : (index + 1) * span] = mixed[:, cut]
            log_ref[0, head : head + 1, index * span : (index + 1) * span] = logs[:, cut]


def attend_back_kernel(
    chunks,
    span,
    first_ref,
    query_ref,
    d_out_ref,
    log_ref,
    delta_ref,
    key_ref,
    value_ref,
    key_t_ref,
    d_query_ref,
    d_key_ref,
    d_value_ref,
):
    rows = REP * span
    d_key_ref[...] = jnp.zeros_like(d_key_ref)
    d_value_ref[...] = jnp.zeros_like(d_value_ref)
    for index in range(chunks):
        query = side_by_side(query_ref, index, span)
        d_out = side_by_side(d_out_ref, index, span)
        query_t = query.T
        d_out_t = d_out.T
        cut = slice(index * span, (index + 1) * span)
        logs = jnp.concatenate([log_ref[0, h : h + 1, cut] for h in range(REP)], axis=1)
        delta = jnp.concatenate([delta_ref[0, h : h + 1, cut] for h in range(REP)], axis=1)
        first_query = first_ref[index]
        full, last = tiles_of(first_query)

        def tile(where, accum, masked):
            first_key = pl.multiple_of(where * KEYS, KEYS)
            here = pl.ds(first_key, KEYS)
            probs = jnp.exp(dot(key_ref[0, here, :], query) - logs)
            if masked:
                probs = jnp.where(allowed(first_query, first_key, span, rows), probs, 0.0)
            d_probs = dot(value_ref[0, here, :], d_out)
            d_scores = (probs * (d_probs - delta)).astype(BF)
            d_value_ref[0, here, :] += dot(probs.astype(BF), d_out_t)
            d_key_ref[0, here, :] += dot(d_scores, query_t)
            return accum + dot(key_t_ref[0, :, here], d_scores)

        accum = tile(last, jnp.zeros((HD, rows), F32), True)
        accum = lax.fori_loop(0, full, lambda where, total: tile(where, total, False), accum)
        for head in range(REP):
            part = accum[:, head * span : (head + 1) * span]
            d_query_ref[0, head, :, cut] = part


def per_head(shape):
    return pl.BlockSpec((1,) + shape, lambda head, first: (head,) + (0,) * len(shape))


def attend(first, query, key, value_t):
    tokens = query.shape[-1]
    chunks = first.shape[0]
    return pl.pallas_call(
        functools.partial(attend_kernel, chunks, tokens // chunks),
        out_shape=(
            jax.ShapeDtypeStruct((KVH, REP, HD, tokens), F32),
            jax.ShapeDtypeStruct((KVH, REP, tokens), F32),
        ),
        grid_spec=pltpu.PrefetchScalarGridSpec(
            num_scalar_prefetch=1,
            grid=(KVH,),
            in_specs=[
                per_head((REP, HD, tokens)),
                per_head((GROUP, HD)),
                per_head((value_t.shape[1], GROUP)),
            ],
            out_specs=[per_head((REP, HD, tokens)), per_head((REP, tokens))],
        ),
        compiler_params=pltpu.CompilerParams(vmem_limit_bytes=32 * 1024 * 1024),
        name="attend",
    )(first, query, key, value_t)


def attend_back(first, query, d_out, logs, delta, key, value, key_t):
    tokens = query.shape[-1]
    chunks = first.shape[0]
    return pl.pallas_call(
        functools.partial(attend_back_kernel, chunks, tokens // chunks),
        out_shape=(
            jax.ShapeDtypeStruct((KVH, REP, HD, tokens), F32),
            jax.ShapeDtypeStruct((KVH, GROUP, HD), F32),
            jax.ShapeDtypeStruct((KVH, GROUP, HD), F32),
        ),
        grid_spec=pltpu.PrefetchScalarGridSpec(
            num_scalar_prefetch=1,
            grid=(KVH,),
            in_specs=[
                per_head((REP, HD, tokens)),
                per_head((REP, HD, tokens)),
                per_head((REP, tokens)),
                per_head((REP, tokens)),
                per_head((GROUP, HD)),
                per_head((GROUP, HD)),
                per_head((HD, GROUP)),
            ],
            out_specs=[
                per_head((REP, HD, tokens)),
                per_head((GROUP, HD)),
                per_head((GROUP, HD)),
            ],
        ),
        compiler_params=pltpu.CompilerParams(vmem_limit_bytes=32 * 1024 * 1024),
        name="attend_back",
    )(first, query, d_out, logs, delta, key, value, key_t)


def body(
    tokens,
    norm1_gain,
    w_query,
    w_key,
    w_value,
    query_gain,
    key_gain,
    w_out,
    norm2_gain,
    w_gate,
    w_up,
    w_down,
    teacher,
    positions,
    token_count,
):
    rows = lax.axis_size("row")
    cores = lax.axis_size("side")
    cols = lax.axis_size("group") * cores
    row_index = lax.axis_index("row")
    group_index = lax.axis_index("group")
    members = rows * cores
    member = row_index * cores + lax.axis_index("side")
    shard, width = tokens.shape
    pieces = 2 * members
    span = shard // pieces
    mine = shard // members * cores
    q_width, k_width = w_query.shape[1], w_key.shape[1]
    ff = w_gate.shape[1]

    def to_members(block):
        parts = block.reshape(pieces, span, width)
        parts = jnp.stack([parts[:members], parts[members:][::-1]], axis=1)
        moved = lax.all_to_all(parts, ("row", "side"), 0, 0, tiled=True)
        moved = moved.reshape(rows, cores, 2 * span, width).transpose(1, 2, 0, 3)
        return moved.reshape(mine, rows * width)

    def from_members(block):
        parts = block.reshape(cores, 2, span, rows, width).transpose(3, 0, 1, 2, 4)
        parts = parts.reshape(members, 2, span, width)
        moved = lax.all_to_all(parts, ("row", "side"), 0, 0, tiled=True)
        moved = jnp.concatenate([moved[:, 0], moved[:, 1][::-1]], axis=0)
        return moved.reshape(shard, width)

    def pick(values):
        part = lax.dynamic_slice_in_dim(values.reshape(-1, cores, pieces, span), group_index, 1, 0)[0]
        low = lax.dynamic_slice_in_dim(part, member, 1, 1)
        high = lax.dynamic_slice_in_dim(part, pieces - 1 - member, 1, 1)
        return jnp.concatenate([low, high], axis=1).reshape(-1)

    first_tokens = (
        jnp.array([0, 0, shard, shard], jnp.int32)
        + jnp.stack([member, pieces - 1 - member] * 2).astype(jnp.int32) * span
    )

    w_project = jnp.concatenate([w_query, w_key, w_value], axis=1)
    w_project = lax.all_gather(w_project, ("group", "side", "row"), axis=0, tiled=True)
    w_project = w_project.reshape(cols, D, q_width + 2 * k_width)
    states = to_members(tokens).astype(F32)
    w_out_all = lax.all_gather(w_out, ("group", "side", "row"), axis=0)
    w_out_all = w_out_all.reshape(cols, rows, q_width, width).transpose(0, 2, 1, 3)
    w_out_all = w_out_all.reshape(QH * HD, D)
    w_gate_all = lax.all_gather(w_gate, "row", axis=0, tiled=True)
    w_up_all = lax.all_gather(w_up, "row", axis=0, tiled=True)
    w_down_all = lax.all_gather(w_down, "row", axis=0).transpose(1, 0, 2).reshape(ff, D)
    gain_one = lax.all_gather(norm1_gain, "row", axis=0, tiled=True)
    gain_two = lax.all_gather(norm2_gain, "row", axis=0, tiled=True)
    target = to_members(teacher)

    half = HD // 2
    freq = jnp.exp(jnp.arange(half, dtype=F32) * (-2.0 * math.log(10000.0) / HD))
    angle = freq[:, None] * pick(positions).astype(F32)[None, :]
    cosine, sine = jnp.cos(angle), jnp.sin(angle)
    inverse_one = rms(states)
    normed_one = (states * inverse_one * gain_one).astype(BF)
    projected = dot(w_project, normed_one, ((1,), (1,)))
    query_raw = projected[:, :q_width].reshape(QH, HD, mine)
    key_sent = projected[:, q_width : q_width + k_width].reshape(KVH, HD, mine).astype(BF)
    value_sent = projected[:, q_width + k_width :].reshape(KVH, HD, mine).astype(BF)
    query_rot, query_back = jax.vjp(
        lambda raw, gain: prepare(raw, gain, cosine, sine), query_raw, query_gain
    )
    key_rot, key_back = jax.vjp(
        lambda raw, gain: prepare(raw, gain, cosine, sine), key_sent.astype(F32), key_gain
    )
    scale = 1.0 / math.sqrt(HD)
    query_use = (query_rot.astype(BF) * BF(scale)).reshape(KVH, REP, HD, mine)
    pair = jnp.stack([key_rot.astype(BF), value_sent])
    pair = lax.all_gather(pair, ("row", "side"), axis=0)

    def natural(stacked):
        lead = stacked.shape[1:-1]
        parts = stacked.reshape((members,) + lead + (cores, 2, span))
        low, high = parts[..., 0, :], parts[..., 1, :]
        both = jnp.concatenate([low, high[::-1]], axis=0)
        return jnp.moveaxis(both, 0, -2).reshape(lead + (GROUP,))

    def dealt(full):
        lead, entry = full.shape[:-2], full.shape[-1]
        parts = full.reshape(lead + (cores, pieces, span, entry))
        low = parts[..., :members, :, :]
        high = parts[..., members:, :, :][..., ::-1, :, :]
        both = jnp.stack([low, high], axis=-3)
        both = jnp.moveaxis(both, -4, 0)
        return both.reshape((members,) + lead + (mine, entry))

    pair = natural(pair)
    key_t, value_t = pair[0], pair[1]
    key_n, value_n = key_t.transpose(0, 2, 1), value_t.transpose(0, 2, 1)
    value_one = jnp.concatenate([value_t, jnp.ones((KVH, 16, GROUP), BF)], axis=1)
    mixed_f, logs = attend(first_tokens, query_use, key_n, value_one)
    mixed = mixed_f.reshape(QH * HD, mine).astype(BF)
    hidden = states + dot(mixed, w_out_all, ((0,), (0,)))

    inverse_two = rms(hidden)
    normed_two = (hidden * inverse_two * gain_two).astype(BF)
    normed_all = lax.all_gather(normed_two, ("group", "side"), axis=0, tiled=True)
    gate = dot(normed_all, w_gate_all)
    up = dot(normed_all, w_up_all)
    sig = jax.nn.sigmoid(gate)
    activated = (gate * sig * up).astype(BF)
    ffn_out = dot(activated, w_down_all).astype(BF)
    ffn_out = lax.psum_scatter(ffn_out, ("group", "side"), scatter_dimension=0, tiled=True)
    result = hidden + ffn_out.astype(F32)
    block_out = from_members(result.astype(BF))

    total_tokens = shard * cols * lax.axis_size("dp")
    loss_scale = total_tokens / token_count[0].astype(F32)
    d_result = loss_scale * (result - target.astype(F32))
    d_low = lax.all_gather(d_result.astype(BF), ("group", "side"), axis=0, tiled=True)
    d_act = dot(d_low, w_down_all, ((1,), (1,)))
    grad_down = dot(activated, d_low, ((0,), (0,))).astype(BF)
    d_up = (d_act * gate * sig).astype(BF)
    d_gate = (d_act * up * sig * (1.0 + gate * (1.0 - sig))).astype(BF)
    d_normed = dot(d_gate, w_gate_all, ((1,), (1,))) + dot(d_up, w_up_all, ((1,), (1,)))
    d_normed = lax.psum_scatter(
        d_normed.astype(BF), ("group", "side"), scatter_dimension=0, tiled=True
    ).astype(F32)
    grad_gate = dot(normed_all, d_gate, ((0,), (0,))).astype(BF)
    grad_up = dot(normed_all, d_up, ((0,), (0,))).astype(BF)
    grad_down = lax.psum_scatter(grad_down, "row", scatter_dimension=1, tiled=True)
    grad_gate = lax.psum_scatter(grad_gate, "row", scatter_dimension=0, tiled=True)
    grad_up = lax.psum_scatter(grad_up, "row", scatter_dimension=0, tiled=True)
    grad_down = lax.psum(grad_down, "dp")
    grad_gate, grad_up, _ = lax.optimization_barrier((grad_gate, grad_up, grad_down))
    grad_gate, grad_up = lax.psum((grad_gate, grad_up), "dp")

    norm_two_part = jnp.sum(d_normed * hidden * inverse_two, axis=0)
    d_hidden = d_result + norm_back(hidden, inverse_two, gain_two, d_normed)
    d_hidden_low = d_hidden.astype(BF)
    grad_out = dot(mixed, d_hidden_low, ((1,), (0,))).astype(BF)
    d_mixed = dot(w_out_all, d_hidden_low, ((1,), (1,))).astype(BF)
    d_mixed = d_mixed.reshape(KVH, REP, HD, mine)
    delta = jnp.sum(d_mixed.astype(F32) * mixed_f, axis=2)
    d_query, d_key_n, d_value_n = attend_back(
        first_tokens, query_use, d_mixed, logs, delta, key_n, value_n, key_t
    )
    d_pair = dealt(jnp.stack([d_key_n, d_value_n])).astype(BF)
    d_pair = lax.psum_scatter(d_pair, ("row", "side"), scatter_dimension=0, tiled=True)[0]
    d_pair = d_pair.astype(F32).transpose(0, 1, 3, 2)
    d_query_raw, query_gain_part = query_back(d_query.reshape(QH, HD, mine) * scale)
    d_key_raw, key_gain_part = key_back(d_pair[0])
    d_projected = jnp.concatenate(
        [
            d_query_raw.reshape(cols, q_width, mine),
            d_key_raw.reshape(cols, k_width, mine),
            d_pair[1].reshape(cols, k_width, mine),
        ],
        axis=1,
    ).astype(BF)
    d_normed_one = dot(d_projected, w_project, ((0, 1), (0, 2)))
    grad_input = d_hidden + norm_back(states, inverse_one, gain_one, d_normed_one)
    norm_one_part = jnp.sum(d_normed_one * states * inverse_one, axis=0)
    grad_input = from_members(grad_input)

    grad_project = lax.dot_general(
        d_projected, normed_one, (((2,), (0,)), ((), ())), preferred_element_type=F32
    )
    grad_project = grad_project.astype(BF).transpose(0, 2, 1)
    grad_project = lax.psum_scatter(
        grad_project.reshape(cols * D, -1),
        ("group", "side", "row"),
        scatter_dimension=0,
        tiled=True,
    )
    grad_out = grad_out.reshape(cols, q_width, rows, width).transpose(0, 2, 1, 3)
    grad_out = lax.psum_scatter(
        grad_out.reshape(cols * rows * q_width, width),
        ("group", "side", "row"),
        scatter_dimension=0,
        tiled=True,
    )
    grad_project, grad_out, _ = lax.optimization_barrier((grad_project, grad_out, grad_gate))
    grad_project, grad_out = lax.psum((grad_project, grad_out), "dp")
    small = jnp.concatenate([norm_one_part, norm_two_part, query_gain_part, key_gain_part])
    small = lax.psum(small, ("dp", "row", "group", "side"))
    grad_norm1 = lax.dynamic_slice_in_dim(small, row_index * width, width, 0)
    grad_norm2 = lax.dynamic_slice_in_dim(small, D + row_index * width, width, 0)
    grad_project = grad_project.astype(F32)
    return (
        block_out,
        grad_input,
        grad_norm1,
        grad_project[:, :q_width],
        grad_project[:, q_width : q_width + k_width],
        grad_project[:, q_width + k_width :],
        small[2 * D : 2 * D + HD],
        small[2 * D + HD :],
        grad_out.astype(F32),
        grad_norm2,
        grad_gate.astype(F32),
        grad_up.astype(F32),
        grad_down.astype(F32),
    )


def solution(mesh):
    dp, row, col = mesh.shape["dp"], mesh.shape["row"], mesh.shape["col"]

    def call(*args):
        side = GROUP * dp * col // args[0].shape[0]
        fine = Mesh(
            mesh.devices.reshape(dp, row, col // side, side), ("dp", "row", "group", "side")
        )
        col_axes = ("group", "side")
        token_spec = P(("dp", "group", "side"), "row")
        wide = P("row", col_axes)
        tall = P(col_axes, "row")
        return jax.shard_map(
            body,
            mesh=fine,
            in_specs=(
                token_spec,
                P("row"),
                wide,
                wide,
                wide,
                P(),
                P(),
                tall,
                P("row"),
                wide,
                wide,
                tall,
                token_spec,
                P("dp"),
                P(),
            ),
            out_specs=(
                token_spec,
                token_spec,
                P("row"),
                wide,
                wide,
                wide,
                P(),
                P(),
                tall,
                P("row"),
                wide,
                wide,
                tall,
            ),
            check_vma=False,
        )(*args)

    return call
```

time: 2940 us -> 1450 us (0.49)
  waiting for transfers between devices: 1940 us -> 778 us
  matrix products: 360 us -> 207 us
  other arithmetic: 186 us -> 69.2 us
  local copies, waits for them, and re-layouts: 285 us -> 174 us
  Pallas kernels: 0 us -> 66.3 us
    all_gather x14 -> x8, waiting for transfers between devices: 1080 us -> 267 us  [the longest x1 60.3 us: body(): lax.all_gather(normed_two, ('group', 'side'), axis=0, tiled=True)]
    reduce_scatter x6 -> x8, waiting for transfers between devices: 423 us -> 264 us  [the longest x1 73.1 us: body(): lax.psum_scatter(grad_project.reshape(cols * D, -1), ('group', 'side', 'r...]
    dot_general x44 -> x15, matrix products: 360 us -> 207 us  [the longest x14 202 us: dot(): lax.dot_general(left, right, (dims, ((), ())), preferred_element_type=F32)]
    all_to_all x4, waiting for transfers between devices: 167 us -> 24.6 us  [the longest x2 24.6 us: to_members(): moved = lax.all_to_all(parts, ('row', 'side'), 0, 0, tiled=True)]
    dynamic_update_slice x16 -> x0, local copies, waits for them, and re-layouts: 93.1 us -> none  [the longest x8 57 us: body(): mixed_blocks, log_totals = lax.map(attend, jnp.arange(block_count))]
    pallas_call x0 -> x2, Pallas kernels: none -> 66.3 us  [the longest x1 36.8 us: attend_back(): pl.pallas_call(functools.partial(attend_back_kernel, chunks, tokens // ch...]
    psum x1 -> x3, waiting for transfers between devices: 272 us -> 219 us  [the longest x1 106 us: body(): grad_down = lax.psum(grad_down, 'dp')]
    all_to_all x4 -> x0, local copies, waits for them, and re-layouts: 47.4 us -> none  [col_to_row(): mine = lax.all_to_all(whole, 'row', split_axis=0, concat_axis=1, tiled=True)]
  transfers between devices with their start and end apart: 25 -> 23, of which waited for: 22 -> 17; matrix products, arithmetic and copies ran while one was open for 6% -> 25% of each run, Pallas kernels for 0% -> 5%
where the time goes in v1:
time: 1450 us; the launch traced here: 1440 us
  waiting for transfers between devices  778 us (54%)
  matrix products  207 us (14%)
  local copies, waits for them, and re-layouts  174 us (12%)
  blocking collectives  112 us (8%)
  other arithmetic  69.2 us (5%)
  Pallas kernels  66.3 us (5%)
  starting transfers between devices  18.7 us (1%)
  between operations  16 us (1%)
    dot_general x14, matrix products, dot(): lax.dot_general(left, right, (dims, ((), ())), preferred_element_type=F32)  202 us
    psum x1, waiting for transfers between devices, body(): grad_down = lax.psum(grad_down, 'dp')  106 us
    reduce_scatter x1, waiting for transfers between devices, body(): lax.psum_scatter(grad_project.reshape(cols * D, -1), ('group', 'side', 'r...  73.1 us
    psum x1, blocking collectives, body(): small = lax.psum(small, ('dp', 'row', 'group', 'side'))  71 us
    psum x1, waiting for transfers between devices, body(): grad_gate, grad_up = lax.psum((grad_gate, grad_up), 'dp')  70.9 us
    all_gather x1, waiting for transfers between devices, body(): lax.all_gather(normed_two, ('group', 'side'), axis=0, tiled=True)  60.3 us
    reduce_scatter x1, waiting for transfers between devices, body(): lax.psum_scatter(grad_out.reshape(cols * rows * q_width, width), ('group'...  59.5 us
    all_gather x1, waiting for transfers between devices, body(): lax.all_gather(d_result.astype(BF), ('group', 'side'), axis=0, tiled=True)  58.4 us
  transfers between devices with their start and end apart: 23, of which 17 were waited for; matrix products, arithmetic and copies ran while one was open for 25% of the time, Pallas kernels for 5%

profile of v1, /device:TPU:0, one launch (start us, length us, event | category | flops | bytes accessed | tf_op | source)
XLA Modules:
  0.0 1441.4 jit_solution(1392945341295747050)
XLA Ops:
  16.4 36.4 %all_gather.40 = f32[2048]{0:T(1024)S(1)} all-gather(f32[1024]{0:T(1024)S(1)} %copy-done.57), channel_id=1, replica_groups=mesh['dp'=4,'row'=2,'group'=2,'side'=2] {'row'}, dimensions={0}, use_global_device_ids=true | all-gather | bytes 12288 | tf_op jit(solution)/shard_map/all_gather | solution.py:269
  102.2 17.8 %all-gather.24.cloned.1.call-done = bf16[2560,1024]{1,0:T(8,128)(2,1)} async-done(((bf16[320,1024]{1,0:T(8,128)(2,1)}), bf16[2560,1024]{1,0:T(8,128)(2,1)}) %all-gather.24.cloned.1.call-update) | async-done | bytes 5242896 | tf_op jit(solution)/shard_map/all_gather | solution.py:263
  180.5 29.5 %attend.1 = (f32[5,4,64,512]{3,2,1,0:T(8,128)S(1)}, f32[5,4,512]{2,1,0:T(4,128)S(1)}) custom-call(s32[4]{0:T(128)S(1)} %fusion.45.first_ref, bf16[5,4,64,512]{3,2,1,0:T(8,128)(2,1)S(1)} %copy-done.3, bf16[5,2048,64]{2,1,0:T(8,128)(2,1)S(1)} %copy.111.key_ref, bf16[5,80,2048]{2,1,0:T(8,128)(2,1)S(1)} %concatenate.59.clone.value_ref), custom_call_target="tpu_custom_call" | custom-call | tf_op jit(solution)/shard_map/attend/pallas_call | solution.py:149
  229.4 58.3 %all-gather.16.cloned.1.call-done = bf16[2048,1280]{1,0:T(8,128)(2,1)} async-done(((bf16[1024,1280]{1,0:T(8,128)(2,1)}), bf16[2048,1280]{1,0:T(8,128)(2,1)}) %all-gather.16.cloned.1.call-update) | async-done | bytes 5242896 | tf_op jit(solution)/shard_map/all_gather | solution.py:266
  287.7 60.3 %all-gather.14.cloned.1.call-done = bf16[2048,2048]{1,0:T(8,128)(2,1)} async-done(((bf16[512,2048]{1,0:T(8,128)(2,1)}), bf16[2048,2048]{1,0:T(8,128)(2,1)}) %all-gather.14.cloned.1.call-update) | async-done | bytes 8388624 | tf_op jit(solution)/shard_map/all_gather | solution.py:320
  364.6 53.6 %all-gather.18.cloned.1.call-done = bf16[2048,1280]{1,0:T(8,128)(2,1)} async-done(((bf16[1024,1280]{1,0:T(8,128)(2,1)}), bf16[2048,1280]{1,0:T(8,128)(2,1)}) %all-gather.18.cloned.1.call-update) | async-done | bytes 5242896 | tf_op jit(solution)/shard_map/all_gather | solution.py:267
  418.2 19.3 %multiply_convert_fusion.2 = (bf16[2048,1280]{1,0:T(8,128)(2,1)S(1)}, f32[2048,1280]{1,0:T(8,128)}) fusion(f32[2048,1280]{1,0:T(8,128)} %fusion.58, bf16[2048,2048]{1,0:T(8,128)(2,1)} %all-gather.14.cloned.1.call-done, bf16[2048,1280]{1,0:T(8,128)(2,1)} %all-gather.18.cloned.1.call-done), kind=kOutput, calls=%fused_computation.3 | convolution fusion | flops 10753146880 | bytes 39845888 | tf_op jit(solution)/shard_map/dot_general | solution.py:29
  462.0 24.6 %all-to-all-done.2 = bf16[4,2,128,1024]{3,2,1,0:T(8,128)(2,1)} async-done(((bf16[4,2,128,1024]{3,2,1,0:T(8,128)(2,1)}), bf16[4,2,128,1024]{3,2,1,0:T(8,128)(2,1)}, u32[]{:S(2)}, u32[]{:S(2)}) %all-to-all-start.2) | async-done | bytes 2097184 | tf_op jit(solution)/shard_map/all_to_all | solution.py:237
  495.9 29.7 %reduce-scatter.9.cloned.1.call-done = bf16[512,2048]{1,0:T(8,128)(2,1)} async-done(((bf16[2048,2048]{1,0:T(8,128)(2,1)}), bf16[512,2048]{1,0:T(8,128)(2,1)}) %reduce-scatter.9.cloned.1.call-update) | async-done | bytes 2097168 | tf_op jit(solution)/shard_map/reduce_scatter | solution.py:326
  532.3 58.4 %all-gather.20.cloned.1.call-done = bf16[2048,2048]{1,0:T(8,128)(2,1)} async-done(((bf16[512,2048]{1,0:T(8,128)(2,1)}), bf16[2048,2048]{1,0:T(8,128)(2,1)}) %all-gather.20.cloned.1.call-update) | async-done | bytes 8388624 | tf_op jit(solution)/shard_map/all_gather | solution.py:333
  607.5 25.0 %multiply_convert_fusion = (bf16[2048,1280]{1,0:T(8,128)(2,1)}, bf16[2048,1280]{1,0:T(8,128)(2,1)}) fusion(f32[2048,1280]{1,0:T(8,128)} %fusion.58, f32[2048,1280]{1,0:T(8,128)} %get-tuple-element.91, bf16[2048,2048]{1,0:T(8,128)(2,1)} %all-gather.20.cloned.1.call-done, bf16[1280,2048]{0,1:T(8,128)(2,1)} %bitcast.212), kind=kOutput, calls=%fused_computation.1 | convolution fusion | flops 10771496960 | bytes 45088768 | tf_op jit(solution)/shard_map/dot_general | solution.py:29
  632.5 17.8 %fusion.59 = f32[2048,2048]{1,0:T(8,128)} fusion(bf16[2048,1280]{1,0:T(8,128)(2,1)} %get-tuple-element.43, bf16[2048,1280]{1,0:T(8,128)(2,1)} %all-gather.16.cloned.1.call-done), kind=kOutput, calls=%fused_computation.148 | convolution fusion | flops 10737418240 | bytes 27262976 | tf_op jit(solution)/shard_map/dot_general | solution.py:29
  650.3 19.4 %add_convert_fusion = bf16[2048,2048]{1,0:T(8,128)(2,1)} fusion(f32[2048,2048]{1,0:T(8,128)} %fusion.59, bf16[2048,1280]{1,0:T(8,128)(2,1)} %get-tuple-element.42, bf16[2048,1280]{1,0:T(8,128)(2,1)} %all-gather.18.cloned.1.call-done), kind=kOutput, calls=%fused_computation | convolution fusion | flops 10745806848 | bytes 35651584 | tf_op jit(solution)/shard_map/dot_general | solution.py:29
  669.8 17.0 %convolution_convert_fusion.4 = bf16[2048,1280]{1,0:T(8,128)(2,1)} fusion(bf16[2048,2048]{1,0:T(8,128)(2,1)} %all-gather.14.cloned.1.call-done, bf16[2048,1280]{1,0:T(8,128)(2,1)} %get-tuple-element.43), kind=kOutput, calls=%fused_computation.14 | convolution fusion | flops 10740039680 | bytes 18874368 | tf_op jit(solution)/shard_map/dot_general | solution.py:29
  686.8 18.4 %convolution_convert_fusion.3 = bf16[2048,1280]{1,0:T(8,128)(2,1)} fusion(bf16[2048,2048]{1,0:T(8,128)(2,1)} %all-gather.14.cloned.1.call-done, bf16[2048,1280]{1,0:T(8,128)(2,1)} %get-tuple-element.42), kind=kOutput, calls=%fused_computation.13 | convolution fusion | flops 10740039680 | bytes 18874368 | tf_op jit(solution)/shard_map/dot_general | solution.py:29
  705.9 41.6 %reduce-scatter.11.cloned.1.call-done = bf16[512,2048]{1,0:T(8,128)(2,1)} async-done(((bf16[2048,2048]{1,0:T(8,128)(2,1)}), bf16[512,2048]{1,0:T(8,128)(2,1)}) %reduce-scatter.11.cloned.1.call-update) | async-done | bytes 2097168 | tf_op jit(solution)/shard_map/reduce_scatter | solution.py:339
  772.0 36.8 %attend_back.1 = (f32[5,4,64,512]{3,2,1,0:T(8,128)S(1)}, f32[5,2048,64]{2,1,0:T(8,128)S(1)}, f32[5,2048,64]{2,1,0:T(8,128)S(1)}) custom-call(s32[4]{0:T(128)S(1)} %fusion.45.first_ref, bf16[5,4,64,512]{3,2,1,0:T(8,128)(2,1)S(1)} %copy-done.4, bf16[5,4,64,512]{3,2,1,0:T(8,128)(2,1)S(1)} %bitcast.174, f32[5,4,512]{2,1,0:T(4,128)S(1)} %get-tuple-element.23.log_ref, ...), custom_call_target="tpu_custom_call" | custom-call | tf_op jit(solution)/shard_map/attend_back/pallas_call | solution.py:173
  829.4 54.1 %reduce-scatter.21.cloned.1.call-done = bf16[1024,1280]{1,0:T(8,128)(2,1)} async-done(((bf16[2048,1280]{1,0:T(8,128)(2,1)}), bf16[1024,1280]{1,0:T(8,128)(2,1)}) %reduce-scatter.21.cloned.1.call-update) | async-done | bytes 2621456 | tf_op jit(solution)/shard_map/reduce_scatter | solution.py:346
  883.5 106.5 %all-reduce.10.cloned.1.call-done = bf16[1280,1024]{1,0:T(8,128)(2,1)} async-done(((bf16[1280,1024]{1,0:T(8,128)(2,1)}), bf16[1280,1024]{1,0:T(8,128)(2,1)}) %all-reduce.10.cloned.1.call-update) | async-done | bytes 2621456 | tf_op jit(solution)/shard_map/psum | solution.py:347
  1061.7 70.9 %all-reduce.12.cloned.1.call-done = bf16[1024,1280]{1,0:T(8,128)(2,1)} async-done(((bf16[1024,1280]{1,0:T(8,128)(2,1)}), bf16[1024,1280]{1,0:T(8,128)(2,1)}) %all-reduce.12.cloned.1.call-update) | async-done | bytes 2621456 | tf_op jit(solution)/shard_map/psum | solution.py:349
  1132.6 59.5 %reduce-scatter.17.cloned.1.call-done = bf16[320,1024]{1,0:T(8,128)(2,1)} async-done(((bf16[2560,1024]{1,0:T(8,128)(2,1)}), bf16[320,1024]{1,0:T(8,128)(2,1)}) %reduce-scatter.17.cloned.1.call-update) | async-done | bytes 655376 | tf_op jit(solution)/shard_map/reduce_scatter | solution.py:390
  1192.1 73.1 %reduce-scatter.15.cloned.1.call-done = bf16[1024,480]{0,1:T(8,128)(2,1)} async-done(((bf16[8192,480]{0,1:T(8,128)(2,1)}), bf16[1024,480]{0,1:T(8,128)(2,1)}) %reduce-scatter.15.cloned.1.call-update) | async-done | bytes 983056 | tf_op jit(solution)/shard_map/reduce_scatter | solution.py:383
  1301.9 71.0 %psum.42 = f32[4224]{0:T(1024)S(1)} all-reduce(f32[4224]{0:T(1024)S(1)} %concatenate.63), channel_id=1, replica_groups=mesh['dp'=4,'row'=2,'group'=2,'side'=2] {'dp','row','group','side'}, use_global_device_ids=true, to_apply=%region_16.0 | all-reduce | flops 4224 | bytes 33792 | tf_op jit(solution)/shard_map/psum | solution.py:399
  1384.5 41.6 %all-reduce.14.cloned.1.call-done = (bf16[1024,480]{0,1:T(8,128)(2,1)}, bf16[320,1024]{1,0:T(8,128)(2,1)}, bf16[1024,1280]{1,0:T(8,128)(2,1)}) async-done(((bf16[1024,480]{0,1:T(8,128)(2,1)}, bf16[320,1024]{1,0:T(8,128)(2,1)}, bf16[1024,1280]{1,0:T(8,128)(2,1)}), (bf16[1024,480]{0,1:T(8,128)(2,1)}, bf16[320,1024]{1,0:T(8,128)(2,1)}, bf16[1024,1280]{1,0:T(8,128)(2,1)})) %all-reduce.14.cloned.1.call-update) | async-done | bytes 4259856 | tf_op jit(solution)/shard_map/psum | solution.py:397
  (291 shorter events, 384.9 us)
Async XLA Ops:
  7.2 68.9 %all-gather.12.cloned.1.call-start = ((), (), s32[]{:S(2)}) async-start(), calls=%async_computation.12 | async-start | bytes 8847360 | tf_op jit(solution)/shard_map/all_gather | solution.py:260
  9.7 110.3 %all-gather.24.cloned.1.call-start = ((), (), s32[]{:S(2)}) async-start(), calls=%async_computation.28 | async-start | bytes 5898240 | tf_op jit(solution)/shard_map/all_gather | solution.py:263
  12.2 41.8 %all-to-all-start = ((bf16[4,2,128,1024]{3,2,1,0:T(8,128)(2,1)}), bf16[4,2,128,1024]{3,2,1,0:T(8,128)(2,1)S(1)}, u32[]{:S(2)}, u32[]{:S(2)}) async-start(bf16[4,2,128,1024]{3,2,1,0:T(8,128)(2,1)} %pad_maximum_fusion.2), calls=%async_computation | async-start | bytes 4194304 | tf_op jit(solution)/shard_map/all_to_all | solution.py:237
  16.4 131.3 %all-gather.22.cloned.1.call-start = ((), (), s32[]{:S(2)}) async-start(), calls=%async_computation.27 | async-start | bytes 3276800 | tf_op jit(solution)/shard_map/all_gather | solution.py:292
  88.4 132.7 %all-gather.26.cloned.1.call-start = ((), (), s32[]{:S(2)}) async-start(), calls=%async_computation.29 | async-start | bytes 7864320 | tf_op jit(solution)/shard_map/all_gather | solution.py:268
  89.0 198.7 %all-gather.16.cloned.1.call-start = ((), (), s32[]{:S(2)}) async-start(), calls=%async_computation.14 | async-start | bytes 7864320 | tf_op jit(solution)/shard_map/all_gather | solution.py:266
  89.6 258.5 %all-gather.14.cloned.1.call-start = ((), (), s32[]{:S(2)}) async-start(), calls=%async_computation.13 | async-start | bytes 10485760 | tf_op jit(solution)/shard_map/all_gather | solution.py:320
  220.2 197.9 %all-gather.18.cloned.1.call-start = ((), (), s32[]{:S(2)}) async-start(), calls=%async_computation.15 | async-start | bytes 7864320 | tf_op jit(solution)/shard_map/all_gather | solution.py:267
  221.0 304.6 %reduce-scatter.9.cloned.1.call-start = ((), (), s32[]{:S(2)}) async-start(), calls=%async_computation.16 | async-start | bytes 10485760 | tf_op jit(solution)/shard_map/reduce_scatter | solution.py:326
  456.4 30.3 %all-to-all-start.2 = ((bf16[4,2,128,1024]{3,2,1,0:T(8,128)(2,1)}), bf16[4,2,128,1024]{3,2,1,0:T(8,128)(2,1)}, u32[]{:S(2)}, u32[]{:S(2)}) async-start(bf16[4,2,128,1024]{3,2,1,0:T(8,128)(2,1)} %pad_maximum_fusion.4), calls=%async_computation.3 | async-start | bytes 4194304 | tf_op jit(solution)/shard_map/all_to_all | solution.py:237
  460.9 129.8 %all-gather.20.cloned.1.call-start = ((), (), s32[]{:S(2)}) async-start(), calls=%async_computation.17 | async-start | bytes 10485760 | tf_op jit(solution)/shard_map/all_gather | solution.py:333
  532.2 173.1 %reduce-scatter.23.cloned.1.call-start = ((), (), s32[]{:S(2)}) async-start(), calls=%async_computation.24 | async-start | bytes 7864320 | tf_op jit(solution)/shard_map/reduce_scatter | solution.py:344
  607.3 140.2 %reduce-scatter.11.cloned.1.call-start = ((), (), s32[]{:S(2)}) async-start(), calls=%async_computation.18 | async-start | bytes 10485760 | tf_op jit(solution)/shard_map/reduce_scatter | solution.py:339
  669.7 159.6 %reduce-scatter.19.cloned.1.call-start = ((), (), s32[]{:S(2)}) async-start(), calls=%async_computation.22 | async-start | bytes 7864320 | tf_op jit(solution)/shard_map/reduce_scatter | solution.py:345
  686.8 196.7 %reduce-scatter.21.cloned.1.call-start = ((), (), s32[]{:S(2)}) async-start(), calls=%async_computation.23 | async-start | bytes 7864320 | tf_op jit(solution)/shard_map/reduce_scatter | solution.py:346
  705.3 284.7 %all-reduce.10.cloned.1.call-start = ((), (), s32[]{:S(2)}) async-start(), calls=%async_computation.25 | async-start | bytes 5242880 | tf_op jit(solution)/shard_map/psum | solution.py:347
  705.8 320.4 %reduce-scatter.13.cloned.1.call-start = ((), (), s32[]{:S(2)}) async-start(), calls=%async_computation.19 | async-start | bytes 3276800 | tf_op jit(solution)/shard_map/reduce_scatter | solution.py:362
  829.3 160.8 %copy-start.22 = (bf16[5,4,64,512]{3,2,1,0:T(8,128)(2,1)S(1)}, bf16[5,4,64,512]{3,2,1,0:T(8,128)(2,1)}, u32[]{:S(2)}) copy-start(bf16[5,4,64,512]{3,2,1,0:T(8,128)(2,1)} %copy-done.21) | copy-start | bytes 3932164
  829.3 303.3 %all-reduce.12.cloned.1.call-start = ((), (), s32[]{:S(2)}) async-start(), calls=%async_computation.26 | async-start | bytes 5242880 | tf_op jit(solution)/shard_map/psum | solution.py:349
  990.0 202.1 %reduce-scatter.17.cloned.1.call-start = ((), (), s32[]{:S(2)}) async-start(), calls=%async_computation.21 | async-start | bytes 5898240 | tf_op jit(solution)/shard_map/reduce_scatter | solution.py:390
  1013.0 252.1 %reduce-scatter.15.cloned.1.call-start = ((), (), s32[]{:S(2)}) async-start(), calls=%async_computation.20 | async-start | bytes 8847360 | tf_op jit(solution)/shard_map/reduce_scatter | solution.py:383
  1046.0 239.3 %all-to-all-start.1 = ((bf16[4,2,128,1024]{3,2,1,0:T(8,128)(2,1)}), bf16[4,2,128,1024]{3,2,1,0:T(8,128)(2,1)S(1)}, u32[]{:S(2)}, u32[]{:S(2)}) async-start(bf16[4,2,128,1024]{3,2,1,0:T(8,128)(2,1)} %bitcast.203), calls=%async_computation.2 | async-start | bytes 4194304 | tf_op jit(solution)/shard_map/all_to_all | solution.py:244
  1049.6 376.5 %all-reduce.14.cloned.1.call-start = ((), (), s32[]{:S(2)}) async-start(), calls=%async_computation.30 | async-start | bytes 8519680 | tf_op jit(solution)/shard_map/psum | solution.py:397
  1285.3 88.9 %all-to-all-start.3 = ((f32[4,2,128,1024]{3,2,1,0:T(8,128)}), f32[4,2,128,1024]{3,2,1,0:T(8,128)}, u32[]{:S(2)}, u32[]{:S(2)}) async-start(f32[4,2,128,1024]{3,2,1,0:T(8,128)} %bitcast.199), calls=%async_computation.6 | async-start | bytes 8388608 | tf_op jit(solution)/shard_map/all_to_all | solution.py:244
  (62 other events, 689.3 us)
Sparse Core Ops, SparseCore 0:
  10.5 65.5 all-gather.11
  77.9 42.0 all-gather.23
  122.1 25.5 all-gather.21
  149.1 68.5 all-gather.25
  219.1 68.5 all-gather.15
  289.7 58.2 all-gather.13
  349.6 68.5 all-gather.17
  453.2 72.3 reduce-scatter.8
  532.3 58.2 all-gather.19
  607.4 65.6 reduce-scatter.22
  675.7 71.7 reduce-scatter.10
  749.7 65.6 reduce-scatter.18
  817.7 65.6 reduce-scatter.20
  885.8 104.0 all-reduce.9
  992.5 33.6 reduce-scatter.12
  1028.4 104.1 all-reduce.11
  1136.4 55.6 reduce-scatter.16
  1195.8 69.3 reduce-scatter.14
  1267.7 158.3 all-reduce.13

commit v2 on v1

--- a/solution.py
+++ b/solution.py
@@ -200,6 +200,189 @@
     )(first, query, d_out, logs, delta, key, value, key_t)
 
 
+AHEAD = 4
+
+
+class Part:
+    def __init__(self, axis, rows, cols, count, base):
+        self.axis, self.rows, self.cols, self.count, self.base = axis, rows, cols, count, base
+
+    def cut(self, ref, index, half):
+        first = index * self.rows
+        if self.axis == 0:
+            return ref.at[pl.ds(half * self.rows * self.count + first, self.rows), :]
+        return ref.at[pl.ds(first, self.rows), pl.ds(half * self.cols, self.cols)]
+
+
+def reduce_kernel(parts, planes, *refs):
+    count = len(parts)
+    grads, outs, own, near, far, wide = (refs[i * count : (i + 1) * count] for i in range(6))
+    own_sem, out_sem, row_send, row_recv, in_send, far_recv, mid_send, wide_recv = refs[6 * count :]
+    plane = lax.axis_index("dp")
+    row = lax.axis_index("row")
+    other_row = {"row": 1 - row}
+    at_end = (plane == 0) | (plane == planes - 1)
+    low = plane < planes // 2
+    end_next = {"dp": jnp.where(low, 1, planes - 2)}
+    mid_outer = {"dp": jnp.where(low, 0, planes - 1)}
+    mid_other = {"dp": jnp.where(low, planes // 2, planes // 2 - 1)}
+
+    def remote(source, target, send, recv, where):
+        return pltpu.make_async_remote_copy(
+            source, target, send, recv, device_id=where, device_id_type=pl.DeviceIdType.MESH
+        )
+
+    barrier = pltpu.get_barrier_semaphore()
+
+    def greet(where):
+        pl.semaphore_signal(barrier, 1, device_id=where, device_id_type=pl.DeviceIdType.MESH)
+
+    greet(other_row)
+
+    @pl.when(at_end)
+    def _():
+        greet(end_next)
+        pl.semaphore_wait(barrier, 2)
+
+    @pl.when(jnp.logical_not(at_end))
+    def _():
+        greet(mid_outer)
+        greet(mid_other)
+        pl.semaphore_wait(barrier, 3)
+
+    def row_copy(j, index):
+        slot = parts[j].base + index
+        return remote(
+            parts[j].cut(grads[j], index, 1), near[j].at[index], row_send.at[slot], row_recv.at[slot], other_row
+        )
+
+    def in_copy(j, index):
+        slot = parts[j].base + index
+        return remote(near[j].at[index], far[j].at[index], in_send.at[slot], far_recv.at[slot], end_next)
+
+    def mid_copy(j, index):
+        slot = parts[j].base + index
+        return remote(far[j].at[index], wide[j].at[index], mid_send.at[slot], wide_recv.at[slot], mid_other)
+
+    def back_copy(j, index):
+        slot = parts[j].base + index
+        return remote(wide[j].at[index], far[j].at[index], in_send.at[slot], far_recv.at[slot], mid_outer)
+
+    def out_copy(j, index, source):
+        slot = parts[j].base + index
+        return pltpu.make_async_copy(source[j].at[index], parts[j].cut(outs[j], index, 0), out_sem.at[slot])
+
+    def own_copy(j, index):
+        slot = parts[j].base + index
+        return pltpu.make_async_copy(parts[j].cut(grads[j], index, 0), own[j].at[index], own_sem.at[slot])
+
+    def each(step, action):
+        for j, part in enumerate(parts):
+            index = step - part.base
+
+            @pl.when((index >= 0) & (index < part.count))
+            def _(j=j, index=index):
+                action(j, index)
+
+    def add(target, j, index, first, second):
+        total = first[j][index].astype(F32) + second[j][index].astype(F32)
+        target[j][index] = total.astype(BF)
+
+    def send_row(j, index):
+        own_copy(j, index).start()
+        row_copy(j, index).start()
+
+    def take_row(j, index):
+        own_copy(j, index).wait()
+        row_copy(j, index).wait_recv()
+        add(near, j, index, near, own)
+
+        @pl.when(at_end)
+        def _():
+            in_copy(j, index).start()
+
+    def take_far(j, index):
+        back_copy(j, index).wait_recv()
+        add(far, j, index, far, near)
+        mid_copy(j, index).start()
+
+    def take_wide(j, index):
+        mid_copy(j, index).wait_recv()
+        add(wide, j, index, wide, far)
+        back_copy(j, index).start()
+        out_copy(j, index, wide).start()
+
+    def take_back(j, index):
+        in_copy(j, index).wait_recv()
+        out_copy(j, index, far).start()
+
+    def finish_end(j, index):
+        row_copy(j, index).wait_send()
+        in_copy(j, index).wait_send()
+        out_copy(j, index, far).wait()
+
+    def finish_mid(j, index):
+        row_copy(j, index).wait_send()
+        mid_copy(j, index).wait_send()
+        back_copy(j, index).wait_send()
+        out_copy(j, index, wide).wait()
+
+    total = sum(part.count for part in parts)
+
+    @pl.loop(0, AHEAD)
+    def _(step):
+        each(step, send_row)
+
+    @pl.loop(0, total + 4)
+    def _(step):
+        each(step + AHEAD, send_row)
+        each(step, take_row)
+
+        @pl.when(at_end)
+        def _():
+            each(step - 4, take_back)
+
+        @pl.when(jnp.logical_not(at_end))
+        def _():
+            each(step - 1, take_far)
+            each(step - 2, take_wide)
+
+    @pl.when(at_end)
+    def _():
+        @pl.loop(0, total)
+        def _(step):
+            each(step, finish_end)
+
+    @pl.when(jnp.logical_not(at_end))
+    def _():
+        @pl.loop(0, total)
+        def _(step):
+            each(step, finish_mid)
+
+
+def reduce_all(planes, grads):
+    parts, base = [], 0
+    for grad, axis, rows in grads:
+        height = grad.shape[0] // (2 if axis == 0 else 1)
+        width = grad.shape[1] // (1 if axis == 0 else 2)
+        parts.append(Part(axis, rows, width, height // rows, base))
+        base += height // rows
+    shapes = [(part.count, part.rows, part.cols) for part in parts]
+    anywhere = pl.BlockSpec(memory_space=pl.ANY)
+    return pl.pallas_call(
+        functools.partial(reduce_kernel, parts, planes),
+        out_shape=[jax.ShapeDtypeStruct((n * r, c), BF) for n, r, c in shapes],
+        in_specs=[anywhere] * len(parts),
+        out_specs=[anywhere] * len(parts),
+        scratch_shapes=[pltpu.VMEM(shape, BF) for _ in range(4) for shape in shapes]
+        + [pltpu.SemaphoreType.DMA((base,)) for _ in range(8)],
+        compiler_params=pltpu.CompilerParams(
+            collective_id=0, has_side_effects=True, vmem_limit_bytes=56 * 1024 * 1024
+        ),
+        name="reduce_grads",
+    )(*[grad for grad, _, _ in grads])
+
+
 def body(
     tokens,
     norm1_gain,
@@ -231,16 +414,53 @@
     q_width, k_width = w_query.shape[1], w_key.shape[1]
     ff = w_gate.shape[1]
 
+    def from_row(block, ahead):
+        pairs = [((r + ahead) % rows, r) for r in range(rows)]
+        return lax.ppermute(block, "row", pairs)
+
+    def gather_rows(block, axis):
+        parts = [block] + [from_row(block, ahead) for ahead in range(1, rows)]
+        return jnp.concatenate(parts, axis=axis)
+
+    def scatter_rows(block, axis):
+        size = block.shape[axis] // rows
+        total = lax.slice_in_dim(block, 0, size, axis=axis).astype(F32)
+        for ahead in range(1, rows):
+            part = lax.slice_in_dim(block, ahead * size, (ahead + 1) * size, axis=axis)
+            total = total + from_row(part, rows - ahead).astype(F32)
+        return total.astype(BF)
+
+    def sum_planes(block, cuts):
+        planes = lax.axis_size("dp")
+        plane = lax.axis_index("dp")
+        half = planes // 2
+        edge = jnp.minimum(plane, planes - 1 - plane)
+        done = []
+        for part in jnp.split(block, cuts, axis=0):
+            for step in range(half - 1):
+                pairs = [(step, step + 1), (planes - 1 - step, planes - 2 - step)]
+                come = lax.ppermute(part, "dp", pairs)
+                part = (part.astype(F32) + come.astype(F32)).astype(BF)
+            come = lax.ppermute(part, "dp", [(half - 1, half), (half, half - 1)])
+            part = (part.astype(F32) + come.astype(F32)).astype(BF)
+            for step in reversed(range(half - 1)):
+                pairs = [(step + 1, step), (planes - 2 - step, planes - 1 - step)]
+                come = lax.ppermute(part, "dp", pairs)
+                part = jnp.where(edge == step, come, part)
+            done.append(part)
+        return jnp.concatenate(done, axis=0)
+
     def to_members(block):
         parts = block.reshape(pieces, span, width)
         parts = jnp.stack([parts[:members], parts[members:][::-1]], axis=1)
         moved = lax.all_to_all(parts, ("row", "side"), 0, 0, tiled=True)
-        moved = moved.reshape(rows, cores, 2 * span, width).transpose(1, 2, 0, 3)
+        moved = jnp.roll(moved.reshape(rows, cores, 2 * span, width), -row_index, 0)
+        moved = moved.transpose(1, 2, 0, 3)
         return moved.reshape(mine, rows * width)
 
     def from_members(block):
         parts = block.reshape(cores, 2, span, rows, width).transpose(3, 0, 1, 2, 4)
-        parts = parts.reshape(members, 2, span, width)
+        parts = jnp.roll(parts, row_index, 0).reshape(members, 2, span, width)
         moved = lax.all_to_all(parts, ("row", "side"), 0, 0, tiled=True)
         moved = jnp.concatenate([moved[:, 0], moved[:, 1][::-1]], axis=0)
         return moved.reshape(shard, width)
@@ -256,18 +476,17 @@
         + jnp.stack([member, pieces - 1 - member] * 2).astype(jnp.int32) * span
     )
 
+    states = to_members(tokens).astype(F32)
+    gain_one = gather_rows(norm1_gain, 0)
+    gain_two = gather_rows(norm2_gain, 0)
     w_project = jnp.concatenate([w_query, w_key, w_value], axis=1)
-    w_project = lax.all_gather(w_project, ("group", "side", "row"), axis=0, tiled=True)
-    w_project = w_project.reshape(cols, D, q_width + 2 * k_width)
-    states = to_members(tokens).astype(F32)
-    w_out_all = lax.all_gather(w_out, ("group", "side", "row"), axis=0)
-    w_out_all = w_out_all.reshape(cols, rows, q_width, width).transpose(0, 2, 1, 3)
-    w_out_all = w_out_all.reshape(QH * HD, D)
-    w_gate_all = lax.all_gather(w_gate, "row", axis=0, tiled=True)
-    w_up_all = lax.all_gather(w_up, "row", axis=0, tiled=True)
-    w_down_all = lax.all_gather(w_down, "row", axis=0).transpose(1, 0, 2).reshape(ff, D)
-    gain_one = lax.all_gather(norm1_gain, "row", axis=0, tiled=True)
-    gain_two = lax.all_gather(norm2_gain, "row", axis=0, tiled=True)
+    w_project = gather_rows(w_project, 0)
+    w_project = lax.all_gather(w_project, ("group", "side"), axis=0)
+    w_out_all = gather_rows(w_out, 1)
+    w_out_all = lax.all_gather(w_out_all, ("group", "side"), axis=0, tiled=True)
+    w_gate_all = gather_rows(w_gate, 0)
+    w_up_all = gather_rows(w_up, 0)
+    w_down_all = gather_rows(w_down, 1)
     target = to_members(teacher)
 
     half = HD // 2
@@ -339,14 +558,8 @@
     d_normed = lax.psum_scatter(
         d_normed.astype(BF), ("group", "side"), scatter_dimension=0, tiled=True
     ).astype(F32)
-    grad_gate = dot(normed_all, d_gate, ((0,), (0,))).astype(BF)
-    grad_up = dot(normed_all, d_up, ((0,), (0,))).astype(BF)
-    grad_down = lax.psum_scatter(grad_down, "row", scatter_dimension=1, tiled=True)
-    grad_gate = lax.psum_scatter(grad_gate, "row", scatter_dimension=0, tiled=True)
-    grad_up = lax.psum_scatter(grad_up, "row", scatter_dimension=0, tiled=True)
-    grad_down = lax.psum(grad_down, "dp")
-    grad_gate, grad_up, _ = lax.optimization_barrier((grad_gate, grad_up, grad_down))
-    grad_gate, grad_up = lax.psum((grad_gate, grad_up), "dp")
+    d_gate_up = jnp.concatenate([d_gate, d_up], axis=1)
+    grad_gate_up = dot(normed_all, d_gate_up, ((0,), (0,))).astype(BF)
 
     norm_two_part = jnp.sum(d_normed * hidden * inverse_two, axis=0)
     d_hidden = d_result + norm_back(hidden, inverse_two, gain_two, d_normed)
@@ -381,20 +594,20 @@
     )
     grad_project = grad_project.astype(BF).transpose(0, 2, 1)
     grad_project = lax.psum_scatter(
-        grad_project.reshape(cols * D, -1),
-        ("group", "side", "row"),
-        scatter_dimension=0,
-        tiled=True,
-    )
-    grad_out = grad_out.reshape(cols, q_width, rows, width).transpose(0, 2, 1, 3)
-    grad_out = lax.psum_scatter(
-        grad_out.reshape(cols * rows * q_width, width),
-        ("group", "side", "row"),
-        scatter_dimension=0,
-        tiled=True,
-    )
-    grad_project, grad_out, _ = lax.optimization_barrier((grad_project, grad_out, grad_gate))
-    grad_project, grad_out = lax.psum((grad_project, grad_out), "dp")
+        grad_project.reshape(cols * D, -1), ("group", "side"), scatter_dimension=0, tiled=True
+    )
+    grad_out = lax.psum_scatter(grad_out, ("group", "side"), scatter_dimension=0, tiled=True)
+    if rows == 2 and lax.axis_size("dp") == 4:
+        grad_down, grad_gate_up, grad_out, grad_project = reduce_all(
+            4, [(grad_down, 1, 128), (grad_gate_up, 0, 64), (grad_out, 1, 64), (grad_project, 0, 256)]
+        )
+    else:
+        grad_down = sum_planes(scatter_rows(grad_down, 1), 2)
+        grad_gate_up = sum_planes(scatter_rows(grad_gate_up, 0), 4)
+        grad_out = sum_planes(scatter_rows(grad_out, 1), 1)
+        grad_project = sum_planes(scatter_rows(grad_project, 0), 2)
+    norm_one_part = jnp.roll(norm_one_part.reshape(rows, width), row_index, 0).reshape(D)
+    norm_two_part = jnp.roll(norm_two_part.reshape(rows, width), row_index, 0).reshape(D)
     small = jnp.concatenate([norm_one_part, norm_two_part, query_gain_part, key_gain_part])
     small = lax.psum(small, ("dp", "row", "group", "side"))
     grad_norm1 = lax.dynamic_slice_in_dim(small, row_index * width, width, 0)
@@ -411,8 +624,8 @@
         small[2 * D + HD :],
         grad_out.astype(F32),
         grad_norm2,
-        grad_gate.astype(F32),
-        grad_up.astype(F32),
+        grad_gate_up[:, :ff].astype(F32),
+        grad_gate_up[:, ff:].astype(F32),
         grad_down.astype(F32),
     )
 

time: 1450 us -> 1300 us (0.90)
  waiting for transfers between devices: 778 us -> 450 us
  Pallas kernels: 66.3 us -> 307 us
  blocking collectives: 112 us -> 61.9 us
  local copies, waits for them, and re-layouts: 174 us -> 138 us
  matrix products: 207 us -> 224 us
    pallas_call x0 -> x1, Pallas kernels: none -> 241 us  [reduce_all(): pl.pallas_call(functools.partial(reduce_kernel, parts, planes), out_shape...]
    ppermute x0 -> x7, waiting for transfers between devices: none -> 228 us  [from_row(): return lax.ppermute(block, 'row', pairs)]
    psum x3 -> x0, waiting for transfers between devices: 219 us -> none  [the longest x1 106 us: body(): grad_down = lax.psum(grad_down, 'dp')]
    reduce_scatter x5 -> x2, waiting for transfers between devices: 187 us -> 0.01 us  [the longest x1 0.01 us: body(): lax.psum_scatter(grad_out, ('group', 'side'), scatter_dimension=0, tiled=...]
    all_gather x5 -> x2, waiting for transfers between devices: 142 us -> 16.6 us  [the longest x1 16.6 us: body(): w_project = lax.all_gather(w_project, ('group', 'side'), axis=0)]
    all_gather x1, waiting for transfers between devices: 60.3 us -> 0.01 us  [body(): lax.all_gather(normed_two, ('group', 'side'), axis=0, tiled=True)]
    all_gather x2 -> x0, blocking collectives: 41.2 us -> none  [the longest x1 36.4 us: body(): gain_one = lax.all_gather(norm1_gain, 'row', axis=0, tiled=True)]
    reduce_scatter x1, waiting for transfers between devices: 41.6 us -> 71.8 us  [body(): lax.psum_scatter(d_normed.astype(BF), ('group', 'side'), scatter_dimensio...]
  transfers between devices with their start and end apart: 23 -> 21, of which waited for: 17 -> 13; matrix products, arithmetic and copies ran while one was open for 25% -> 15% of each run, Pallas kernels for 5% -> 2%
where the time goes in v2:
time: 1300 us; the launch traced here: 1290 us
  waiting for transfers between devices  450 us (35%)
  Pallas kernels  307 us (24%)
  matrix products  224 us (17%)
  local copies, waits for them, and re-layouts  138 us (11%)
  other arithmetic  65.1 us (5%)
  blocking collectives  61.9 us (5%)
  starting transfers between devices  30.5 us (2%)
  between operations  16.4 us (1%)
    pallas_call x1, Pallas kernels, reduce_all(): pl.pallas_call(functools.partial(reduce_kernel, parts, planes), out_shape...  241 us
    ppermute x7, waiting for transfers between devices, from_row(): return lax.ppermute(block, 'row', pairs)  228 us
    dot_general x13, matrix products, dot(): lax.dot_general(left, right, (dims, ((), ())), preferred_element_type=F32)  217 us
    reduce_scatter x1, waiting for transfers between devices, body(): lax.psum_scatter(d_normed.astype(BF), ('group', 'side'), scatter_dimensio...  71.8 us
    psum x1, blocking collectives, body(): small = lax.psum(small, ('dp', 'row', 'group', 'side'))  61.9 us
    all_gather x1, waiting for transfers between devices, body(): lax.all_gather(d_result.astype(BF), ('group', 'side'), axis=0, tiled=True)  58.4 us
    unnamed x150, local copies, waits for them, and re-layouts  43 us
    pallas_call x1, Pallas kernels, attend_back(): pl.pallas_call(functools.partial(attend_back_kernel, chunks, tokens // ch...  37.1 us
  transfers between devices with their start and end apart: 21, of which 13 were waited for; matrix products, arithmetic and copies ran while one was open for 15% of the time, Pallas kernels for 2%

profile of v2, /device:TPU:0, one launch (start us, length us, event | category | flops | bytes accessed | tf_op | source)
XLA Modules:
  0.0 1293.3 jit_solution(4092756200740727691)
XLA Ops:
  13.4 21.8 %collective-permute-done = bf16[1024,480]{0,1:T(8,128)(2,1)S(1)} collective-permute-done((bf16[1024,480]{0,1:T(8,128)(2,1)S(1)}, bf16[1024,480]{0,1:T(8,128)(2,1)S(1)}, u32[]{:S(2)}, u32[]{:S(2)}) %collective-permute-start) | collective-permute-done | bytes 983072 | tf_op jit(solution)/shard_map/ppermute | solution.py:419
  45.2 22.6 %collective-permute-done.1 = f32[1024]{0:T(1024)S(1)} collective-permute-done((f32[1024]{0:T(1024)S(1)}, f32[1024]{0:T(1024)S(1)}, u32[]{:S(2)}, u32[]{:S(2)}) %collective-permute-start.1) | collective-permute-done | bytes 4128 | tf_op jit(solution)/shard_map/ppermute | solution.py:419
  77.0 16.6 %all-gather.14.cloned.1.call-done = bf16[8192,480]{0,1:T(8,128)(2,1)} async-done(((bf16[2048,480]{0,1:T(8,128)(2,1)}), bf16[8192,480]{0,1:T(8,128)(2,1)}) %all-gather.14.cloned.1.call-update) | async-done | bytes 7864336 | tf_op jit(solution)/shard_map/all_gather | solution.py:484
  108.2 23.0 %collective-permute-done.2 = bf16[320,1024]{1,0:T(8,128)(2,1)S(1)} collective-permute-done((bf16[320,1024]{1,0:T(8,128)(2,1)S(1)}, bf16[320,1024]{1,0:T(8,128)(2,1)S(1)}, u32[]{:S(2)}, u32[]{:S(2)}) %collective-permute-start.2) | collective-permute-done | bytes 655392 | tf_op jit(solution)/shard_map/ppermute | solution.py:419
  176.9 29.5 %attend.1 = (f32[5,4,64,512]{3,2,1,0:T(8,128)S(1)}, f32[5,4,512]{2,1,0:T(4,128)S(1)}) custom-call(s32[4]{0:T(128)S(1)} %fusion.53.first_ref, bf16[5,4,64,512]{3,2,1,0:T(8,128)(2,1)S(1)} %copy-done.2, bf16[5,2048,64]{2,1,0:T(8,128)(2,1)S(1)} %copy.108.key_ref, bf16[5,80,2048]{2,1,0:T(8,128)(2,1)S(1)} %concatenate.99.clone.value_ref), custom_call_target="tpu_custom_call" | custom-call | tf_op jit(solution)/shard_map/attend/pallas_call | solution.py:149
  230.1 50.3 %collective-permute-done.4 = bf16[1024,1280]{1,0:T(8,128)(2,1)S(1)} collective-permute-done((bf16[1024,1280]{1,0:T(8,128)(2,1)}, bf16[1024,1280]{1,0:T(8,128)(2,1)S(1)}, u32[]{:S(2)}, u32[]{:S(2)}) %collective-permute-start.4) | collective-permute-done | bytes 2621472 | tf_op jit(solution)/shard_map/ppermute | solution.py:419
  280.5 56.0 %collective-permute-done.5 = bf16[1024,1280]{1,0:T(8,128)(2,1)S(1)} collective-permute-done((bf16[1024,1280]{1,0:T(8,128)(2,1)}, bf16[1024,1280]{1,0:T(8,128)(2,1)S(1)}, u32[]{:S(2)}, u32[]{:S(2)}) %collective-permute-start.5) | collective-permute-done | bytes 2621472 | tf_op jit(solution)/shard_map/ppermute | solution.py:419
  336.7 52.9 %collective-permute-done.6 = bf16[1280,1024]{1,0:T(8,128)(2,1)S(1)} collective-permute-done((bf16[1280,1024]{1,0:T(8,128)(2,1)}, bf16[1280,1024]{1,0:T(8,128)(2,1)S(1)}, u32[]{:S(2)}, u32[]{:S(2)}) %collective-permute-start.6) | collective-permute-done | bytes 2621472 | tf_op jit(solution)/shard_map/ppermute | solution.py:419
  391.4 29.4 %fusion.66 = f32[2048,1280]{0,1:T(8,128)} fusion(bf16[2048,2048]{1,0:T(8,128)(2,1)} %all-gather.10.cloned.1.call-done, bf16[2048,1280]{1,0:T(8,128)(2,1)} %copy-done.35), kind=kOutput, calls=%fused_computation.182 | convolution fusion | flops 10737418240 | bytes 24117248 | tf_op jit(solution)/shard_map/dot_general | solution.py:29
  420.9 21.1 %multiply_convert_fusion.2 = (bf16[2048,1280]{0,1:T(8,128)(2,1)}, f32[2048,1280]{0,1:T(8,128)}) fusion(f32[2048,1280]{0,1:T(8,128)} %fusion.66, bf16[2048,2048]{1,0:T(8,128)(2,1)} %all-gather.10.cloned.1.call-done, bf16[2048,1280]{1,0:T(8,128)(2,1)} %copy-done.34), kind=kOutput, calls=%fused_computation.7 | convolution fusion | flops 10753146880 | bytes 39845888 | tf_op jit(solution)/shard_map/dot_general | solution.py:29
  442.0 17.0 %convolution_convert_fusion.3 = bf16[2048,2048]{1,0:T(8,128)(2,1)} fusion(bf16[2048,1280]{0,1:T(8,128)(2,1)} %get-tuple-element.154, bf16[1280,2048]{1,0:T(8,128)(2,1)} %constant_dynamic-update-slice_fusion.7), kind=kOutput, calls=%fused_computation.18 | convolution fusion | flops 10741612544 | bytes 18874368 | tf_op jit(solution)/shard_map/dot_general | solution.py:29
  467.6 25.0 %all-to-all-done.2 = bf16[4,2,128,1024]{3,2,1,0:T(8,128)(2,1)} async-done(((bf16[4,2,128,1024]{3,2,1,0:T(8,128)(2,1)}), bf16[4,2,128,1024]{3,2,1,0:T(8,128)(2,1)}, u32[]{:S(2)}, u32[]{:S(2)}) %all-to-all-start.2) | async-done | bytes 2097184 | tf_op jit(solution)/shard_map/all_to_all | solution.py:456
  502.3 28.8 %reduce-scatter.6.cloned.1.call-done = bf16[512,2048]{1,0:T(8,128)(2,1)} async-done(((bf16[2048,2048]{1,0:T(8,128)(2,1)}), bf16[512,2048]{1,0:T(8,128)(2,1)}) %reduce-scatter.6.cloned.1.call-update) | async-done | bytes 2097168 | tf_op jit(solution)/shard_map/reduce_scatter | solution.py:545
  537.8 58.4 %all-gather.12.cloned.1.call-done = bf16[2048,2048]{1,0:T(8,128)(2,1)} async-done(((bf16[512,2048]{1,0:T(8,128)(2,1)}), bf16[2048,2048]{1,0:T(8,128)(2,1)}) %all-gather.12.cloned.1.call-update) | async-done | bytes 8388624 | tf_op jit(solution)/shard_map/all_gather | solution.py:552
  596.2 25.1 %multiply_convert_fusion.1 = (bf16[2048,1280]{0,1:T(8,128)(2,1)}, bf16[2048,1280]{0,1:T(8,128)(2,1)}) fusion(f32[2048,1280]{0,1:T(8,128)} %fusion.66, f32[2048,1280]{0,1:T(8,128)} %get-tuple-element.155, bf16[2048,2048]{1,0:T(8,128)(2,1)} %all-gather.12.cloned.1.call-done, bf16[1280,2048]{1,0:T(8,128)(2,1)} %constant_dynamic-update-slice_fusion.7), kind=kOutput, calls=%fused_computation.6 | convolution fusion | flops 10771496960 | bytes 45088768 | tf_op jit(solution)/shard_map/dot_general | solution.py:29
  621.3 18.0 %fusion.67 = f32[2048,2048]{1,0:T(8,128)} fusion(bf16[2048,1280]{0,1:T(8,128)(2,1)} %get-tuple-element.107, bf16[2048,1280]{1,0:T(8,128)(2,1)} %copy-done.34), kind=kOutput, calls=%fused_computation.183 | convolution fusion | flops 10737418240 | bytes 27262976 | tf_op jit(solution)/shard_map/dot_general | solution.py:29
  639.3 19.4 %add_convert_fusion = bf16[2048,2048]{1,0:T(8,128)(2,1)} fusion(f32[2048,2048]{1,0:T(8,128)} %fusion.67, bf16[2048,1280]{0,1:T(8,128)(2,1)} %get-tuple-element.106, bf16[2048,1280]{1,0:T(8,128)(2,1)} %copy-done.35), kind=kOutput, calls=%fused_computation | convolution fusion | flops 10745806848 | bytes 35651584 | tf_op jit(solution)/shard_map/dot_general | solution.py:29
  658.8 71.8 %reduce-scatter.8.cloned.1.call-done = bf16[512,2048]{1,0:T(8,128)(2,1)} async-done(((bf16[2048,2048]{1,0:T(8,128)(2,1)}), bf16[512,2048]{1,0:T(8,128)(2,1)}) %reduce-scatter.8.cloned.1.call-update) | async-done | bytes 2097168 | tf_op jit(solution)/shard_map/reduce_scatter | solution.py:558
  747.8 37.1 %attend_back.1 = (f32[5,4,64,512]{3,2,1,0:T(8,128)S(1)}, f32[5,2048,64]{2,1,0:T(8,128)S(1)}, f32[5,2048,64]{2,1,0:T(8,128)S(1)}) custom-call(s32[4]{0:T(128)S(1)} %fusion.53.first_ref, bf16[5,4,64,512]{3,2,1,0:T(8,128)(2,1)S(1)} %copy-done.3, bf16[5,4,64,512]{3,2,1,0:T(8,128)(2,1)S(1)} %bitcast.170, f32[5,4,512]{2,1,0:T(4,128)S(1)} %get-tuple-element.25.log_ref, ...), custom_call_target="tpu_custom_call" | custom-call | tf_op jit(solution)/shard_map/attend_back/pallas_call | solution.py:173
  819.2 20.8 %reduce-scatter.10.cloned.1.call-done = bf16[1,2,5,512,64]{3,4,2,1,0:T(8,128)(2,1)} async-done(((bf16[4,2,5,512,64]{3,4,2,1,0:T(8,128)(2,1)}), bf16[1,2,5,512,64]{3,4,2,1,0:T(8,128)(2,1)}) %reduce-scatter.10.cloned.1.call-update) | async-done | bytes 655376 | tf_op jit(solution)/shard_map/reduce_scatter | solution.py:575
  861.2 29.8 %convolution_convert_fusion.refs_1_ = bf16[2048,2560]{1,0:T(8,128)(2,1)} fusion(bf16[2048,2048]{1,0:T(8,128)(2,1)} %all-gather.10.cloned.1.call-done, bf16[2048,1280]{0,1:T(8,128)(2,1)} %get-tuple-element.107, bf16[2048,1280]{0,1:T(8,128)(2,1)} %get-tuple-element.106), kind=kOutput, calls=%fused_computation.1 | convolution fusion | flops 21501050880 | bytes 29360128 | tf_op jit(solution)/shard_map/dot_general | solution.py:29
  935.7 16.5 %convolution_convert_fusion.2.refs_0_ = bf16[1280,2048]{1,0:T(8,128)(2,1)} fusion(bf16[2048,1280]{0,1:T(8,128)(2,1)} %get-tuple-element.154, bf16[2048,2048]{1,0:T(8,128)(2,1)} %all-gather.12.cloned.1.call-done), kind=kOutput, calls=%fused_computation.17 | convolution fusion | flops 10740039680 | bytes 18874368 | tf_op jit(solution)/shard_map/dot_general | solution.py:29
  956.4 61.9 %psum.7 = f32[4224]{0:T(1024)S(1)} all-reduce(f32[4224]{0:T(1024)S(1)} %concatenate.110), channel_id=1, replica_groups=mesh['dp'=4,'row'=2,'group'=2,'side'=2] {'dp','row','group','side'}, use_global_device_ids=true, to_apply=%region_16.19 | all-reduce | flops 4224 | bytes 33792 | tf_op jit(solution)/shard_map/psum | solution.py:612
  1029.8 240.8 %reduce_grads.1 = (bf16[1280,1024]{1,0:T(8,128)(2,1)}, bf16[1024,2560]{1,0:T(8,128)(2,1)}, bf16[320,1024]{1,0:T(8,128)(2,1)}, bf16[1024,480]{1,0:T(8,128)(2,1)}) custom-call(bf16[1280,2048]{1,0:T(8,128)(2,1)} %convolution_convert_fusion.2.refs_0_, bf16[2048,2560]{1,0:T(8,128)(2,1)} %convolution_convert_fusion.refs_1_, ...), custom_call_target="tpu_custom_call" | custom-call | tf_op jit(solution)/shard_map/reduce_grads/pallas_call | solution.py:372
  (298 shorter events, 283.3 us)
Async XLA Ops:
  7.2 86.4 %all-gather.14.cloned.1.call-start = ((), (), s32[]{:S(2)}) async-start(), calls=%async_computation.17 | async-start | bytes 9830400 | tf_op jit(solution)/shard_map/all_gather | solution.py:484
  10.4 24.8 %collective-permute-start = (bf16[1024,480]{0,1:T(8,128)(2,1)S(1)}, bf16[1024,480]{0,1:T(8,128)(2,1)S(1)}, u32[]{:S(2)}, u32[]{:S(2)}) collective-permute-start(bf16[1024,480]{0,1:T(8,128)(2,1)S(1)} %constant_dynamic-update-slice_fusion), channel_id=1, source_target_pairs={{4,0},{0,4},{5,1},{1,5},{6,2},{2,6},{7,3},{3,7},{12,8},{8,12},{13,... | collective-permute-start | bytes 2949128 | tf_op jit(solution)/shard_map/ppermute | solution.py:419
  38.4 29.4 %all-to-all-start = ((bf16[4,2,128,1024]{3,2,1,0:T(8,128)(2,1)}), bf16[4,2,128,1024]{3,2,1,0:T(8,128)(2,1)S(1)}, u32[]{:S(2)}, u32[]{:S(2)}) async-start(bf16[4,2,128,1024]{3,2,1,0:T(8,128)(2,1)} %pad_maximum_fusion.2), calls=%async_computation | async-start | bytes 4194304 | tf_op jit(solution)/shard_map/all_to_all | solution.py:456
  42.0 100.5 %all-gather.16.cloned.1.call-start = ((), (), s32[]{:S(2)}) async-start(), calls=%async_computation.18 | async-start | bytes 3276800 | tf_op jit(solution)/shard_map/all_gather | solution.py:511
  42.1 25.7 %collective-permute-start.1 = (f32[1024]{0:T(1024)S(1)}, f32[1024]{0:T(1024)S(1)}, u32[]{:S(2)}, u32[]{:S(2)}) collective-permute-start(f32[1024]{0:T(1024)S(1)} %copy-done.63), channel_id=1, source_target_pairs={{4,0},{0,4},{5,1},{1,5},{6,2},{2,6},{7,3},{3,7},{12,8},{8,12},{13,... | collective-permute-start | bytes 12296 | tf_op jit(solution)/shard_map/ppermute | solution.py:419
  45.1 95.5 %copy-start.30 = (f32[32,512]{1,0:T(8,128)}, f32[32,512]{1,0:T(8,128)S(1)}, u32[]{:S(2)}) copy-start(f32[32,512]{1,0:T(8,128)S(1)} %get-tuple-element.146) | copy-start | bytes 196612
  45.1 95.5 %copy-start.32 = (f32[32,512]{1,0:T(8,128)}, f32[32,512]{1,0:T(8,128)S(1)}, u32[]{:S(2)}) copy-start(f32[32,512]{1,0:T(8,128)S(1)} %get-tuple-element.147) | copy-start | bytes 196612
  106.6 102.5 %all-gather.8.cloned.1.call-start = ((), (), s32[]{:S(2)}) async-start(), calls=%async_computation.9 | async-start | bytes 6553600 | tf_op jit(solution)/shard_map/all_gather | solution.py:486
  106.7 24.5 %collective-permute-start.2 = (bf16[320,1024]{1,0:T(8,128)(2,1)S(1)}, bf16[320,1024]{1,0:T(8,128)(2,1)S(1)}, u32[]{:S(2)}, u32[]{:S(2)}) collective-permute-start(bf16[320,1024]{1,0:T(8,128)(2,1)S(1)} %copy-done.40), channel_id=1, source_target_pairs={{4,0},{0,4},{5,1},{1,5},{6,2},{2,6},{7,3},{3,7},{12,8},{8,12},{13,... | collective-permute-start | bytes 1966088 | tf_op jit(solution)/shard_map/ppermute | solution.py:419
  132.4 259.0 %all-gather.10.cloned.1.call-start = ((), (), s32[]{:S(2)}) async-start(), calls=%async_computation.10 | async-start | bytes 10485760 | tf_op jit(solution)/shard_map/all_gather | solution.py:539
  132.5 4.2 collective-permute-start.3
  220.2 310.9 %reduce-scatter.6.cloned.1.call-start = ((), (), s32[]{:S(2)}) async-start(), calls=%async_computation.11 | async-start | bytes 10485760 | tf_op jit(solution)/shard_map/reduce_scatter | solution.py:545
  220.3 60.1 %collective-permute-start.4 = (bf16[1024,1280]{1,0:T(8,128)(2,1)}, bf16[1024,1280]{1,0:T(8,128)(2,1)S(1)}, u32[]{:S(2)}, u32[]{:S(2)}) collective-permute-start(bf16[1024,1280]{1,0:T(8,128)(2,1)} %param.29), channel_id=1, source_target_pairs={{4,0},{0,4},{5,1},{1,5},{6,2},{2,6},{7,3},{3,7},{12,8},{8,12},{13,... | collective-permute-start | bytes 7864328 | tf_op jit(solution)/shard_map/ppermute | solution.py:419
  222.3 114.2 %collective-permute-start.5 = (bf16[1024,1280]{1,0:T(8,128)(2,1)}, bf16[1024,1280]{1,0:T(8,128)(2,1)S(1)}, u32[]{:S(2)}, u32[]{:S(2)}) collective-permute-start(bf16[1024,1280]{1,0:T(8,128)(2,1)} %param.30), channel_id=1, source_target_pairs={{4,0},{0,4},{5,1},{1,5},{6,2},{2,6},{7,3},{3,7},{12,8},{8,12},{13,... | collective-permute-start | bytes 7864328 | tf_op jit(solution)/shard_map/ppermute | solution.py:419
  222.4 167.2 %collective-permute-start.6 = (bf16[1280,1024]{1,0:T(8,128)(2,1)}, bf16[1280,1024]{1,0:T(8,128)(2,1)S(1)}, u32[]{:S(2)}, u32[]{:S(2)}) collective-permute-start(bf16[1280,1024]{1,0:T(8,128)(2,1)} %param.31), channel_id=1, source_target_pairs={{4,0},{0,4},{5,1},{1,5},{6,2},{2,6},{7,3},{3,7},{12,8},{8,12},{13,... | collective-permute-start | bytes 7864328 | tf_op jit(solution)/shard_map/ppermute | solution.py:419
  280.5 109.1 %copy-start.35 = (bf16[2048,1280]{1,0:T(8,128)(2,1)}, bf16[2048,1280]{1,0:T(8,128)(2,1)S(1)}, u32[]{:S(2)}) copy-start(bf16[2048,1280]{1,0:T(8,128)(2,1)S(1)} %constant_dynamic-update-slice_fusion.3) | copy-start | bytes 15728644
  462.4 30.3 %all-to-all-start.2 = ((bf16[4,2,128,1024]{3,2,1,0:T(8,128)(2,1)}), bf16[4,2,128,1024]{3,2,1,0:T(8,128)(2,1)}, u32[]{:S(2)}, u32[]{:S(2)}) async-start(bf16[4,2,128,1024]{3,2,1,0:T(8,128)(2,1)} %pad_maximum_fusion.4), calls=%async_computation.3 | async-start | bytes 4194304 | tf_op jit(solution)/shard_map/all_to_all | solution.py:456
  466.9 129.3 %all-gather.12.cloned.1.call-start = ((), (), s32[]{:S(2)}) async-start(), calls=%async_computation.12 | async-start | bytes 10485760 | tf_op jit(solution)/shard_map/all_gather | solution.py:552
  537.7 192.9 %reduce-scatter.8.cloned.1.call-start = ((), (), s32[]{:S(2)}) async-start(), calls=%async_computation.13 | async-start | bytes 10485760 | tf_op jit(solution)/shard_map/reduce_scatter | solution.py:558
  658.7 181.3 %reduce-scatter.10.cloned.1.call-start = ((), (), s32[]{:S(2)}) async-start(), calls=%async_computation.14 | async-start | bytes 3276800 | tf_op jit(solution)/shard_map/reduce_scatter | solution.py:575
  805.2 224.6 %reduce-scatter.12.cloned.1.call-start = ((), (), s32[]{:S(2)}) async-start(), calls=%async_computation.15 | async-start | bytes 6553600 | tf_op jit(solution)/shard_map/reduce_scatter | solution.py:599
  813.1 216.7 %reduce-scatter.14.cloned.1.call-start = ((), (), s32[]{:S(2)}) async-start(), calls=%async_computation.16 | async-start | bytes 10485760 | tf_op jit(solution)/shard_map/reduce_scatter | solution.py:596
  898.1 32.5 %all-to-all-start.1 = ((bf16[4,2,128,1024]{3,2,1,0:T(8,128)(2,1)}), bf16[4,2,128,1024]{3,2,1,0:T(8,128)(2,1)S(1)}, u32[]{:S(2)}, u32[]{:S(2)}) async-start(bf16[4,2,128,1024]{3,2,1,0:T(8,128)(2,1)} %bitcast.192), calls=%async_computation.2 | async-start | bytes 4194304 | tf_op jit(solution)/shard_map/all_to_all | solution.py:464
  930.6 88.9 %all-to-all-start.3 = ((f32[4,2,128,1024]{3,2,1,0:T(8,128)}), f32[4,2,128,1024]{3,2,1,0:T(8,128)}, u32[]{:S(2)}, u32[]{:S(2)}) async-start(f32[4,2,128,1024]{3,2,1,0:T(8,128)} %bitcast.187), calls=%async_computation.6 | async-start | bytes 8388608 | tf_op jit(solution)/shard_map/all_to_all | solution.py:464
  (65 other events, 855.1 us)
Sparse Core Ops, SparseCore 0:
  36.7 56.7 all-gather.13
  106.7 32.5 all-gather.15
  141.4 40.5 all-gather.7
  220.3 58.5 all-gather.9
  459.2 71.9 reduce-scatter.5
  537.9 58.2 all-gather.11
  658.9 71.6 reduce-scatter.7
  805.3 34.6 reduce-scatter.9
  843.3 51.3 reduce-scatter.11
  897.2 72.2 reduce-scatter.13

commit v3 on v2

--- a/solution.py
+++ b/solution.py
@@ -201,26 +201,47 @@
 
 
 AHEAD = 4
+SLOTS = AHEAD + 2
+LAG = 4
+SMALL = 40
 
 
 class Part:
-    def __init__(self, axis, rows, cols, count, base):
-        self.axis, self.rows, self.cols, self.count, self.base = axis, rows, cols, count, base
-
-    def cut(self, ref, index, half):
-        first = index * self.rows
+    def __init__(self, axis, rows, cols, count, base, col):
+        self.axis, self.rows, self.cols = axis, rows, cols
+        self.count, self.base, self.col = count, base, col
+
+    def cut(self, ref, index, half, lead=()):
+        first = pl.ds(index * self.rows, self.rows)
         if self.axis == 0:
-            return ref.at[pl.ds(half * self.rows * self.count + first, self.rows), :]
-        return ref.at[pl.ds(first, self.rows), pl.ds(half * self.cols, self.cols)]
+            first = pl.ds((half * self.count + index) * self.rows, self.rows)
+            return ref.at[(*lead, first, slice(None))]
+        return ref.at[(*lead, first, pl.ds(half * self.cols, self.cols))]
 
 
 def reduce_kernel(parts, planes, *refs):
     count = len(parts)
-    grads, outs, own, near, far, wide = (refs[i * count : (i + 1) * count] for i in range(6))
-    own_sem, out_sem, row_send, row_recv, in_send, far_recv, mid_send, wide_recv = refs[6 * count :]
-    plane = lax.axis_index("dp")
-    row = lax.axis_index("row")
-    other_row = {"row": 1 - row}
+    refs = list(refs)
+
+    def take(number):
+        taken = refs[:number]
+        del refs[:number]
+        return taken
+
+    grads = take(count)
+    (small_ref,) = take(1)
+    outs = take(count)
+    (small_out,) = take(1)
+    near, far, wide, own = take(count), take(count), take(count), take(count)
+    col_parts = [j for j in range(count) if parts[j].col]
+    mate_in = dict(zip(col_parts, take(len(col_parts))))
+    far_in = dict(zip(col_parts, take(len(col_parts))))
+    own_sem, out_sem, row_send, row_recv, in_send, far_recv, mid_send, wide_recv = take(8)
+    col_own, col_send, col_recv, x_send, x_recv, small_local, small_send, small_recv = take(8)
+    small_in, small_sum = take(2)
+    plane, row = lax.axis_index("dp"), lax.axis_index("row")
+    group, side = lax.axis_index("group"), lax.axis_index("side")
+    other_row, mate, far_dev = {"row": 1 - row}, {"side": 1 - side}, {"group": 1 - group}
     at_end = (plane == 0) | (plane == planes - 1)
     low = plane < planes // 2
     end_next = {"dp": jnp.where(low, 1, planes - 2)}
@@ -237,24 +258,69 @@
     def greet(where):
         pl.semaphore_signal(barrier, 1, device_id=where, device_id_type=pl.DeviceIdType.MESH)
 
-    greet(other_row)
+    for where in (other_row, mate, far_dev):
+        greet(where)
 
     @pl.when(at_end)
     def _():
         greet(end_next)
-        pl.semaphore_wait(barrier, 2)
+        pl.semaphore_wait(barrier, 4)
 
     @pl.when(jnp.logical_not(at_end))
     def _():
         greet(mid_outer)
         greet(mid_other)
-        pl.semaphore_wait(barrier, 3)
+        pl.semaphore_wait(barrier, 5)
+
+    def col_slot(j, half, index):
+        before = sum(2 * parts[i].count for i in col_parts if i < j)
+        return before + half * parts[j].count + index
+
+    def col_own_copy(j, half, index, target):
+        return pltpu.make_async_copy(
+            parts[j].cut(grads[j], index, half, (2 * target + side,)),
+            own[j].at[target, half, index],
+            col_own.at[target, col_slot(j, half, index)],
+        )
+
+    def col_copy(j, half, index, target):
+        slot = col_slot(j, half, index)
+        return remote(
+            parts[j].cut(grads[j], index, half, (2 * target + 1 - side,)),
+            mate_in[j].at[target, half, index],
+            col_send.at[target, slot],
+            col_recv.at[target, slot],
+            mate,
+        )
+
+    def x_copy(j, half, index):
+        slot = col_slot(j, half, index)
+        return remote(
+            mate_in[j].at[1 - group, half, index],
+            far_in[j].at[half, index],
+            x_send.at[slot],
+            x_recv.at[slot],
+            far_dev,
+        )
+
+    def take_col(j, half, index):
+        for target in range(2):
+            col_own_copy(j, half, index, target).wait()
+            col_copy(j, half, index, target).wait_recv()
+            total = own[j][target, half, index].astype(F32)
+            total += mate_in[j][target, half, index].astype(F32)
+            mate_in[j][target, half, index] = total.astype(BF)
+        x_copy(j, half, index).start()
+
+    def take_x(j, half, index):
+        x_copy(j, half, index).wait_recv()
+        total = far_in[j][half, index].astype(F32) + mate_in[j][group, half, index].astype(F32)
+        far_in[j][half, index] = total.astype(BF)
 
     def row_copy(j, index):
         slot = parts[j].base + index
-        return remote(
-            parts[j].cut(grads[j], index, 1), near[j].at[index], row_send.at[slot], row_recv.at[slot], other_row
-        )
+        source = far_in[j].at[1, index] if parts[j].col else parts[j].cut(grads[j], index, 1)
+        return remote(source, near[j].at[index], row_send.at[slot], row_recv.at[slot], other_row)
 
     def in_copy(j, index):
         slot = parts[j].base + index
@@ -274,7 +340,9 @@
 
     def own_copy(j, index):
         slot = parts[j].base + index
-        return pltpu.make_async_copy(parts[j].cut(grads[j], index, 0), own[j].at[index], own_sem.at[slot])
+        return pltpu.make_async_copy(
+            parts[j].cut(grads[j], index, 0), own[j].at[index % SLOTS], own_sem.at[slot]
+        )
 
     def each(step, action):
         for j, part in enumerate(parts):
@@ -284,18 +352,19 @@
             def _(j=j, index=index):
                 action(j, index)
 
-    def add(target, j, index, first, second):
-        total = first[j][index].astype(F32) + second[j][index].astype(F32)
-        target[j][index] = total.astype(BF)
-
     def send_row(j, index):
-        own_copy(j, index).start()
+        if not parts[j].col:
+            own_copy(j, index).start()
         row_copy(j, index).start()
 
     def take_row(j, index):
-        own_copy(j, index).wait()
         row_copy(j, index).wait_recv()
-        add(near, j, index, near, own)
+        if parts[j].col:
+            mine = far_in[j][0, index]
+        else:
+            own_copy(j, index).wait()
+            mine = own[j][index % SLOTS]
+        near[j][index] = (near[j][index].astype(F32) + mine.astype(F32)).astype(BF)
 
         @pl.when(at_end)
         def _():
@@ -303,12 +372,12 @@
 
     def take_far(j, index):
         back_copy(j, index).wait_recv()
-        add(far, j, index, far, near)
+        far[j][index] = (far[j][index].astype(F32) + near[j][index].astype(F32)).astype(BF)
         mid_copy(j, index).start()
 
     def take_wide(j, index):
         mid_copy(j, index).wait_recv()
-        add(wide, j, index, wide, far)
+        wide[j][index] = (wide[j][index].astype(F32) + far[j][index].astype(F32)).astype(BF)
         back_copy(j, index).start()
         out_copy(j, index, wide).start()
 
@@ -327,60 +396,523 @@
         back_copy(j, index).wait_send()
         out_copy(j, index, wide).wait()
 
+    def small_copy(stage, source, where):
+        return remote(small_sum.at[source], small_in.at[stage], small_send.at[stage], small_recv.at[stage], where)
+
+    plane_hops = [small_copy(0, 0, mate), small_copy(1, 1, far_dev), small_copy(2, 2, other_row)]
+    small_end = small_copy(3, 3, end_next)
+    small_mid = small_copy(4, 4, mid_other)
+    small_back = small_copy(3, 5, mid_outer)
+    small_load = pltpu.make_async_copy(small_ref, small_sum.at[0], small_local.at[0])
+    small_store = pltpu.make_async_copy(small_sum.at[5], small_out, small_local.at[1])
+
     total = sum(part.count for part in parts)
+    small_load.start()
+    for j in col_parts:
+        for half in (1, 0):
+            for index in range(parts[j].count):
+                for target in range(2):
+                    col_own_copy(j, half, index, target).start()
+                    col_copy(j, half, index, target).start()
 
     @pl.loop(0, AHEAD)
     def _(step):
         each(step, send_row)
 
-    @pl.loop(0, total + 4)
+    pieces = [(j, half, index) for j in col_parts for half in (1, 0) for index in range(parts[j].count)]
+
+    @pl.loop(0, total + LAG)
     def _(step):
         each(step + AHEAD, send_row)
         each(step, take_row)
 
         @pl.when(at_end)
         def _():
-            each(step - 4, take_back)
+            each(step - LAG, take_back)
 
         @pl.when(jnp.logical_not(at_end))
         def _():
             each(step - 1, take_far)
             each(step - 2, take_wide)
 
+        for place, piece in enumerate(pieces):
+            @pl.when(step == place + 1)
+            def _(piece=piece):
+                take_col(*piece)
+
+            @pl.when(step == place + 5)
+            def _(piece=piece):
+                take_x(*piece)
+
+        @pl.when(step == 0)
+        def _():
+            small_load.wait()
+            plane_hops[0].start()
+
+        for hop in range(3):
+            @pl.when(step == hop + 1)
+            def _(hop=hop):
+                plane_hops[hop].wait_recv()
+                small_sum[hop + 1] = small_sum[hop] + small_in[hop]
+                if hop < 2:
+                    plane_hops[hop + 1].start()
+
+        @pl.when(at_end & (step == 3))
+        def _():
+            small_end.start()
+
+        @pl.when(at_end & (step == 10))
+        def _():
+            small_end.wait_recv()
+            small_sum[5] = small_in[3]
+            small_store.start()
+
+        @pl.when(jnp.logical_not(at_end) & (step == 5))
+        def _():
+            small_back.wait_recv()
+            small_sum[4] = small_sum[3] + small_in[3]
+            small_mid.start()
+
+        @pl.when(jnp.logical_not(at_end) & (step == 7))
+        def _():
+            small_mid.wait_recv()
+            small_sum[5] = small_sum[4] + small_in[4]
+            small_back.start()
+            small_store.start()
+
+    for copy in plane_hops:
+        copy.wait_send()
+    small_store.wait()
+    for j, half, index in pieces:
+        for target in range(2):
+            col_copy(j, half, index, target).wait_send()
+        x_copy(j, half, index).wait_send()
+
     @pl.when(at_end)
     def _():
+        small_end.wait_send()
+
         @pl.loop(0, total)
         def _(step):
             each(step, finish_end)
 
     @pl.when(jnp.logical_not(at_end))
     def _():
+        small_mid.wait_send()
+        small_back.wait_send()
+
         @pl.loop(0, total)
         def _(step):
             each(step, finish_mid)
 
 
-def reduce_all(planes, grads):
+def reduce_all(planes, grads, small):
     parts, base = [], 0
     for grad, axis, rows in grads:
-        height = grad.shape[0] // (2 if axis == 0 else 1)
-        width = grad.shape[1] // (1 if axis == 0 else 2)
-        parts.append(Part(axis, rows, width, height // rows, base))
+        height, width = grad.shape[-2:]
+        height, width = (height // 2, width) if axis == 0 else (height, width // 2)
+        parts.append(Part(axis, rows, width, height // rows, base, grad.ndim == 3))
         base += height // rows
     shapes = [(part.count, part.rows, part.cols) for part in parts]
+    col_shapes = [(2, *shape) for part, shape in zip(parts, shapes) if part.col]
+    pieces = sum(shape[1] * 2 for shape in col_shapes)
+    own_shapes = [
+        (2, 2, *shape) if part.col else (SLOTS, *shape[1:]) for part, shape in zip(parts, shapes)
+    ]
     anywhere = pl.BlockSpec(memory_space=pl.ANY)
+    dma = pltpu.SemaphoreType.DMA
     return pl.pallas_call(
         functools.partial(reduce_kernel, parts, planes),
-        out_shape=[jax.ShapeDtypeStruct((n * r, c), BF) for n, r, c in shapes],
-        in_specs=[anywhere] * len(parts),
-        out_specs=[anywhere] * len(parts),
-        scratch_shapes=[pltpu.VMEM(shape, BF) for _ in range(4) for shape in shapes]
-        + [pltpu.SemaphoreType.DMA((base,)) for _ in range(8)],
+        out_shape=[jax.ShapeDtypeStruct((n * r, c), BF) for n, r, c in shapes]
+        + [jax.ShapeDtypeStruct(small.shape, F32)],
+        in_specs=[anywhere] * (len(parts) + 1),
+        out_specs=[anywhere] * (len(parts) + 1),
+        scratch_shapes=[pltpu.VMEM(shape, BF) for _ in range(3) for shape in shapes]
+        + [pltpu.VMEM(shape, BF) for shape in own_shapes]
+        + [pltpu.VMEM((2, *shape), BF) for shape in col_shapes]
+        + [pltpu.VMEM(shape, BF) for shape in col_shapes]
+        + [dma((base,)) for _ in range(8)]
+        + [dma((2, pieces)), dma((2, pieces)), dma((2, pieces)), dma((pieces,)), dma((pieces,))]
+        + [dma((2,)), dma((5,)), dma((5,))]
+        + [pltpu.VMEM((5, *small.shape), F32), pltpu.VMEM((6, *small.shape), F32)],
         compiler_params=pltpu.CompilerParams(
-            collective_id=0, has_side_effects=True, vmem_limit_bytes=56 * 1024 * 1024
+            collective_id=0, has_side_effects=True, vmem_limit_bytes=60 * 1024 * 1024
         ),
         name="reduce_grads",
-    )(*[grad for grad, _, _ in grads])
+    )(*[grad for grad, _, _ in grads], small)
+
+
+TILE = 256
+STEPS = 8
+
+
+def spread_kernel(forward, *refs):
+    if forward:
+        mine_ref, *weights = refs[:7]
+        all_ref, gate_ref, up_ref, act_ref, out_ref = refs[7:12]
+        rest = refs[12:]
+    else:
+        mine_ref, *weights = refs[:7]
+        gate_ref, up_ref = refs[7:9]
+        all_ref, d_gate_up_ref, out_ref = refs[9:12]
+        rest = refs[12:]
+    block, w_gate, w_up, w_down, kept, to_mate, from_mate, far_part, to_far, from_mate_far, far_sum, from_far = rest[:12]
+    (
+        weight_sem, block_sem, out_sem, mate_send, mate_recv, x_send, x_recv, pass_send, pass_recv,
+        sum_send, sum_recv, part_send, part_recv, back_send, back_recv,
+    ) = rest[12:27]
+    stage = rest[27:]
+    tokens, depth = mine_ref.shape
+    quarter = tokens // 4
+    width = w_gate.shape[1]
+    group, side = lax.axis_index("group"), lax.axis_index("side")
+    mate, far = {"side": 1 - side}, {"group": 1 - group}
+
+    def remote(source, target, send, recv, where):
+        return pltpu.make_async_remote_copy(
+            source, target, send, recv, device_id=where, device_id_type=pl.DeviceIdType.MESH
+        )
+
+    barrier = pltpu.get_barrier_semaphore()
+    for where in (mate, far):
+        pl.semaphore_signal(barrier, 1, device_id=where, device_id_type=pl.DeviceIdType.MESH)
+
+    half = depth // 2
+    loads = []
+    for index, (source, target) in enumerate(
+        [
+            (weights[0], w_gate.at[pl.ds(0, half), :]),
+            (weights[1], w_gate.at[pl.ds(half, half), :]),
+            (weights[2], w_up.at[pl.ds(0, half), :]),
+            (weights[3], w_up.at[pl.ds(half, half), :]),
+            (weights[4], w_down.at[:, pl.ds(0, half)]),
+            (weights[5], w_down.at[:, pl.ds(half, half)]),
+        ]
+    ):
+        loads.append(pltpu.make_async_copy(source, target, weight_sem.at[index]))
+    order = loads if forward else loads[4:] + loads[:4]
+    mine_copies = [
+        pltpu.make_async_copy(
+            mine_ref.at[pl.ds(i * 2 * quarter, 2 * quarter), :], block.at[i], block_sem.at[i]
+        )
+        for i in range(2)
+    ]
+    for copy in mine_copies:
+        copy.start()
+    for copy in order:
+        copy.start()
+    pl.semaphore_wait(barrier, 2)
+
+    def piece(index):
+        return mine_ref.at[pl.ds(index * quarter, quarter), :]
+
+    def mate_copy(index):
+        return remote(
+            piece(index),
+            block.at[2 + index // 2, pl.ds(index % 2 * quarter, quarter), :],
+            mate_send.at[index],
+            mate_recv.at[index],
+            mate,
+        )
+
+    def x_copy(index):
+        return remote(
+            piece(index), block.at[4 + index, pl.ds(0, quarter), :], x_send.at[index], x_recv.at[index], far
+        )
+
+    def pass_copy(index):
+        return remote(
+            block.at[4 + index, pl.ds(0, quarter), :],
+            block.at[4 + index, pl.ds(quarter, quarter), :],
+            pass_send.at[index],
+            pass_recv.at[index],
+            mate,
+        )
+
+    def sum_copy(index):
+        return remote(to_mate.at[index], from_mate.at[index], sum_send.at[index], sum_recv.at[index], mate)
+
+    def part_copy(index):
+        return remote(to_far.at[index], from_mate_far.at[index], part_send.at[index], part_recv.at[index], mate)
+
+    def back_copy(index):
+        return remote(far_sum.at[index], from_far.at[index], back_send.at[index], back_recv.at[index], far)
+
+    x_copy(0).start()
+    for index in range(4):
+        mate_copy(index).start()
+    x_copy(1).start()
+    for copy in mine_copies:
+        copy.wait()
+
+    def emit(step, where, part):
+        @pl.when(step < 2)
+        def _():
+            kept[jnp.minimum(step, 1), :, where] = part
+
+        @pl.when((step >= 2) & (step < 4))
+        def _():
+            to_mate[jnp.clip(step - 2, 0, 1), :, where] = part.astype(BF)
+
+        @pl.when(step >= 4)
+        def _():
+            far_part[jnp.maximum(step - 4, 0), :, where] = part[:quarter]
+            to_far[jnp.maximum(step - 4, 0), :, where] = part[quarter:].astype(BF)
+
+    def all_copy(step):
+        return pltpu.make_async_copy(block.at[step], all_ref.at[step], out_sem.at[0, step])
+
+    if forward:
+        stage_gate, stage_up, stage_act = stage
+
+        def saves(step):
+            slot = step % 2
+            return [
+                pltpu.make_async_copy(stage_gate.at[slot], gate_ref.at[step], out_sem.at[1, step]),
+                pltpu.make_async_copy(stage_up.at[slot], up_ref.at[step], out_sem.at[2, step]),
+                pltpu.make_async_copy(stage_act.at[slot], act_ref.at[step], out_sem.at[3, step]),
+            ]
+
+        def fetches(step):
+            return []
+
+        def first_loads():
+            for copy in loads[:4]:
+                copy.wait()
+
+        def second_loads():
+            for copy in loads[4:]:
+                copy.wait()
+
+        def first_half(step):
+            slot = step % 2
+
+            @pl.loop(0, width // TILE)
+            def _(tile):
+                where = pl.ds(pl.multiple_of(tile * TILE, TILE), TILE)
+                gate = dot(block[step], w_gate[:, where])
+                up = dot(block[step], w_up[:, where])
+                stage_gate[slot, :, where] = gate.astype(BF)
+                stage_up[slot, :, where] = up.astype(BF)
+                stage_act[slot, :, where] = (gate * up / (1.0 + jnp.exp(-gate))).astype(BF)
+
+        def second_half(step):
+            slot = step % 2
+
+            @pl.loop(0, depth // TILE)
+            def _(tile):
+                where = pl.ds(pl.multiple_of(tile * TILE, TILE), TILE)
+                emit(step, where, dot(stage_act[slot], w_down[:, where]))
+
+    else:
+        stage_gate, stage_up, stage_d, fetch_sem = stage
+
+        def saves(step):
+            return [
+                pltpu.make_async_copy(stage_d.at[step % 2], d_gate_up_ref.at[step], out_sem.at[1, step])
+            ]
+
+        def fetches(step):
+            slot = step % 2
+            return [
+                pltpu.make_async_copy(gate_ref.at[step], stage_gate.at[slot], fetch_sem.at[0, step]),
+                pltpu.make_async_copy(up_ref.at[step], stage_up.at[slot], fetch_sem.at[1, step]),
+            ]
+
+        def first_loads():
+            for copy in loads[4:]:
+                copy.wait()
+
+        def second_loads():
+            for copy in loads[:4]:
+                copy.wait()
+
+        def first_half(step):
+            slot = step % 2
+
+            @pl.loop(0, width // TILE)
+            def _(tile):
+                first = pl.multiple_of(tile * TILE, TILE)
+                where = pl.ds(first, TILE)
+                d_act = dot(block[step], w_down[where, :], ((1,), (1,)))
+                gate = stage_gate[slot, :, where].astype(F32)
+                up = stage_up[slot, :, where].astype(F32)
+                sig = 1.0 / (1.0 + jnp.exp(-gate))
+                d_gate = d_act * up * sig * (1.0 + gate * (1.0 - sig))
+                stage_d[slot, :, where] = d_gate.astype(BF)
+                stage_d[slot, :, pl.ds(pl.multiple_of(width + first, TILE), TILE)] = (d_act * gate * sig).astype(BF)
+
+        def second_half(step):
+            slot = step % 2
+
+            @pl.loop(0, depth // TILE)
+            def _(tile):
+                where = pl.ds(pl.multiple_of(tile * TILE, TILE), TILE)
+                part = dot(stage_d[slot, :, :width], w_gate[where, :], ((1,), (1,)))
+                part += dot(stage_d[slot, :, width:], w_up[where, :], ((1,), (1,)))
+                emit(step, where, part)
+
+    def finish_far(index):
+        part_copy(index).wait_recv()
+        total = far_part[index] + from_mate_far[index].astype(F32)
+        far_sum[index] = total.astype(BF)
+        back_copy(index).start()
+
+    for copy in fetches(0):
+        copy.start()
+
+    @pl.loop(0, STEPS)
+    def _(step):
+        @pl.when((step == 2) | (step == 3))
+        def _():
+            index = jnp.clip(2 * (step - 2), 0, 2)
+            mate_copy(index).wait_recv()
+            mate_copy(index + 1).wait_recv()
+
+        @pl.when(step >= 4)
+        def _():
+            index = jnp.maximum(step - 4, 0)
+            x_copy(index).wait_recv()
+            pass_copy(index).start()
+            pass_copy(index).wait_recv()
+
+        all_copy(step).start()
+        for copy in fetches(step):
+            copy.wait()
+
+        if not forward:
+            @pl.when(step < STEPS - 1)
+            def _():
+                for copy in fetches(jnp.minimum(step + 1, STEPS - 1)):
+                    copy.start()
+
+        @pl.when(step == 0)
+        def _():
+            first_loads()
+
+        @pl.when(step >= 2)
+        def _():
+            for copy in saves(jnp.maximum(step - 2, 0)):
+                copy.wait()
+
+        first_half(step)
+
+        @pl.when(step == 0)
+        def _():
+            second_loads()
+
+        second_half(step)
+        for copy in saves(step):
+            copy.start()
+
+        @pl.when((step == 1) | (step == 3))
+        def _():
+            x_copy(2 + step // 2).start()
+
+        @pl.when((step >= 2) & (step < 4))
+        def _():
+            sum_copy(jnp.clip(step - 2, 0, 1)).start()
+
+        @pl.when(step >= 4)
+        def _():
+            part_copy(jnp.maximum(step - 4, 0)).start()
+
+        @pl.when(step >= 5)
+        def _():
+            finish_far(jnp.maximum(step - 5, 0))
+
+    finish_far(3)
+    for index in range(2):
+        sum_copy(index).wait_recv()
+        kept[index] = kept[index] + from_mate[index].astype(F32)
+    results = []
+    for index in range(4):
+        back_copy(index).wait_recv()
+        rows = pl.ds(index % 2 * quarter, quarter)
+        kept[index // 2, rows, :] = kept[index // 2, rows, :] + from_far[index].astype(F32)
+        if index % 2:
+            copy = pltpu.make_async_copy(kept.at[index // 2], out_ref.at[index // 2], block_sem.at[index // 2])
+            copy.start()
+            results.append(copy)
+    for copy in results:
+        copy.wait()
+
+    @pl.loop(0, STEPS)
+    def _(step):
+        all_copy(step).wait()
+
+        @pl.when(step >= STEPS - 2)
+        def _():
+            for copy in saves(step):
+                copy.wait()
+
+        @pl.when(step < 4)
+        def _():
+            index = jnp.minimum(step, 3)
+            mate_copy(index).wait_send()
+            x_copy(index).wait_send()
+            pass_copy(index).wait_send()
+            part_copy(index).wait_send()
+            back_copy(index).wait_send()
+
+        @pl.when(step < 2)
+        def _():
+            sum_copy(jnp.minimum(step, 1)).wait_send()
+
+
+def spread(forward, mine, weights, *kept):
+    tokens, depth = mine.shape
+    quarter, double = tokens // 4, tokens // 2
+    width = weights[0].shape[1]
+    anywhere = pl.BlockSpec(memory_space=pl.ANY)
+    wide = jax.ShapeDtypeStruct((STEPS, double, width), BF)
+    whole = jax.ShapeDtypeStruct((STEPS, double, depth), BF)
+    out = jax.ShapeDtypeStruct((2, double, depth), F32)
+    if forward:
+        outs = [whole, wide, wide, wide, out]
+        stage = [pltpu.VMEM((2, double, width), BF) for _ in range(3)]
+    else:
+        outs = [whole, jax.ShapeDtypeStruct((STEPS, double, 2 * width), BF), out]
+        stage = [
+            pltpu.VMEM((2, double, width), BF),
+            pltpu.VMEM((2, double, width), BF),
+            pltpu.VMEM((2, double, 2 * width), BF),
+            pltpu.SemaphoreType.DMA((2, STEPS)),
+        ]
+    result = pl.pallas_call(
+        functools.partial(spread_kernel, forward),
+        out_shape=outs,
+        in_specs=[anywhere] * (7 + len(kept)),
+        out_specs=[anywhere] * len(outs),
+        scratch_shapes=[
+            pltpu.VMEM((STEPS, double, depth), BF),
+            pltpu.VMEM((depth, width), BF),
+            pltpu.VMEM((depth, width), BF),
+            pltpu.VMEM((width, depth), BF),
+            pltpu.VMEM((2, double, depth), F32),
+            pltpu.VMEM((2, double, depth), BF),
+            pltpu.VMEM((2, double, depth), BF),
+            pltpu.VMEM((4, quarter, depth), F32),
+            pltpu.VMEM((4, quarter, depth), BF),
+            pltpu.VMEM((4, quarter, depth), BF),
+            pltpu.VMEM((4, quarter, depth), BF),
+            pltpu.VMEM((4, quarter, depth), BF),
+            pltpu.SemaphoreType.DMA((6,)),
+            pltpu.SemaphoreType.DMA((2,)),
+            pltpu.SemaphoreType.DMA((4, STEPS)),
+        ]
+        + [pltpu.SemaphoreType.DMA((4,)) for _ in range(6)]
+        + [pltpu.SemaphoreType.DMA((2,)) for _ in range(2)]
+        + [pltpu.SemaphoreType.DMA((4,)) for _ in range(4)]
+        + stage,
+        compiler_params=pltpu.CompilerParams(
+            collective_id=1 if forward else 2,
+            has_side_effects=True,
+            vmem_limit_bytes=60 * 1024 * 1024,
+        ),
+        name="feed_forward" if forward else "feed_forward_back",
+    )(mine, *weights, *kept)
+    return result
 
 
 def body(
@@ -484,9 +1016,12 @@
     w_project = lax.all_gather(w_project, ("group", "side"), axis=0)
     w_out_all = gather_rows(w_out, 1)
     w_out_all = lax.all_gather(w_out_all, ("group", "side"), axis=0, tiled=True)
-    w_gate_all = gather_rows(w_gate, 0)
-    w_up_all = gather_rows(w_up, 0)
-    w_down_all = gather_rows(w_down, 1)
+    def halves(block, axis):
+        if rows == 2:
+            return [block, from_row(block, 1)]
+        return jnp.split(gather_rows(block, axis), 2, axis=axis)
+
+    ffn_weights = halves(w_gate, 0) + halves(w_up, 0) + halves(w_down, 1)
     target = to_members(teacher)
 
     half = HD // 2
@@ -536,30 +1071,19 @@
 
     inverse_two = rms(hidden)
     normed_two = (hidden * inverse_two * gain_two).astype(BF)
-    normed_all = lax.all_gather(normed_two, ("group", "side"), axis=0, tiled=True)
-    gate = dot(normed_all, w_gate_all)
-    up = dot(normed_all, w_up_all)
-    sig = jax.nn.sigmoid(gate)
-    activated = (gate * sig * up).astype(BF)
-    ffn_out = dot(activated, w_down_all).astype(BF)
-    ffn_out = lax.psum_scatter(ffn_out, ("group", "side"), scatter_dimension=0, tiled=True)
-    result = hidden + ffn_out.astype(F32)
+    normed_all, gate, up, activated, ffn_out = spread(True, normed_two, ffn_weights)
+    ffn_out = ffn_out.reshape(mine, D)
+    result = hidden + ffn_out
     block_out = from_members(result.astype(BF))
 
     total_tokens = shard * cols * lax.axis_size("dp")
     loss_scale = total_tokens / token_count[0].astype(F32)
     d_result = loss_scale * (result - target.astype(F32))
-    d_low = lax.all_gather(d_result.astype(BF), ("group", "side"), axis=0, tiled=True)
-    d_act = dot(d_low, w_down_all, ((1,), (1,)))
-    grad_down = dot(activated, d_low, ((0,), (0,))).astype(BF)
-    d_up = (d_act * gate * sig).astype(BF)
-    d_gate = (d_act * up * sig * (1.0 + gate * (1.0 - sig))).astype(BF)
-    d_normed = dot(d_gate, w_gate_all, ((1,), (1,))) + dot(d_up, w_up_all, ((1,), (1,)))
-    d_normed = lax.psum_scatter(
-        d_normed.astype(BF), ("group", "side"), scatter_dimension=0, tiled=True
-    ).astype(F32)
-    d_gate_up = jnp.concatenate([d_gate, d_up], axis=1)
-    grad_gate_up = dot(normed_all, d_gate_up, ((0,), (0,))).astype(BF)
+    d_low, d_gate_up, d_normed = spread(False, d_result.astype(BF), ffn_weights, gate, up)
+    d_normed = d_normed.reshape(mine, D)
+    d_low, normed_all = d_low.reshape(-1, D), normed_all.reshape(-1, D)
+    grad_down = dot(activated.reshape(-1, ff), d_low, ((0,), (0,))).astype(BF)
+    grad_gate_up = dot(normed_all, d_gate_up.reshape(-1, 2 * ff), ((0,), (0,))).astype(BF)
 
     norm_two_part = jnp.sum(d_normed * hidden * inverse_two, axis=0)
     d_hidden = d_result + norm_back(hidden, inverse_two, gain_two, d_normed)
@@ -593,23 +1117,27 @@
         d_projected, normed_one, (((2,), (0,)), ((), ())), preferred_element_type=F32
     )
     grad_project = grad_project.astype(BF).transpose(0, 2, 1)
-    grad_project = lax.psum_scatter(
-        grad_project.reshape(cols * D, -1), ("group", "side"), scatter_dimension=0, tiled=True
-    )
-    grad_out = lax.psum_scatter(grad_out, ("group", "side"), scatter_dimension=0, tiled=True)
-    if rows == 2 and lax.axis_size("dp") == 4:
-        grad_down, grad_gate_up, grad_out, grad_project = reduce_all(
-            4, [(grad_down, 1, 128), (grad_gate_up, 0, 64), (grad_out, 1, 64), (grad_project, 0, 256)]
-        )
-    else:
-        grad_down = sum_planes(scatter_rows(grad_down, 1), 2)
-        grad_gate_up = sum_planes(scatter_rows(grad_gate_up, 0), 4)
-        grad_out = sum_planes(scatter_rows(grad_out, 1), 1)
-        grad_project = sum_planes(scatter_rows(grad_project, 0), 2)
+    grad_out = grad_out.reshape(cols, q_width, D)
     norm_one_part = jnp.roll(norm_one_part.reshape(rows, width), row_index, 0).reshape(D)
     norm_two_part = jnp.roll(norm_two_part.reshape(rows, width), row_index, 0).reshape(D)
     small = jnp.concatenate([norm_one_part, norm_two_part, query_gain_part, key_gain_part])
-    small = lax.psum(small, ("dp", "row", "group", "side"))
+    if rows == 2 and cols == 4 and lax.axis_size("dp") == 4:
+        padded = jnp.pad(small, (0, SMALL * 128 - small.shape[0])).reshape(SMALL, 128)
+        grad_down, grad_gate_up, grad_out, grad_project, small = reduce_all(
+            4,
+            [(grad_down, 1, 128), (grad_gate_up, 0, 64), (grad_out, 1, 160), (grad_project, 0, 512)],
+            padded,
+        )
+        small = small.reshape(-1)[: 2 * D + 2 * HD]
+    else:
+        small = lax.psum(small, ("dp", "row", "group", "side"))
+        col_axes = ("group", "side")
+        grad_project = lax.psum_scatter(grad_project, col_axes, scatter_dimension=0, tiled=True)
+        grad_out = lax.psum_scatter(grad_out, col_axes, scatter_dimension=0, tiled=True)
+        grad_down = sum_planes(scatter_rows(grad_down, 1), 2)
+        grad_gate_up = sum_planes(scatter_rows(grad_gate_up, 0), 4)
+        grad_out = sum_planes(scatter_rows(grad_out[0], 1), 1)
+        grad_project = sum_planes(scatter_rows(grad_project[0], 0), 2)
     grad_norm1 = lax.dynamic_slice_in_dim(small, row_index * width, width, 0)
     grad_norm2 = lax.dynamic_slice_in_dim(small, D + row_index * width, width, 0)
     grad_project = grad_project.astype(F32)

time: 1300 us -> 1050 us (0.81)
  waiting for transfers between devices: 450 us -> 170 us
  Pallas kernels: 307 us -> 545 us
  matrix products: 224 us -> 89.7 us
  blocking collectives: 61.9 us -> 0 us
  local copies, waits for them, and re-layouts: 138 us -> 121 us
    pallas_call x0 -> x2, Pallas kernels: none -> 203 us  [spread(): pl.pallas_call(functools.partial(spread_kernel, forward), out_shape=outs,...]
    dot_general x13 -> x7, matrix products: 217 us -> 79.9 us  [dot(): lax.dot_general(left, right, (dims, ((), ())), preferred_element_type=F32)]
    reduce_scatter x4 -> x0, waiting for transfers between devices: 101 us -> none  [the longest x1 71.8 us: body(): lax.psum_scatter(d_normed.astype(BF), ('group', 'side'), scatter_dimensio...]
    ppermute x7, waiting for transfers between devices: 228 us -> 148 us  [from_row(): return lax.ppermute(block, 'row', pairs)]
    psum x1 -> x0, blocking collectives: 61.9 us -> none  [body(): small = lax.psum(small, ('dp', 'row', 'group', 'side'))]
    all_gather x2 -> x0, waiting for transfers between devices: 58.4 us -> none  [the longest x1 58.4 us: body(): lax.all_gather(d_result.astype(BF), ('group', 'side'), axis=0, tiled=True)]
    pallas_call x1, Pallas kernels: 241 us -> 275 us  [reduce_all(): pl.pallas_call(functools.partial(reduce_kernel, parts, planes), out_shape...]
    reduce_scatter x1, waiting for transfers between devices: 20.8 us -> 0.02 us  [body(): lax.psum_scatter(d_pair, ('row', 'side'), scatter_dimension=0, tiled=True)]
  transfers between devices with their start and end apart: 21 -> 15, of which waited for: 13 -> 6; matrix products, arithmetic and copies ran while one was open for 15% -> 20% of each run, Pallas kernels for 2% -> 29%
where the time goes in v3:
time: 1050 us; the launch traced here: 1040 us
  Pallas kernels  545 us (52%)
  waiting for transfers between devices  170 us (16%)
  local copies, waits for them, and re-layouts  121 us (12%)
  matrix products  89.7 us (9%)
  other arithmetic  72.7 us (7%)
  starting transfers between devices  26.5 us (3%)
  between operations  15.7 us (1%)
    pallas_call x1, Pallas kernels, reduce_all(): pl.pallas_call(functools.partial(reduce_kernel, parts, planes), out_shape...  275 us
    pallas_call x2, Pallas kernels, spread(): pl.pallas_call(functools.partial(spread_kernel, forward), out_shape=outs,...  203 us
    ppermute x7, waiting for transfers between devices, from_row(): return lax.ppermute(block, 'row', pairs)  148 us
    dot_general x7, matrix products, dot(): lax.dot_general(left, right, (dims, ((), ())), preferred_element_type=F32)  79.9 us
    pallas_call x1, Pallas kernels, attend_back(): pl.pallas_call(functools.partial(attend_back_kernel, chunks, tokens // ch...  37.1 us
    unnamed x89, local copies, waits for them, and re-layouts  30.5 us
    pallas_call x1, Pallas kernels, attend(): pl.pallas_call(functools.partial(attend_kernel, chunks, tokens // chunks)...  29.5 us
    all_to_all x2, waiting for transfers between devices, to_members(): moved = lax.all_to_all(parts, ('row', 'side'), 0, 0, tiled=True)  22.4 us
  transfers between devices with their start and end apart: 15, of which 6 were waited for; matrix products, arithmetic and copies ran while one was open for 20% of the time, Pallas kernels for 29%

profile of v3, /device:TPU:0, one launch (start us, length us, event | category | flops | bytes accessed | tf_op | source)
XLA Modules:
  0.0 1041.0 jit_solution(7420822348909529841)
XLA Ops:
  13.3 21.8 %collective-permute-done = bf16[1024,480]{0,1:T(8,128)(2,1)S(1)} collective-permute-done((bf16[1024,480]{0,1:T(8,128)(2,1)S(1)}, bf16[1024,480]{0,1:T(8,128)(2,1)S(1)}, u32[]{:S(2)}, u32[]{:S(2)}) %collective-permute-start) | collective-permute-done | bytes 983072 | tf_op jit(solution)/shard_map/ppermute | solution.py:951
  45.2 22.4 %all-to-all-done = bf16[4,2,128,1024]{3,2,1,0:T(8,128)(2,1)S(1)} async-done(((bf16[4,2,128,1024]{3,2,1,0:T(8,128)(2,1)}), bf16[4,2,128,1024]{3,2,1,0:T(8,128)(2,1)S(1)}, u32[]{:S(2)}, u32[]{:S(2)}) %all-to-all-start) | async-done | bytes 2097184 | tf_op jit(solution)/shard_map/all_to_all | solution.py:988
  75.2 22.7 %collective-permute-done.1 = f32[1024]{0:T(1024)S(1)} collective-permute-done((f32[1024]{0:T(1024)S(1)}, f32[1024]{0:T(1024)S(1)}, u32[]{:S(2)}, u32[]{:S(2)}) %collective-permute-start.1) | collective-permute-done | bytes 4128 | tf_op jit(solution)/shard_map/ppermute | solution.py:951
  97.9 5.4 convert_bitcast_fusion
  111.5 11.0 %fusion.61 = (bf16[4,480,512]{2,1,0:T(8,128)(2,1)S(1)}, f32[4,480,512]{2,1,0:T(8,128)}) fusion(f32[512,2048]{1,0:T(8,128)} %bitcast.197, f32[2048]{0:T(1024)S(1)} %pad_maximum_fusion.11, f32[512]{0:T(512)S(1)} %bitcast.243, bf16[60,4,8,2048]{3,2,1,0:T(8,128)(2,1)} %bitcast.250), kind=kOutput, calls=%fused_computation.167 | convolution fusion | flops 4030660608 | bytes 17967104 | tf_op jit(solution)/shard_map/dot_general | solution.py:29
  124.2 23.0 %collective-permute-done.2 = bf16[320,1024]{1,0:T(8,128)(2,1)S(1)} collective-permute-done((bf16[320,1024]{1,0:T(8,128)(2,1)S(1)}, bf16[320,1024]{1,0:T(8,128)(2,1)S(1)}, u32[]{:S(2)}, u32[]{:S(2)}) %collective-permute-start.2) | collective-permute-done | bytes 655392 | tf_op jit(solution)/shard_map/ppermute | solution.py:951
  153.4 5.4 copy.144
  200.5 29.5 %attend.1 = (f32[5,4,64,512]{3,2,1,0:T(8,128)S(1)}, f32[5,4,512]{2,1,0:T(4,128)S(1)}) custom-call(s32[4]{0:T(128)S(1)} %fusion.50.first_ref, bf16[5,4,64,512]{3,2,1,0:T(8,128)(2,1)S(1)} %copy-done.2, bf16[5,2048,64]{2,1,0:T(8,128)(2,1)S(1)} %copy.140.key_ref, bf16[5,80,2048]{2,1,0:T(8,128)(2,1)S(1)} %concatenate.87.clone.value_ref), custom_call_target="tpu_custom_call" | custom-call | tf_op jit(solution)/shard_map/attend/pallas_call | solution.py:149
  232.7 7.2 multiply_reduce_fusion
  242.6 25.6 %collective-permute-done.5.refs_4_ = bf16[1024,1280]{1,0:T(8,128)(2,1)} collective-permute-done((bf16[1024,1280]{1,0:T(8,128)(2,1)}, bf16[1024,1280]{1,0:T(8,128)(2,1)}, u32[]{:S(2)}, u32[]{:S(2)}) %collective-permute-start.5) | collective-permute-done | bytes 2621472 | tf_op jit(solution)/shard_map/ppermute | solution.py:951
  268.2 54.8 %collective-permute-done.6.refs_6_ = bf16[1280,1024]{1,0:T(8,128)(2,1)} collective-permute-done((bf16[1280,1024]{1,0:T(8,128)(2,1)}, bf16[1280,1024]{1,0:T(8,128)(2,1)}, u32[]{:S(2)}, u32[]{:S(2)}) %collective-permute-start.6) | collective-permute-done | bytes 2621472 | tf_op jit(solution)/shard_map/ppermute | solution.py:951
  323.0 99.9 %feed_forward.1 = (bf16[8,256,2048]{2,1,0:T(8,128)(2,1)}, bf16[8,256,1280]{2,1,0:T(8,128)(2,1)}, bf16[8,256,1280]{2,1,0:T(8,128)(2,1)}, bf16[8,256,1280]{2,1,0:T(8,128)(2,1)}, f32[2,256,2048]{2,1,0:T(8,128)}) custom-call(bf16[512,2048]{1,0:T(8,128)(2,1)} %multiply_convert_fusion.refs_0_, bf16[1024,1280]{1,0:T(8,128)(2,1)} %refs_1_.3, ...), custom_call_target="tpu_custom_call" | custom-call | tf_op jit(solution)/shard_map/feed_forward/pallas_call | solution.py:882
  422.9 7.5 fusion.26.refs_0_
  430.4 102.9 %feed_forward_back.1 = (bf16[8,256,2048]{2,1,0:T(8,128)(2,1)}, bf16[8,256,2560]{2,1,0:T(8,128)(2,1)}, f32[2,256,2048]{2,1,0:T(8,128)}) custom-call(bf16[512,2048]{1,0:T(8,128)(2,1)} %fusion.26.refs_0_, bf16[1024,1280]{1,0:T(8,128)(2,1)} %refs_1_.3, bf16[1024,1280]{1,0:T(8,128)(2,1)} %collective-permute-done.4.refs_2_, bf16[1024,1280]{1,0:T(8,128)(2,1)} %refs_3_.3, ...), custom_call_target="tpu_custom_call" | custom-call | tf_op jit(solution)/shard_map/feed_forward_back/pallas_call | solution.py:882
  539.3 5.6 fusion.14
  550.2 37.1 %attend_back.1 = (f32[5,4,64,512]{3,2,1,0:T(8,128)S(1)}, f32[5,2048,64]{2,1,0:T(8,128)S(1)}, f32[5,2048,64]{2,1,0:T(8,128)S(1)}) custom-call(s32[4]{0:T(128)S(1)} %fusion.50.first_ref, bf16[5,4,64,512]{3,2,1,0:T(8,128)(2,1)S(1)} %copy-done.3, bf16[5,4,64,512]{3,2,1,0:T(8,128)(2,1)S(1)} %bitcast.190, f32[5,4,512]{2,1,0:T(4,128)S(1)} %get-tuple-element.38.log_ref, ...), custom_call_target="tpu_custom_call" | custom-call | tf_op jit(solution)/shard_map/attend_back/pallas_call | solution.py:173
  621.0 16.8 %bitcast_convert_fusion.1.refs_0_ = bf16[1280,2048]{1,0:T(8,128)(2,1)} fusion(bf16[8,256,1280]{2,1,0:T(8,128)(2,1)} %get-tuple-element.42, bf16[8,256,2048]{2,1,0:T(8,128)(2,1)} %get-tuple-element.43), kind=kOutput, calls=%fused_computation.1 | convolution fusion | flops 10740039680 | bytes 18874368 | tf_op jit(solution)/shard_map/dot_general | solution.py:29
  642.4 28.4 %bitcast_convert_fusion.refs_1_ = bf16[2048,2560]{1,0:T(8,128)(2,1)} fusion(bf16[8,256,2048]{2,1,0:T(8,128)(2,1)} %get-tuple-element.44, bf16[8,256,2560]{2,1,0:T(8,128)(2,1)} %get-tuple-element.45), kind=kOutput, calls=%fused_computation | convolution fusion | flops 21480079360 | bytes 29360128 | tf_op jit(solution)/shard_map/dot_general | solution.py:29
  673.9 8.9 fusion.12
  686.0 6.6 reshape.359
  708.2 9.8 convolution_convert_fusion.1
  718.0 11.4 %copy.154 = bf16[4,480,2048]{1,2,0:T(8,128)(2,1)} copy(bf16[4,480,2048]{2,1,0:T(8,128)(2,1)} %convolution_convert_fusion.1) | data formatting | bytes 15728640 | tf_op jit(solution)/shard_map/convert_element_type | solution.py:1119
  730.1 275.1 %reduce_grads.1 = (bf16[1280,1024]{1,0:T(8,128)(2,1)}, bf16[1024,2560]{1,0:T(8,128)(2,1)}, bf16[320,1024]{1,0:T(8,128)(2,1)}, bf16[1024,480]{1,0:T(8,128)(2,1)}, f32[40,128]{1,0:T(8,128)}) custom-call(bf16[1280,2048]{1,0:T(8,128)(2,1)} %bitcast_convert_fusion.1.refs_0_, bf16[2048,2560]{1,0:T(8,128)(2,1)} %bitcast_convert_fusion.refs_1_, ...), custom_call_target="tpu_custom_call" | custom-call | tf_op jit(solution)/shard_map/reduce_grads/pallas_call | solution.py:524
  1016.2 7.4 slice_convert_fusion
  (213 shorter events, 179.0 us)
Async XLA Ops:
  7.2 104.3 %all-gather.8.cloned.1.call-start = ((), (), s32[]{:S(2)}) async-start(), calls=%async_computation.7 | async-start | bytes 9830400 | tf_op jit(solution)/shard_map/all_gather | solution.py:1016
  10.2 26.3 %copy-start.23 = (bf16[1024,1024]{1,0:T(8,128)(2,1)S(1)}, bf16[1024,1024]{1,0:T(8,128)(2,1)}, u32[]{:S(2)}) copy-start(bf16[1024,1024]{1,0:T(8,128)(2,1)} %param.20) | copy-start | bytes 6291460
  10.2 24.8 %collective-permute-start = (bf16[1024,480]{0,1:T(8,128)(2,1)S(1)}, bf16[1024,480]{0,1:T(8,128)(2,1)S(1)}, u32[]{:S(2)}, u32[]{:S(2)}) collective-permute-start(bf16[1024,480]{0,1:T(8,128)(2,1)S(1)} %constant_dynamic-update-slice_fusion), channel_id=1, source_target_pairs={{4,0},{0,4},{5,1},{1,5},{6,2},{2,6},{7,3},{3,7},{12,8},{8,12},{13,... | collective-permute-start | bytes 2949128 | tf_op jit(solution)/shard_map/ppermute | solution.py:951
  38.3 29.3 %all-to-all-start = ((bf16[4,2,128,1024]{3,2,1,0:T(8,128)(2,1)}), bf16[4,2,128,1024]{3,2,1,0:T(8,128)(2,1)S(1)}, u32[]{:S(2)}, u32[]{:S(2)}) async-start(bf16[4,2,128,1024]{3,2,1,0:T(8,128)(2,1)} %pad_maximum_fusion.2), calls=%async_computation | async-start | bytes 4194304 | tf_op jit(solution)/shard_map/all_to_all | solution.py:988
  45.2 26.9 %copy-start.34 = (f32[1024]{0:T(1024)S(1)}, f32[1024]{0:T(1024)}, u32[]{:S(2)}) copy-start(f32[1024]{0:T(1024)} %param.21) | copy-start | bytes 12292
  67.5 30.3 %all-to-all-start.2 = ((bf16[4,2,128,1024]{3,2,1,0:T(8,128)(2,1)}), bf16[4,2,128,1024]{3,2,1,0:T(8,128)(2,1)}, u32[]{:S(2)}, u32[]{:S(2)}) async-start(bf16[4,2,128,1024]{3,2,1,0:T(8,128)(2,1)} %pad_maximum_fusion.4), calls=%async_computation.2 | async-start | bytes 4194304 | tf_op jit(solution)/shard_map/all_to_all | solution.py:988
  72.1 94.5 %all-gather.10.cloned.1.call-start = ((), (), s32[]{:S(2)}) async-start(), calls=%async_computation.8 | async-start | bytes 3276800 | tf_op jit(solution)/shard_map/all_gather | solution.py:1046
  72.1 25.7 %collective-permute-start.1 = (f32[1024]{0:T(1024)S(1)}, f32[1024]{0:T(1024)S(1)}, u32[]{:S(2)}, u32[]{:S(2)}) collective-permute-start(f32[1024]{0:T(1024)S(1)} %copy-done.34), channel_id=1, source_target_pairs={{4,0},{0,4},{5,1},{1,5},{6,2},{2,6},{7,3},{3,7},{12,8},{8,12},{13,... | collective-permute-start | bytes 12296 | tf_op jit(solution)/shard_map/ppermute | solution.py:951
  111.5 11.1 %copy-start.32 = (f32[64]{0:T(128)S(1)}, f32[64]{0:T(128)}, u32[]{:S(2)}) copy-start(f32[64]{0:T(128)} %param.26) | copy-start | bytes 772
  123.8 24.7 %copy-start.35 = (f32[1024]{0:T(1024)S(1)}, f32[1024]{0:T(1024)}, u32[]{:S(2)}) copy-start(f32[1024]{0:T(1024)} %param.28) | copy-start | bytes 12292
  123.8 28.8 %copy-start.36 = (s32[4]{0:T(128)S(1)}, s32[4]{0:T(128)}, u32[]{:S(2)}) copy-start(s32[4]{0:T(128)} %constant.166.clone) | copy-start | bytes 52
  123.8 108.9 %all-gather.6.cloned.1.call-start = ((), (), s32[]{:S(2)}) async-start(), calls=%async_computation.5 | async-start | bytes 6553600 | tf_op jit(solution)/shard_map/all_gather | solution.py:1018
  123.9 23.4 %collective-permute-start.2 = (bf16[320,1024]{1,0:T(8,128)(2,1)S(1)}, bf16[320,1024]{1,0:T(8,128)(2,1)S(1)}, u32[]{:S(2)}, u32[]{:S(2)}) collective-permute-start(bf16[320,1024]{1,0:T(8,128)(2,1)S(1)} %copy-done.27), channel_id=1, source_target_pairs={{4,0},{0,4},{5,1},{1,5},{6,2},{2,6},{7,3},{3,7},{12,8},{8,12},{13,... | collective-permute-start | bytes 1966088 | tf_op jit(solution)/shard_map/ppermute | solution.py:951
  148.5 522.4 %reduce-scatter.2.cloned.1.call-start = ((), (), s32[]{:S(2)}) async-start(), calls=%async_computation.6 | async-start | bytes 3276800 | tf_op jit(solution)/shard_map/reduce_scatter | solution.py:1099
  148.5 4.9 collective-permute-start.3
  149.1 93.5 %collective-permute-start.4 = (bf16[1024,1280]{1,0:T(8,128)(2,1)}, bf16[1024,1280]{1,0:T(8,128)(2,1)}, u32[]{:S(2)}, u32[]{:S(2)}) collective-permute-start(bf16[1024,1280]{1,0:T(8,128)(2,1)} %refs_1_.3), channel_id=1, source_target_pairs={{4,0},{0,4},{5,1},{1,5},{6,2},{2,6},{7,3},{3,7},{12,8},{8,12},{13,... | collective-permute-start | bytes 7864328 | tf_op jit(solution)/shard_map/ppermute | solution.py:951
  150.6 117.6 %collective-permute-start.5 = (bf16[1024,1280]{1,0:T(8,128)(2,1)}, bf16[1024,1280]{1,0:T(8,128)(2,1)}, u32[]{:S(2)}, u32[]{:S(2)}) collective-permute-start(bf16[1024,1280]{1,0:T(8,128)(2,1)} %refs_3_.3), channel_id=1, source_target_pairs={{4,0},{0,4},{5,1},{1,5},{6,2},{2,6},{7,3},{3,7},{12,8},{8,12},{13,... | collective-permute-start | bytes 7864328 | tf_op jit(solution)/shard_map/ppermute | solution.py:951
  151.1 171.9 %collective-permute-start.6 = (bf16[1280,1024]{1,0:T(8,128)(2,1)}, bf16[1280,1024]{1,0:T(8,128)(2,1)}, u32[]{:S(2)}, u32[]{:S(2)}) collective-permute-start(bf16[1280,1024]{1,0:T(8,128)(2,1)} %refs_5_.3), channel_id=1, source_target_pairs={{4,0},{0,4},{5,1},{1,5},{6,2},{2,6},{7,3},{3,7},{12,8},{8,12},{13,... | collective-permute-start | bytes 7864328 | tf_op jit(solution)/shard_map/ppermute | solution.py:951
  533.4 11.5 %slice-start = ((s8[5242880]{0:T(1024)(128)(4,1)}), s8[4194304]{0:T(1024)(128)(4,1)S(1)}, s32[]{:S(2)}) async-start(s8[5242880]{0:T(1024)(128)(4,1)} %bitcast.218), calls=%async_computation.9 | async-start | bytes 8388608
  617.3 81.8 %all-to-all-start.1 = ((bf16[4,2,128,1024]{3,2,1,0:T(8,128)(2,1)}), bf16[4,2,128,1024]{3,2,1,0:T(8,128)(2,1)S(1)}, u32[]{:S(2)}, u32[]{:S(2)}) async-start(bf16[4,2,128,1024]{3,2,1,0:T(8,128)(2,1)} %bitcast.212), calls=%async_computation.1 | async-start | bytes 4194304 | tf_op jit(solution)/shard_map/all_to_all | solution.py:996
  621.0 16.8 %copy-start.16 = (f32[512,2048]{1,0:T(8,128)S(1)}, f32[512,2048]{1,0:T(8,128)}, u32[]{:S(2)}) copy-start(f32[512,2048]{1,0:T(8,128)} %copy-done.15) | copy-start | bytes 12582916
  621.0 16.8 %copy-start.20 = (bf16[5,4,64,512]{3,2,1,0:T(8,128)(2,1)S(1)}, bf16[5,4,64,512]{3,2,1,0:T(8,128)(2,1)}, u32[]{:S(2)}) copy-start(bf16[5,4,64,512]{3,2,1,0:T(8,128)(2,1)} %convert_element_type.147) | copy-start | bytes 3932164
  672.2 10.6 %copy-start.29 = (bf16[1,5,64,512]{3,2,1,0:T(8,128)(2,1)}, bf16[1,5,64,512]{3,2,1,0:T(8,128)(2,1)S(1)}, u32[]{:S(2)}) copy-start(bf16[1,5,64,512]{3,2,1,0:T(8,128)(2,1)S(1)} %get-tuple-element.168) | copy-start | bytes 983044
  699.1 324.5 %all-to-all-start.3 = ((f32[4,2,128,1024]{3,2,1,0:T(8,128)}), f32[4,2,128,1024]{3,2,1,0:T(8,128)}, u32[]{:S(2)}, u32[]{:S(2)}) async-start(f32[4,2,128,1024]{3,2,1,0:T(8,128)} %bitcast.207), calls=%async_computation.4 | async-start | bytes 8388608 | tf_op jit(solution)/shard_map/all_to_all | solution.py:996
  (30 other events, 100.3 us)
Sparse Core Ops, SparseCore 0:
  36.6 56.7 all-gather.7
  123.9 36.1 all-gather.9
  161.7 40.7 all-gather.5
  611.0 49.3 reduce-scatter.1

commit v4 on v3

--- a/solution.py
+++ b/solution.py
@@ -99,14 +99,17 @@
     d_out_ref,
     log_ref,
     delta_ref,
-    key_ref,
-    value_ref,
     key_t_ref,
+    value_t_ref,
     d_query_ref,
     d_key_ref,
     d_value_ref,
+    key_ref,
+    value_ref,
 ):
     rows = REP * span
+    key_ref[...] = key_t_ref[0].T
+    value_ref[...] = value_t_ref[0].T
     d_key_ref[...] = jnp.zeros_like(d_key_ref)
     d_value_ref[...] = jnp.zeros_like(d_value_ref)
     for index in range(chunks):
@@ -123,10 +126,10 @@
         def tile(where, accum, masked):
             first_key = pl.multiple_of(where * KEYS, KEYS)
             here = pl.ds(first_key, KEYS)
-            probs = jnp.exp(dot(key_ref[0, here, :], query) - logs)
+            probs = jnp.exp(dot(key_ref[here, :], query) - logs)
             if masked:
                 probs = jnp.where(allowed(first_query, first_key, span, rows), probs, 0.0)
-            d_probs = dot(value_ref[0, here, :], d_out)
+            d_probs = dot(value_ref[here, :], d_out)
             d_scores = (probs * (d_probs - delta)).astype(BF)
             d_value_ref[0, here, :] += dot(probs.astype(BF), d_out_t)
             d_key_ref[0, here, :] += dot(d_scores, query_t)
@@ -167,7 +170,7 @@
     )(first, query, key, value_t)
 
 
-def attend_back(first, query, d_out, logs, delta, key, value, key_t):
+def attend_back(first, query, d_out, logs, delta, key_t, value_t):
     tokens = query.shape[-1]
     chunks = first.shape[0]
     return pl.pallas_call(
@@ -185,8 +188,7 @@
                 per_head((REP, HD, tokens)),
                 per_head((REP, tokens)),
                 per_head((REP, tokens)),
-                per_head((GROUP, HD)),
-                per_head((GROUP, HD)),
+                per_head((HD, GROUP)),
                 per_head((HD, GROUP)),
             ],
             out_specs=[
@@ -194,10 +196,11 @@
                 per_head((GROUP, HD)),
                 per_head((GROUP, HD)),
             ],
+            scratch_shapes=[pltpu.VMEM((GROUP, HD), BF), pltpu.VMEM((GROUP, HD), BF)],
         ),
         compiler_params=pltpu.CompilerParams(vmem_limit_bytes=32 * 1024 * 1024),
         name="attend_back",
-    )(first, query, d_out, logs, delta, key, value, key_t)
+    )(first, query, d_out, logs, delta, key_t, value_t)
 
 
 AHEAD = 4
@@ -546,27 +549,43 @@
 STEPS = 8
 
 
-def spread_kernel(forward, *refs):
+def spread_kernel(forward, fast, *refs):
+    refs = list(refs)
+
+    def take(number):
+        taken = refs[:number]
+        del refs[:number]
+        return taken
+
+    (mine_ref,) = take(1)
+    weights = take(5 if forward and fast else 6)
+    if not forward:
+        gate_ref, up_ref = take(2)
+    dealt_in = take(1) if fast else None
     if forward:
-        mine_ref, *weights = refs[:7]
-        all_ref, gate_ref, up_ref, act_ref, out_ref = refs[7:12]
-        rest = refs[12:]
+        all_ref, gate_ref, up_ref, act_ref, out_ref = take(5)
+        if fast:
+            (down_out,) = take(1)
     else:
-        mine_ref, *weights = refs[:7]
-        gate_ref, up_ref = refs[7:9]
-        all_ref, d_gate_up_ref, out_ref = refs[9:12]
-        rest = refs[12:]
-    block, w_gate, w_up, w_down, kept, to_mate, from_mate, far_part, to_far, from_mate_far, far_sum, from_far = rest[:12]
+        all_ref, d_gate_up_ref, out_ref = take(3)
+    dealt_out = take(1) if fast else None
+    block, w_gate, w_up, w_down, kept, to_mate, from_mate, far_part, to_far, from_mate_far, far_sum, from_far = take(12)
     (
         weight_sem, block_sem, out_sem, mate_send, mate_recv, x_send, x_recv, pass_send, pass_recv,
         sum_send, sum_recv, part_send, part_recv, back_send, back_recv,
-    ) = rest[12:27]
-    stage = rest[27:]
+    ) = take(15)
+    deal_send, deal_recv, deal_local, row_send, row_recv, plane_send, plane_recv = take(7)
+    stage = refs
     tokens, depth = mine_ref.shape
     quarter = tokens // 4
     width = w_gate.shape[1]
+    half = depth // 2
+    row = lax.axis_index("row")
     group, side = lax.axis_index("group"), lax.axis_index("side")
     mate, far = {"side": 1 - side}, {"group": 1 - group}
+    other_row, cross = {"row": 1 - row}, {"row": 1 - row, "side": 1 - side}
+    parity = lax.axis_index("dp") % 2
+    next_plane = {"dp": lax.axis_index("dp") + 1 - 2 * parity}
 
     def remote(source, target, send, recv, where):
         return pltpu.make_async_remote_copy(
@@ -574,10 +593,48 @@
         )
 
     barrier = pltpu.get_barrier_semaphore()
-    for where in (mate, far):
+    greeted = [mate, far]
+    if fast:
+        greeted += [other_row, cross] + ([next_plane] if forward else [])
+    for where in greeted:
         pl.semaphore_signal(barrier, 1, device_id=where, device_id_type=pl.DeviceIdType.MESH)
 
-    half = depth // 2
+    dealt_own, dealt_sent, down_chunks = [], [], []
+    if fast:
+        span = tokens // 4
+        member = 2 * row + side
+        for index, (to_row, to_side, where) in enumerate(
+            [(1 - row, side, other_row), (1 - row, 1 - side, cross), (row, 1 - side, mate), (row, side, None)]
+        ):
+            slot = 0 if index >= 2 else 1
+            there = 2 * to_row + to_side
+            for high in range(2):
+                piece = 7 - there if high else there
+                if not forward:
+                    piece = 7 - member if high else member
+                whole = pl.ds(pl.multiple_of(piece * span, span), span), slice(None)
+                of_side = side if forward else to_side
+                first = pl.multiple_of(of_side * 2 * span + high * span, span)
+                part = pl.ds(first, span), pl.ds(slot * half, half)
+                source = dealt_in[0].at[whole] if forward else dealt_in[0].at[part]
+                target = dealt_out[0].at[part] if forward else dealt_out[0].at[whole]
+                if where is None:
+                    dealt_own.append(pltpu.make_async_copy(source, target, deal_local.at[high]))
+                else:
+                    sems = deal_send.at[index, high], deal_recv.at[index, high]
+                    dealt_sent.append(remote(source, target, *sems, where))
+        if forward:
+            rows = width // 8
+            for index in range(4):
+                here = pl.ds(pl.multiple_of((4 * parity + index) * rows, 16), rows)
+                place = w_down.at[here, pl.ds(half, half)]
+                down_chunks.append(
+                    (
+                        remote(weights[4].at[here, :], place, row_send.at[index], row_recv.at[index], other_row),
+                        remote(place, place, plane_send.at[index], plane_recv.at[index], next_plane),
+                    )
+                )
+
     loads = []
     for index, (source, target) in enumerate(
         [
@@ -586,8 +643,8 @@
             (weights[2], w_up.at[pl.ds(0, half), :]),
             (weights[3], w_up.at[pl.ds(half, half), :]),
             (weights[4], w_down.at[:, pl.ds(0, half)]),
-            (weights[5], w_down.at[:, pl.ds(half, half)]),
         ]
+        + ([] if forward and fast else [(weights[5], w_down.at[:, pl.ds(half, half)])])
     ):
         loads.append(pltpu.make_async_copy(source, target, weight_sem.at[index]))
     order = loads if forward else loads[4:] + loads[:4]
@@ -601,7 +658,9 @@
         copy.start()
     for copy in order:
         copy.start()
-    pl.semaphore_wait(barrier, 2)
+    pl.semaphore_wait(barrier, len(greeted))
+    for over_row, over_planes in down_chunks:
+        over_row.start()
 
     def piece(index):
         return mine_ref.at[pl.ds(index * quarter, quarter), :]
@@ -642,6 +701,8 @@
     for index in range(4):
         mate_copy(index).start()
     x_copy(1).start()
+    for copy in dealt_sent + dealt_own:
+        copy.start()
     for copy in mine_copies:
         copy.wait()
 
@@ -670,7 +731,7 @@
             return [
                 pltpu.make_async_copy(stage_gate.at[slot], gate_ref.at[step], out_sem.at[1, step]),
                 pltpu.make_async_copy(stage_up.at[slot], up_ref.at[step], out_sem.at[2, step]),
-                pltpu.make_async_copy(stage_act.at[slot], act_ref.at[step], out_sem.at[3, step]),
+                pltpu.make_async_copy(stage_act.at[step], act_ref.at[step], out_sem.at[3, step]),
             ]
 
         def fetches(step):
@@ -694,15 +755,13 @@
                 up = dot(block[step], w_up[:, where])
                 stage_gate[slot, :, where] = gate.astype(BF)
                 stage_up[slot, :, where] = up.astype(BF)
-                stage_act[slot, :, where] = (gate * up / (1.0 + jnp.exp(-gate))).astype(BF)
-
-        def second_half(step):
-            slot = step % 2
-
-            @pl.loop(0, depth // TILE)
+                stage_act[step, :, where] = (gate * up / (1.0 + jnp.exp(-gate))).astype(BF)
+
+        def second_half(step, first=0, last=depth // TILE):
+            @pl.loop(first, last)
             def _(tile):
                 where = pl.ds(pl.multiple_of(tile * TILE, TILE), TILE)
-                emit(step, where, dot(stage_act[slot], w_down[:, where]))
+                emit(step, where, dot(stage_act[step], w_down[:, where]))
 
     else:
         stage_gate, stage_up, stage_d, fetch_sem = stage
@@ -758,6 +817,8 @@
         far_sum[index] = total.astype(BF)
         back_copy(index).start()
 
+    if forward and fast:
+        down_saved = pltpu.make_async_copy(w_down.at[:, pl.ds(half, half)], down_out, weight_sem.at[5])
     for copy in fetches(0):
         copy.start()
 
@@ -801,7 +862,34 @@
         def _():
             second_loads()
 
-        second_half(step)
+        if forward and fast:
+            @pl.when(step < 4)
+            def _():
+                second_half(step, 0, half // TILE)
+
+            for index in range(4):
+                @pl.when(step == min(index + 1, 3))
+                def _(index=index):
+                    down_chunks[index][0].wait_recv()
+                    down_chunks[index][1].start()
+
+            @pl.when(step == 3)
+            def _():
+                for _, over_planes in down_chunks:
+                    over_planes.wait_recv()
+                down_saved.start()
+
+                @pl.loop(0, 4)
+                def _(early):
+                    second_half(early, half // TILE)
+
+                sum_copy(0).start()
+
+            @pl.when(step >= 4)
+            def _():
+                second_half(step)
+        else:
+            second_half(step)
         for copy in saves(step):
             copy.start()
 
@@ -809,7 +897,7 @@
         def _():
             x_copy(2 + step // 2).start()
 
-        @pl.when((step >= 2) & (step < 4))
+        @pl.when((step == 3) if forward and fast else ((step >= 2) & (step < 4)))
         def _():
             sum_copy(jnp.clip(step - 2, 0, 1)).start()
 
@@ -834,8 +922,15 @@
             copy = pltpu.make_async_copy(kept.at[index // 2], out_ref.at[index // 2], block_sem.at[index // 2])
             copy.start()
             results.append(copy)
-    for copy in results:
+    for copy in results + dealt_own:
         copy.wait()
+    for copy in dealt_sent:
+        copy.wait()
+    for over_row, over_planes in down_chunks:
+        over_row.wait_send()
+        over_planes.wait_send()
+    if forward and fast:
+        down_saved.wait()
 
     @pl.loop(0, STEPS)
     def _(step):
@@ -860,7 +955,7 @@
             sum_copy(jnp.minimum(step, 1)).wait_send()
 
 
-def spread(forward, mine, weights, *kept):
+def spread(forward, mine, weights, kept=(), dealt=None):
     tokens, depth = mine.shape
     quarter, double = tokens // 4, tokens // 2
     width = weights[0].shape[1]
@@ -870,19 +965,29 @@
     out = jax.ShapeDtypeStruct((2, double, depth), F32)
     if forward:
         outs = [whole, wide, wide, wide, out]
-        stage = [pltpu.VMEM((2, double, width), BF) for _ in range(3)]
+        if dealt is not None:
+            outs.append(jax.ShapeDtypeStruct((width, depth // 2), BF))
+            outs.append(jax.ShapeDtypeStruct((tokens, depth), BF))
+        stage = [
+            pltpu.VMEM((2, double, width), BF),
+            pltpu.VMEM((2, double, width), BF),
+            pltpu.VMEM((STEPS, double, width), BF),
+        ]
     else:
         outs = [whole, jax.ShapeDtypeStruct((STEPS, double, 2 * width), BF), out]
+        if dealt is not None:
+            outs.append(jax.ShapeDtypeStruct((2 * tokens, depth // 2), BF))
         stage = [
             pltpu.VMEM((2, double, width), BF),
             pltpu.VMEM((2, double, width), BF),
             pltpu.VMEM((2, double, 2 * width), BF),
             pltpu.SemaphoreType.DMA((2, STEPS)),
         ]
-    result = pl.pallas_call(
-        functools.partial(spread_kernel, forward),
+    inputs = [mine, *weights, *kept] + ([] if dealt is None else [dealt])
+    return pl.pallas_call(
+        functools.partial(spread_kernel, forward, dealt is not None),
         out_shape=outs,
-        in_specs=[anywhere] * (7 + len(kept)),
+        in_specs=[anywhere] * len(inputs),
         out_specs=[anywhere] * len(outs),
         scratch_shapes=[
             pltpu.VMEM((STEPS, double, depth), BF),
@@ -904,6 +1009,8 @@
         + [pltpu.SemaphoreType.DMA((4,)) for _ in range(6)]
         + [pltpu.SemaphoreType.DMA((2,)) for _ in range(2)]
         + [pltpu.SemaphoreType.DMA((4,)) for _ in range(4)]
+        + [pltpu.SemaphoreType.DMA((3, 2)), pltpu.SemaphoreType.DMA((3, 2)), pltpu.SemaphoreType.DMA((2,))]
+        + [pltpu.SemaphoreType.DMA((4,)) for _ in range(4)]
         + stage,
         compiler_params=pltpu.CompilerParams(
             collective_id=1 if forward else 2,
@@ -911,8 +1018,412 @@
             vmem_limit_bytes=60 * 1024 * 1024,
         ),
         name="feed_forward" if forward else "feed_forward_back",
-    )(mine, *weights, *kept)
-    return result
+    )(*inputs)
+
+
+def front_kernel(*refs):
+    refs = list(refs)
+
+    def take(number):
+        taken = refs[:number]
+        del refs[:number]
+        return taken
+
+    tokens_ref, w_project_ref, w_out_ref, gains_ref, gate_ref, up_ref = take(6)
+    cos_ref, sin_ref, query_gain_ref, key_gain_ref = take(4)
+    (
+        states_out, normed_out, raw_out, query_out, key_out, pair_out, mixed_out, logs_out, hidden_out, normed_two_out,
+        w_project_out, w_out_out, gate_out, up_out, gains_out,
+    ) = take(15)
+    states, normed, w_project, raw, key_raw, query, pair_own, pair, key_n, mixed_t, logs, mixed = take(12)
+    w_out, hidden, gains = take(3)
+    token_send, token_recv, token_local = take(3)
+    project_send, project_recv, out_send, out_recv, gain_send, gain_recv = take(6)
+    pair_send, pair_recv, row_send, row_recv, plane_send, plane_recv, local, store = take(8)
+
+    plane, row = lax.axis_index("dp"), lax.axis_index("row")
+    group, side = lax.axis_index("group"), lax.axis_index("side")
+    other_row, mate, far = {"row": 1 - row}, {"side": 1 - side}, {"group": 1 - group}
+    cross = {"row": 1 - row, "side": 1 - side}
+    parity = plane % 2
+    next_plane = {"dp": plane + 1 - 2 * parity}
+    shard, width = tokens_ref.shape
+    mine, depth = states.shape
+    pieces = 8
+    span = shard // pieces
+    member = 2 * row + side
+    kv_rows = key_raw.shape[0]
+
+    def remote(source, target, send, recv, where):
+        return pltpu.make_async_remote_copy(
+            source, target, send, recv, device_id=where, device_id_type=pl.DeviceIdType.MESH
+        )
+
+    barrier = pltpu.get_barrier_semaphore()
+    for where in (other_row, mate, far, cross, next_plane):
+        pl.semaphore_signal(barrier, 1, device_id=where, device_id_type=pl.DeviceIdType.MESH)
+
+    def token_copies(to_row, to_side, index, where):
+        target_member = 2 * to_row + to_side
+        slot = 1 if to_row is not row else 0
+        copies = []
+        for high in range(2):
+            piece = pieces - 1 - target_member if high else target_member
+            source = tokens_ref.at[pl.ds(pl.multiple_of(piece * span, span), span), :]
+            first = pl.multiple_of(side * 2 * span + high * span, span)
+            target = states.at[pl.ds(first, span), pl.ds(slot * width, width)]
+            if where is None:
+                copies.append(pltpu.make_async_copy(source, target, token_local.at[high]))
+            else:
+                sems = token_send.at[index, high], token_recv.at[index, high]
+                copies.append(remote(source, target, *sems, where))
+        return copies
+
+    own_tokens = token_copies(row, side, 0, None)
+    other = 1 - row
+    sent_tokens = token_copies(other, side, 0, other_row)
+    sent_tokens += token_copies(other, 1 - side, 1, cross)
+    sent_tokens += token_copies(row, 1 - side, 2, mate)
+
+    me, far_col = 2 * group + side, 2 * (1 - group) + side
+
+    class Spread:
+        def __init__(self, source, place, send, recv):
+            self.copies = []
+
+            def add(origin, target, where):
+                index = len(self.copies)
+                self.copies.append(remote(origin, target, send.at[index], recv.at[index], where))
+                return self.copies[-1]
+
+            here, there = parity, 1 - parity
+            rows = source.shape[0] // 2
+            first_half = source.at[pl.ds(pl.multiple_of(here * rows, 16), rows), :]
+            self.to_row = add(first_half, place(me, 1, here), other_row)
+            self.to_plane = add(place(me, 1, here), place(me, 1, here), next_plane)
+            self.to_far = [add(source, place(me, 0, None), far)]
+            self.to_far += [add(place(me, 1, half), place(me, 1, half), far) for half in (here, there)]
+            self.to_mate = [add(source, place(me, 0, None), mate)]
+            self.to_mate += [add(place(me, 1, half), place(me, 1, half), mate) for half in (here, there)]
+            self.to_mate += [add(place(far_col, 0, None), place(far_col, 0, None), mate)]
+            self.to_mate += [
+                add(place(far_col, 1, half), place(far_col, 1, half), mate) for half in (here, there)
+            ]
+
+        def first(self):
+            self.to_row.start()
+            self.to_far[0].start()
+            self.to_mate[0].start()
+
+        def row_in(self):
+            self.to_row.wait_recv()
+            for copy in (self.to_plane, self.to_far[1], self.to_mate[1]):
+                copy.start()
+
+        def plane_in(self):
+            self.to_plane.wait_recv()
+            self.to_far[2].start()
+            self.to_mate[2].start()
+
+        def far_in(self, index):
+            self.to_far[index].wait_recv()
+            self.to_mate[3 + index].start()
+
+        def mate_in(self, first, last):
+            for copy in self.to_mate[first:last]:
+                copy.wait_recv()
+
+        def sent(self):
+            for copy in self.copies:
+                copy.wait_send()
+
+    q_width = w_out_ref.shape[0]
+
+    def project_place(col, slot, half):
+        if half is None:
+            return w_project.at[col, slot]
+        return w_project.at[col, slot, pl.ds(pl.multiple_of(half * (width // 2), 16), width // 2), :]
+
+    def out_place(col, slot, half):
+        first, rows = col * q_width, q_width
+        if half is not None:
+            rows = q_width // 2
+            first = first + half * rows
+        return w_out.at[pl.ds(pl.multiple_of(first, 16), rows), pl.ds(slot * width, width)]
+
+    project = Spread(w_project_ref, project_place, project_send, project_recv)
+    output = Spread(w_out_ref, out_place, out_send, out_recv)
+    own_project = pltpu.make_async_copy(w_project_ref, w_project.at[me, 0], local.at[0])
+    own_output = pltpu.make_async_copy(w_out_ref, out_place(me, 0, None), local.at[1])
+    own_gains = pltpu.make_async_copy(gains_ref, gains.at[0], local.at[2])
+    sent_gains = remote(gains_ref, gains.at[1], gain_send.at[0], gain_recv.at[0], other_row)
+
+    chunks = []
+    for index, (source, target) in enumerate([(gate_ref, gate_out), (up_ref, up_out)]):
+        rows = source.shape[0] // 4
+        for part in range(2):
+            here = pl.ds(pl.multiple_of((2 * parity + part) * rows, 64), rows)
+            slot = 2 * index + part
+            over_row = remote(source.at[here, :], target.at[here, :], row_send.at[slot], row_recv.at[slot], other_row)
+            over_planes = remote(
+                target.at[here, :], target.at[here, :], plane_send.at[slot], plane_recv.at[slot], next_plane
+            )
+            chunks.append((over_row, over_planes))
+
+    def pass_on(index):
+        chunks[index][0].wait_recv()
+        chunks[index][1].start()
+
+    own_copies = [own_gains, *own_tokens, own_project, own_output]
+    for copy in own_copies:
+        copy.start()
+    pl.semaphore_wait(barrier, 5)
+    sent_gains.start()
+    project.first()
+    for copy in sent_tokens:
+        copy.start()
+    output.first()
+    chunks[0][0].start()
+    for copy in own_copies:
+        copy.wait()
+    sent_gains.wait_recv()
+    project.row_in()
+    for copy in sent_tokens:
+        copy.wait_recv()
+
+    stores = []
+
+    def save(source, target):
+        copy = pltpu.make_async_copy(source, target, store.at[len(stores)])
+        copy.start()
+        stores.append(copy)
+        return copy
+
+    block = mine // 4
+
+    @pl.loop(0, 4)
+    def _(index):
+        here = pl.ds(pl.multiple_of(index * block, block), block)
+        values = states[here, :].astype(F32)
+        inverse = lax.rsqrt(jnp.mean(values * values, axis=1, keepdims=True) + EPSILON)
+        for slot in range(2):
+            part = values[:, slot * width : (slot + 1) * width] * inverse
+            normed[here, slot * width : (slot + 1) * width] = (part * gains[slot, 0:1, :]).astype(BF)
+
+    save(states, states_out)
+    normed_saved = save(normed, normed_out)
+    save(gains, gains_out)
+
+    def project_col(col):
+        part = dot(normed[:, :width], w_project[col, 0]) + dot(normed[:, width:], w_project[col, 1])
+        part = part.T
+        heads = q_width // HD
+        for head in range(heads):
+            raw[col * heads + head] = part[head * HD : (head + 1) * HD]
+        k_width = kv_rows // 4
+        first = pl.multiple_of(col * k_width, 16)
+        key_raw[pl.ds(first, k_width), :] = part[q_width : q_width + k_width].astype(BF)
+        first = pl.multiple_of(kv_rows + col * k_width, 16)
+        pair_own[pl.ds(first, k_width), :] = part[q_width + k_width :].astype(BF)
+
+    project.plane_in()
+    project.far_in(0)
+    project_col(me)
+    project.mate_in(0, 3)
+    project_col(2 * group + 1 - side)
+    project.far_in(1)
+    project.far_in(2)
+    project_col(far_col)
+    project.mate_in(3, 6)
+    project_col(2 * (1 - group) + 1 - side)
+    save(raw, raw_out)
+    save(key_raw, key_out)
+    save(w_project, w_project_out)
+
+    cosine, sine = cos_ref[...], sin_ref[...]
+
+    def turned(values, gain):
+        values = values * lax.rsqrt(jnp.mean(values * values, axis=0, keepdims=True) + EPSILON) * gain
+        first, second = values[: HD // 2], values[HD // 2 :]
+        return jnp.concatenate([first * cosine - second * sine, second * cosine + first * sine], axis=0)
+
+    for head in range(kv_rows // HD):
+        cut = slice(head * HD, (head + 1) * HD)
+        pair_own[cut, :] = turned(key_raw[cut, :].astype(F32), key_gain_ref[...]).astype(BF)
+
+    def places(who):
+        starts = [who, pieces - 1 - who, pieces + who, 2 * pieces - 1 - who]
+        return [pair.at[:, pl.ds(pl.multiple_of(start * span, span), span)] for start in starts]
+
+    for index, place in enumerate(places(member)):
+        place[...] = pair_own[:, index * span : (index + 1) * span]
+    to_mate, to_row, passed = [], [], []
+    for index, place in enumerate(places(member)):
+        to_row.append(remote(place, place, pair_send.at[0, index], pair_recv.at[0, index], other_row))
+        to_mate.append(remote(place, place, pair_send.at[1, index], pair_recv.at[1, index], mate))
+    for index, place in enumerate(places(2 * (1 - row) + side)):
+        passed.append(remote(place, place, pair_send.at[2, index], pair_recv.at[2, index], mate))
+    for copy in to_row + to_mate:
+        copy.start()
+    chunks[1][0].start()
+    output.row_in()
+    output.far_in(0)
+
+    @pl.loop(0, raw.shape[0])
+    def _(head):
+        values = turned(raw[head], query_gain_ref[...]).astype(BF)
+        query[head] = values * BF(1.0 / math.sqrt(HD))
+
+    for index in range(4):
+        to_row[index].wait_recv()
+        passed[index].start()
+    chunks[2][0].start()
+    output.plane_in()
+    pass_on(0)
+    for index in range(4):
+        to_mate[index].wait_recv()
+        passed[index].wait_recv()
+    chunks[3][0].start()
+    output.far_in(1)
+    output.far_in(2)
+
+    firsts = [member, pieces - 1 - member, pieces + member, 2 * pieces - 1 - member]
+    rows = REP * span
+    ones = jnp.ones((16, KEYS), BF)
+
+    @pl.loop(0, kv_rows // HD)
+    def _(head):
+        key_n[...] = pair[pl.ds(pl.multiple_of(head * HD, HD), HD), :].T
+        value_rows = pl.ds(pl.multiple_of(kv_rows + head * HD, HD), HD)
+        for index in range(4):
+            cut = slice(index * span, (index + 1) * span)
+            query_here = jnp.concatenate([query[head * REP + rep, :, cut] for rep in range(REP)], axis=1)
+            first_query = firsts[index] * span
+            full, last = tiles_of(first_query)
+
+            def tile(where, accum, masked):
+                first_key = pl.multiple_of(where * KEYS, KEYS)
+                expo = jnp.exp(dot(key_n[pl.ds(first_key, KEYS), :], query_here))
+                if masked:
+                    expo = jnp.where(allowed(first_query, first_key, span, rows), expo, 0.0)
+                value = jnp.concatenate([pair[value_rows, pl.ds(first_key, KEYS)], ones], axis=0)
+                return accum + dot(value, expo.astype(BF))
+
+            accum = tile(last, jnp.zeros((HD + 16, rows), F32), True)
+            accum = lax.fori_loop(0, full, lambda where, total: tile(where, total, False), accum)
+            total = accum[HD : HD + 1]
+            result = accum[:HD] / total
+            log = jnp.log(total)
+            for rep in range(REP):
+                part = slice(rep * span, (rep + 1) * span)
+                mixed_t[pl.ds(pl.multiple_of((head * REP + rep) * HD, HD), HD), cut] = result[:, part]
+                logs[head, rep : rep + 1, cut] = log[:, part]
+
+        for number, index in ((1, 1), (3, 2)):
+            @pl.when(head == number)
+            def _(index=index):
+                pass_on(index)
+
+    save(query, query_out)
+    save(mixed_t, mixed_out)
+    save(logs, logs_out)
+    save(pair, pair_out)
+    pass_on(3)
+    output.mate_in(0, 6)
+    save(w_out, w_out_out)
+
+    @pl.loop(0, mixed_t.shape[0] // 128)
+    def _(index):
+        here = pl.ds(pl.multiple_of(index * 128, 128), 128)
+        mixed[:, here] = mixed_t[here, :].astype(BF).T
+
+    @pl.loop(0, depth // TILE)
+    def _(index):
+        here = pl.ds(pl.multiple_of(index * TILE, TILE), TILE)
+        hidden[:, here] = states[:, here].astype(F32) + dot(mixed[...], w_out[:, here])
+
+    normed_saved.wait()
+
+    @pl.loop(0, 4)
+    def _(index):
+        here = pl.ds(pl.multiple_of(index * block, block), block)
+        values = hidden[here, :]
+        inverse = lax.rsqrt(jnp.mean(values * values, axis=1, keepdims=True) + EPSILON)
+        for slot in range(2):
+            part = values[:, slot * width : (slot + 1) * width] * inverse
+            normed[here, slot * width : (slot + 1) * width] = (part * gains[slot, 1:2, :]).astype(BF)
+
+    save(hidden, hidden_out)
+    save(normed, normed_two_out)
+    for copy in stores:
+        if copy is not normed_saved:
+            copy.wait()
+    sent_gains.wait_send()
+    for copy in sent_tokens + to_row + to_mate + passed:
+        copy.wait_send()
+    project.sent()
+    output.sent()
+    for over_row, over_planes in chunks:
+        over_row.wait_send()
+        over_planes.wait_recv()
+        over_planes.wait_send()
+
+
+def front(tokens, w_project, w_out, gains, w_gate, w_up, cosine, sine, query_gain, key_gain):
+    shard, width = tokens.shape
+    mine, depth = shard // 2, 2 * width
+    q_width, columns = w_out.shape[0], w_project.shape[1]
+    kv_rows = KVH * HD
+    anywhere = pl.BlockSpec(memory_space=pl.ANY)
+    inside = pl.BlockSpec(memory_space=pltpu.VMEM)
+    dma = pltpu.SemaphoreType.DMA
+    shape = jax.ShapeDtypeStruct
+    return pl.pallas_call(
+        front_kernel,
+        out_shape=[
+            shape((mine, depth), BF),
+            shape((mine, depth), BF),
+            shape((QH, HD, mine), F32),
+            shape((QH, HD, mine), BF),
+            shape((kv_rows, mine), BF),
+            shape((2 * kv_rows, GROUP), BF),
+            shape((QH * HD, mine), F32),
+            shape((KVH, REP, mine), F32),
+            shape((mine, depth), F32),
+            shape((mine, depth), BF),
+            shape((4, 2, width, columns), BF),
+            shape((4 * q_width, depth), BF),
+            shape(w_gate.shape, BF),
+            shape(w_up.shape, BF),
+            shape((2, 2, width), F32),
+        ],
+        in_specs=[anywhere] * 6 + [inside] * 4,
+        out_specs=[anywhere] * 15,
+        scratch_shapes=[
+            pltpu.VMEM((mine, depth), BF),
+            pltpu.VMEM((mine, depth), BF),
+            pltpu.VMEM((4, 2, width, columns), BF),
+            pltpu.VMEM((QH, HD, mine), F32),
+            pltpu.VMEM((kv_rows, mine), BF),
+            pltpu.VMEM((QH, HD, mine), BF),
+            pltpu.VMEM((2 * kv_rows, mine), BF),
+            pltpu.VMEM((2 * kv_rows, GROUP), BF),
+            pltpu.VMEM((GROUP, HD), BF),
+            pltpu.VMEM((QH * HD, mine), F32),
+            pltpu.VMEM((KVH, REP, mine), F32),
+            pltpu.VMEM((mine, QH * HD), BF),
+            pltpu.VMEM((4 * q_width, depth), BF),
+            pltpu.VMEM((mine, depth), F32),
+            pltpu.VMEM((2, 2, width), F32),
+            dma((3, 2)), dma((3, 2)), dma((2,)),
+            dma((11,)), dma((11,)), dma((11,)), dma((11,)), dma((1,)), dma((1,)),
+            dma((3, 4)), dma((3, 4)), dma((4,)), dma((4,)), dma((4,)), dma((4,)), dma((3,)), dma((13,)),
+        ],
+        compiler_params=pltpu.CompilerParams(
+            collective_id=3, has_side_effects=True, vmem_limit_bytes=56 * 1024 * 1024
+        ),
+        name="front",
+    )(tokens, w_project, w_out, gains, w_gate, w_up, cosine, sine, query_gain, key_gain)
 
 
 def body(
@@ -1008,50 +1519,10 @@
         + jnp.stack([member, pieces - 1 - member] * 2).astype(jnp.int32) * span
     )
 
-    states = to_members(tokens).astype(F32)
-    gain_one = gather_rows(norm1_gain, 0)
-    gain_two = gather_rows(norm2_gain, 0)
-    w_project = jnp.concatenate([w_query, w_key, w_value], axis=1)
-    w_project = gather_rows(w_project, 0)
-    w_project = lax.all_gather(w_project, ("group", "side"), axis=0)
-    w_out_all = gather_rows(w_out, 1)
-    w_out_all = lax.all_gather(w_out_all, ("group", "side"), axis=0, tiled=True)
-    def halves(block, axis):
-        if rows == 2:
-            return [block, from_row(block, 1)]
-        return jnp.split(gather_rows(block, axis), 2, axis=axis)
-
-    ffn_weights = halves(w_gate, 0) + halves(w_up, 0) + halves(w_down, 1)
-    target = to_members(teacher)
-
     half = HD // 2
     freq = jnp.exp(jnp.arange(half, dtype=F32) * (-2.0 * math.log(10000.0) / HD))
     angle = freq[:, None] * pick(positions).astype(F32)[None, :]
     cosine, sine = jnp.cos(angle), jnp.sin(angle)
-    inverse_one = rms(states)
-    normed_one = (states * inverse_one * gain_one).astype(BF)
-    projected = dot(w_project, normed_one, ((1,), (1,)))
-    query_raw = projected[:, :q_width].reshape(QH, HD, mine)
-    key_sent = projected[:, q_width : q_width + k_width].reshape(KVH, HD, mine).astype(BF)
-    value_sent = projected[:, q_width + k_width :].reshape(KVH, HD, mine).astype(BF)
-    query_rot, query_back = jax.vjp(
-        lambda raw, gain: prepare(raw, gain, cosine, sine), query_raw, query_gain
-    )
-    key_rot, key_back = jax.vjp(
-        lambda raw, gain: prepare(raw, gain, cosine, sine), key_sent.astype(F32), key_gain
-    )
-    scale = 1.0 / math.sqrt(HD)
-    query_use = (query_rot.astype(BF) * BF(scale)).reshape(KVH, REP, HD, mine)
-    pair = jnp.stack([key_rot.astype(BF), value_sent])
-    pair = lax.all_gather(pair, ("row", "side"), axis=0)
-
-    def natural(stacked):
-        lead = stacked.shape[1:-1]
-        parts = stacked.reshape((members,) + lead + (cores, 2, span))
-        low, high = parts[..., 0, :], parts[..., 1, :]
-        both = jnp.concatenate([low, high[::-1]], axis=0)
-        return jnp.moveaxis(both, 0, -2).reshape(lead + (GROUP,))
-
     def dealt(full):
         lead, entry = full.shape[:-2], full.shape[-1]
         parts = full.reshape(lead + (cores, pieces, span, entry))
@@ -1061,25 +1532,103 @@
         both = jnp.moveaxis(both, -4, 0)
         return both.reshape((members,) + lead + (mine, entry))
 
-    pair = natural(pair)
-    key_t, value_t = pair[0], pair[1]
-    key_n, value_n = key_t.transpose(0, 2, 1), value_t.transpose(0, 2, 1)
-    value_one = jnp.concatenate([value_t, jnp.ones((KVH, 16, GROUP), BF)], axis=1)
-    mixed_f, logs = attend(first_tokens, query_use, key_n, value_one)
-    mixed = mixed_f.reshape(QH * HD, mine).astype(BF)
-    hidden = states + dot(mixed, w_out_all, ((0,), (0,)))
-
-    inverse_two = rms(hidden)
-    normed_two = (hidden * inverse_two * gain_two).astype(BF)
-    normed_all, gate, up, activated, ffn_out = spread(True, normed_two, ffn_weights)
+    w_project = jnp.concatenate([w_query, w_key, w_value], axis=1)
+    scale = 1.0 / math.sqrt(HD)
+    fast = rows == 2 and cols == 4 and lax.axis_size("dp") % 2 == 0 and mine == 4 * span
+    if fast:
+        (
+            states, normed_one, query_raw, query_use, key_sent, pair, mixed_f, logs, hidden,
+            normed_two, w_project, w_out_all, gate_other, up_other, gains,
+        ) = front(
+            tokens, w_project, w_out, jnp.stack([norm1_gain, norm2_gain]), w_gate, w_up,
+            cosine, sine, query_gain[:, None], key_gain[:, None],
+        )
+        states = states.astype(F32)
+        inverse_one, inverse_two = rms(states), rms(hidden)
+        gain_one, gain_two = gains[:, 0].reshape(D), gains[:, 1].reshape(D)
+        key_sent = key_sent.reshape(KVH, HD, mine)
+        query_use = query_use.reshape(KVH, REP, HD, mine)
+        mixed_f = mixed_f.reshape(KVH, REP, HD, mine)
+        pair = pair.reshape(2, KVH, HD, GROUP)
+        key_t, value_t = pair[0], pair[1]
+        mixed = mixed_f.reshape(QH * HD, mine).astype(BF)
+        w_project = w_project.reshape(cols, D, -1)
+        ffn_weights = [w_gate, gate_other, w_up, up_other, w_down]
+        query_back = jax.vjp(
+            lambda raw, gain: prepare(raw, gain, cosine, sine), query_raw, query_gain
+        )[1]
+        key_back = jax.vjp(
+            lambda raw, gain: prepare(raw, gain, cosine, sine), key_sent.astype(F32), key_gain
+        )[1]
+    else:
+        states = to_members(tokens).astype(F32)
+        gain_one = gather_rows(norm1_gain, 0)
+        gain_two = gather_rows(norm2_gain, 0)
+        w_project = gather_rows(w_project, 0)
+        w_project = lax.all_gather(w_project, ("group", "side"), axis=0)
+        w_out_all = gather_rows(w_out, 1)
+        w_out_all = lax.all_gather(w_out_all, ("group", "side"), axis=0, tiled=True)
+        def halves(block, axis):
+            if rows == 2:
+                return [block, from_row(block, 1)]
+            return jnp.split(gather_rows(block, axis), 2, axis=axis)
+
+        ffn_weights = halves(w_gate, 0) + halves(w_up, 0) + halves(w_down, 1)
+        inverse_one = rms(states)
+        normed_one = (states * inverse_one * gain_one).astype(BF)
+        projected = dot(w_project, normed_one, ((1,), (1,)))
+        query_raw = projected[:, :q_width].reshape(QH, HD, mine)
+        key_sent = projected[:, q_width : q_width + k_width].reshape(KVH, HD, mine).astype(BF)
+        value_sent = projected[:, q_width + k_width :].reshape(KVH, HD, mine).astype(BF)
+        query_rot, query_back = jax.vjp(
+            lambda raw, gain: prepare(raw, gain, cosine, sine), query_raw, query_gain
+        )
+        key_rot, key_back = jax.vjp(
+            lambda raw, gain: prepare(raw, gain, cosine, sine), key_sent.astype(F32), key_gain
+        )
+        query_use = (query_rot.astype(BF) * BF(scale)).reshape(KVH, REP, HD, mine)
+        pair = jnp.stack([key_rot.astype(BF), value_sent])
+        pair = lax.all_gather(pair, ("row", "side"), axis=0)
+
+        def natural(stacked):
+            lead = stacked.shape[1:-1]
+            parts = stacked.reshape((members,) + lead + (cores, 2, span))
+            low, high = parts[..., 0, :], parts[..., 1, :]
+            both = jnp.concatenate([low, high[::-1]], axis=0)
+            return jnp.moveaxis(both, 0, -2).reshape(lead + (GROUP,))
+
+        pair = natural(pair)
+        key_t, value_t = pair[0], pair[1]
+        key_n = key_t.transpose(0, 2, 1)
+        value_one = jnp.concatenate([value_t, jnp.ones((KVH, 16, GROUP), BF)], axis=1)
+        mixed_f, logs = attend(first_tokens, query_use, key_n, value_one)
+        mixed = mixed_f.reshape(QH * HD, mine).astype(BF)
+        hidden = states + dot(mixed, w_out_all, ((0,), (0,)))
+
+        inverse_two = rms(hidden)
+        normed_two = (hidden * inverse_two * gain_two).astype(BF)
+
+    if fast:
+        normed_all, gate, up, activated, ffn_out, down_other, target = spread(
+            True, normed_two, ffn_weights, dealt=teacher
+        )
+        ffn_weights.append(down_other)
+    else:
+        normed_all, gate, up, activated, ffn_out = spread(True, normed_two, ffn_weights)
+        target = to_members(teacher)
     ffn_out = ffn_out.reshape(mine, D)
     result = hidden + ffn_out
-    block_out = from_members(result.astype(BF))
 
     total_tokens = shard * cols * lax.axis_size("dp")
     loss_scale = total_tokens / token_count[0].astype(F32)
     d_result = loss_scale * (result - target.astype(F32))
-    d_low, d_gate_up, d_normed = spread(False, d_result.astype(BF), ffn_weights, gate, up)
+    if fast:
+        d_low, d_gate_up, d_normed, block_out = spread(
+            False, d_result.astype(BF), ffn_weights, (gate, up), result.astype(BF)
+        )
+    else:
+        d_low, d_gate_up, d_normed = spread(False, d_result.astype(BF), ffn_weights, (gate, up))
+        block_out = from_members(result.astype(BF))
     d_normed = d_normed.reshape(mine, D)
     d_low, normed_all = d_low.reshape(-1, D), normed_all.reshape(-1, D)
     grad_down = dot(activated.reshape(-1, ff), d_low, ((0,), (0,))).astype(BF)
@@ -1093,7 +1642,7 @@
     d_mixed = d_mixed.reshape(KVH, REP, HD, mine)
     delta = jnp.sum(d_mixed.astype(F32) * mixed_f, axis=2)
     d_query, d_key_n, d_value_n = attend_back(
-        first_tokens, query_use, d_mixed, logs, delta, key_n, value_n, key_t
+        first_tokens, query_use, d_mixed, logs, delta, key_t, value_t
     )
     d_pair = dealt(jnp.stack([d_key_n, d_value_n])).astype(BF)
     d_pair = lax.psum_scatter(d_pair, ("row", "side"), scatter_dimension=0, tiled=True)[0]

time: 1050 us -> 915 us (0.87)
  waiting for transfers between devices: 170 us -> 0.04 us
  Pallas kernels: 545 us -> 684 us
  local copies, waits for them, and re-layouts: 121 us -> 70.1 us
  starting transfers between devices: 26.5 us -> 5.47 us
  other arithmetic: 72.7 us -> 55.8 us
  matrix products: 89.7 us -> 73.4 us
    ppermute x7 -> x0, waiting for transfers between devices: 148 us -> none  [from_row(): return lax.ppermute(block, 'row', pairs)]
    pallas_call x3, Pallas kernels: 232 us -> 372 us  [the longest x2 222 us: spread(): pl.pallas_call(functools.partial(spread_kernel, forward, dealt is not Non...]
    all_to_all x2 -> x0, waiting for transfers between devices: 22.4 us -> none  [to_members(): moved = lax.all_to_all(parts, ('row', 'side'), 0, 0, tiled=True)]
    dot_general x7 -> x5, matrix products: 79.9 us -> 64 us  [dot(): lax.dot_general(left, right, (dims, ((), ())), preferred_element_type=F32)]
    unnamed x89 -> x75, local copies, waits for them, and re-layouts: 30.5 us -> 16.6 us
  transfers between devices with their start and end apart: 15 -> 2, of which waited for: 6 -> 0; matrix products, arithmetic and copies ran while one was open for 20% -> 11% of each run, Pallas kernels for 29% -> 30%
where the time goes in v4:
time: 915 us; the launch traced here: 904 us
  Pallas kernels  684 us (75%)
  matrix products  73.4 us (8%)
  local copies, waits for them, and re-layouts  70.1 us (8%)
  other arithmetic  55.8 us (6%)
  between operations  15.9 us (2%)
    pallas_call x1, Pallas kernels, reduce_all(): pl.pallas_call(functools.partial(reduce_kernel, parts, planes), out_shape...  272 us
    pallas_call x2, Pallas kernels, spread(): pl.pallas_call(functools.partial(spread_kernel, forward, dealt is not Non...  222 us
    pallas_call x1, Pallas kernels, front(): pl.pallas_call(front_kernel, out_shape=[shape((mine, depth), BF), shape((...  150 us
    dot_general x5, matrix products, dot(): lax.dot_general(left, right, (dims, ((), ())), preferred_element_type=F32)  64 us
    pallas_call x1, Pallas kernels, attend_back(): pl.pallas_call(functools.partial(attend_back_kernel, chunks, tokens // ch...  38.9 us
  transfers between devices with their start and end apart: 2, of which 0 were waited for; matrix products, arithmetic and copies ran while one was open for 11% of the time, Pallas kernels for 30%

profile of v4, /device:TPU:0, one launch (start us, length us, event | category | flops | bytes accessed | tf_op | source)
XLA Modules:
  0.0 904.2 jit_solution(4241015417461220017)
XLA Ops:
  18.7 150.3 %front.1 = (bf16[512,2048]{1,0:T(8,128)(2,1)}, bf16[512,2048]{1,0:T(8,128)(2,1)}, f32[20,64,512]{2,1,0:T(8,128)}, bf16[20,64,512]{2,1,0:T(8,128)(2,1)}, bf16[320...) custom-call(bf16[1024,1024]{1,0:T(8,128)(2,1)} %refs_0_.1, ...), custom_call_target="tpu_custom_call" | custom-call | tf_op jit(solution)/shard_map/front/pallas_call | solution.py:1381
  169.0 118.0 %feed_forward.1 = (bf16[8,256,2048]{2,1,0:T(8,128)(2,1)}, bf16[8,256,1280]{2,1,0:T(8,128)(2,1)}, bf16[8,256,1280]{2,1,0:T(8,128)(2,1)}, bf16[8,256,1280]{2,1,0:T...) custom-call(bf16[512,2048]{1,0:T(8,128)(2,1)} %get-tuple-element.49.refs_0_, ...), custom_call_target="tpu_custom_call" | custom-call | tf_op jit(solution)/shard_map/feed_forward/pallas_call | solution.py:987
  287.1 7.8 fusion.19
  294.9 103.9 %feed_forward_back.1 = (bf16[8,256,2048]{2,1,0:T(8,128)(2,1)}, bf16[8,256,2560]{2,1,0:T(8,128)(2,1)}, f32[2,256,2048]{2,1,0:T(8,128)}, bf16[1024,1024]{1,0:T(8,128)(2,1)}) custom-call(bf16[512,2048]{1,0:T(8,128)(2,1)} %get-tuple-element.143.refs_0_, bf16[1024,1280]{1,0:T(8,128)(2,1)} %refs_1_.3, bf16[1024,1280]{1,0:T(8,128)(2,1)} %get-tuple-element.50.refs_2_, ...), custom_call_target="tpu_custom_call" | custom-call | tf_op jit(solution)/shard_map/feed_forward_back/pallas_call | solution.py:987
  398.8 5.1 fusion.13
  414.5 38.9 %attend_back.1 = (f32[5,4,64,512]{3,2,1,0:T(8,128)S(1)}, f32[5,2048,64]{2,1,0:T(8,128)S(1)}, f32[5,2048,64]{2,1,0:T(8,128)S(1)}) custom-call(s32[4]{0:T(128)S(1)} %fusion.40.first_ref, bf16[5,4,64,512]{3,2,1,0:T(8,128)(2,1)S(1)} %bitcast.119, bf16[5,4,64,512]{3,2,1,0:T(8,128)(2,1)S(1)} %bitcast.118, f32[5,4,512]{2,1,0:T(4,128)S(1)} %copy-done.3, ...), custom_call_target="tpu_custom_call" | custom-call | tf_op jit(solution)/shard_map/attend_back/pallas_call | solution.py:176
  458.2 4.5 copy.80
  462.6 4.5 copy.81
  469.4 4.2 copy.82
  473.6 5.1 convert_element_type.100
  483.0 17.5 %bitcast_convert_fusion.1.refs_0_ = bf16[1280,2048]{1,0:T(8,128)(2,1)} fusion(bf16[8,256,1280]{2,1,0:T(8,128)(2,1)} %get-tuple-element.72, bf16[8,256,2048]{2,1,0:T(8,128)(2,1)} %get-tuple-element.73), kind=kOutput, calls=%fused_computation.1 | convolution fusion | flops 10740039680 | bytes 18874368 | tf_op jit(solution)/shard_map/dot_general | solution.py:29
  501.8 3.6 fusion.15
  505.3 28.6 %bitcast_convert_fusion.refs_1_ = bf16[2048,2560]{1,0:T(8,128)(2,1)} fusion(bf16[8,256,2048]{2,1,0:T(8,128)(2,1)} %get-tuple-element.74, bf16[8,256,2560]{2,1,0:T(8,128)(2,1)} %get-tuple-element.75), kind=kOutput, calls=%fused_computation | convolution fusion | flops 21480079360 | bytes 29360128 | tf_op jit(solution)/shard_map/dot_general | solution.py:29
  536.2 8.1 fusion.7
  547.5 6.6 reshape.267
  560.6 5.4 all-to-all-start
  566.1 6.8 convolution_convert_fusion
  572.9 9.4 %convolution_convert_fusion.1 = bf16[4,480,2048]{2,1,0:T(8,128)(2,1)} fusion(bf16[512,2048]{1,0:T(8,128)(2,1)} %get-tuple-element.76, bf16[4,80,512]{2,1,0:T(8,128)(2,1)S(1)} %bitcast.134, bf16[4,80,512]{2,1,0:T(8,128)(2,1)S(1)} %bitcast.136, bf16[4,320,512]{2,1,0:T(8,128)(2,1)} %bitcast.130), kind=kOutput, calls=%fused_computation.11 | convolution fusion | flops 4036362240 | bytes 11927552 | tf_op jit(solution)/shard_map/dot_general | solution.py:1665
  582.3 11.3 %copy.88 = bf16[4,480,2048]{1,2,0:T(8,128)(2,1)} copy(bf16[4,480,2048]{2,1,0:T(8,128)(2,1)} %convolution_convert_fusion.1) | data formatting | bytes 15728640 | tf_op jit(solution)/shard_map/convert_element_type | solution.py:1668
  594.3 272.4 %reduce_grads.1 = (bf16[1280,1024]{1,0:T(8,128)(2,1)}, bf16[1024,2560]{1,0:T(8,128)(2,1)}, bf16[320,1024]{1,0:T(8,128)(2,1)}, bf16[1024,480]{1,0:T(8,128)(2,1)}, f32[40,128]{1,0:T(8,128)}) custom-call(bf16[1280,2048]{1,0:T(8,128)(2,1)} %bitcast_convert_fusion.1.refs_0_, bf16[2048,2560]{1,0:T(8,128)(2,1)} %bitcast_convert_fusion.refs_1_, ...), custom_call_target="tpu_custom_call" | custom-call | tf_op jit(solution)/shard_map/reduce_grads/pallas_call | solution.py:527
  866.7 4.8 convert_element_type.114
  877.7 7.4 slice_convert_fusion
  885.1 4.0 slice_bitcast_fusion.1
  890.6 5.0 pad_maximum_fusion
  (130 shorter events, 55.1 us)
Async XLA Ops:
  7.2 526.8 %reduce-scatter.2.cloned.1.call-start = ((), (), s32[]{:S(2)}) async-start(), calls=%async_computation.2 | async-start | bytes 3276800 | tf_op jit(solution)/shard_map/reduce_scatter | solution.py:1648
  287.1 7.8 copy-start.27
  294.9 103.9 %copy-start.13 = (bf16[512,2048]{1,0:T(8,128)(2,1)S(1)}, bf16[512,2048]{1,0:T(8,128)(2,1)}, u32[]{:S(2)}) copy-start(bf16[512,2048]{1,0:T(8,128)(2,1)} %get-tuple-element.60) | copy-start | bytes 6291460
  398.8 7.6 copy-start.6
  398.8 7.6 copy-start.9
  398.8 7.6 copy-start.12
  403.9 3.6 copy-start.4
  403.9 6.2 slice-start
  407.5 2.6 slice-start.1
  410.1 3.0 copy-start.7
  410.1 3.2 copy-start.17
  453.4 2.4 copy-start
  479.6 2.7 copy-start.5
  482.9 17.6 %copy-start.10 = (f32[20,32,512]{2,1,0:T(8,128)S(1)}, f32[20,32,512]{2,1,0:T(8,128)}, u32[]{:S(2)}) copy-start(f32[20,32,512]{2,1,0:T(8,128)} %get-tuple-element.149) | copy-start | bytes 3932164
  482.9 17.6 %copy-start.11 = (f32[20,32,512]{2,1,0:T(8,128)S(1)}, f32[20,32,512]{2,1,0:T(8,128)}, u32[]{:S(2)}) copy-start(f32[20,32,512]{2,1,0:T(8,128)} %get-tuple-element.150) | copy-start | bytes 3932164
  483.0 17.6 %copy-start.29 = (f32[64]{0:T(128)S(1)}, f32[64]{0:T(128)}, u32[]{:S(2)}) copy-start(f32[64]{0:T(128)} %param.23) | copy-start | bytes 772
  535.9 8.3 copy-start.24
  536.2 8.1 copy-start.8
  560.6 5.4 copy-start.18
  560.6 324.5 %all-to-all-start = ((f32[4,2,128,1024]{3,2,1,0:T(8,128)}), f32[4,2,128,1024]{3,2,1,0:T(8,128)}, u32[]{:S(2)}, u32[]{:S(2)}) async-start(f32[4,2,128,1024]{3,2,1,0:T(8,128)} %bitcast.121), calls=%async_computation.1 | async-start | bytes 8388608 | tf_op jit(solution)/shard_map/all_to_all | solution.py:1507
  566.0 6.9 copy-start.25
  866.7 4.8 copy-start.15
  873.2 3.2 copy-start.26
  890.6 5.0 copy-start.19
  (11 other events, 16.4 us)
Sparse Core Ops, SparseCore 0:
  478.9 35.4 reduce-scatter.1

commit v5 on v4

--- a/solution.py
+++ b/solution.py
@@ -205,7 +205,7 @@
 
 AHEAD = 4
 SLOTS = AHEAD + 2
-LAG = 4
+FAR_LAG, WIDE_LAG, LAG = 1, 2, 4
 SMALL = 40
 
 
@@ -232,19 +232,20 @@
         return taken
 
     grads = take(count)
-    (small_ref,) = take(1)
+    (small_ref, mine_ref) = take(2)
     outs = take(count)
-    (small_out,) = take(1)
+    (small_out, dealt_ref) = take(2)
     near, far, wide, own = take(count), take(count), take(count), take(count)
     col_parts = [j for j in range(count) if parts[j].col]
     mate_in = dict(zip(col_parts, take(len(col_parts))))
     far_in = dict(zip(col_parts, take(len(col_parts))))
     own_sem, out_sem, row_send, row_recv, in_send, far_recv, mid_send, wide_recv = take(8)
     col_own, col_send, col_recv, x_send, x_recv, small_local, small_send, small_recv = take(8)
-    small_in, small_sum = take(2)
+    small_in, small_sum, deal_send, deal_recv, deal_local = take(5)
     plane, row = lax.axis_index("dp"), lax.axis_index("row")
     group, side = lax.axis_index("group"), lax.axis_index("side")
     other_row, mate, far_dev = {"row": 1 - row}, {"side": 1 - side}, {"group": 1 - group}
+    cross = {"row": 1 - row, "side": 1 - side}
     at_end = (plane == 0) | (plane == planes - 1)
     low = plane < planes // 2
     end_next = {"dp": jnp.where(low, 1, planes - 2)}
@@ -261,19 +262,19 @@
     def greet(where):
         pl.semaphore_signal(barrier, 1, device_id=where, device_id_type=pl.DeviceIdType.MESH)
 
-    for where in (other_row, mate, far_dev):
+    for where in (other_row, mate, far_dev, cross):
         greet(where)
 
     @pl.when(at_end)
     def _():
         greet(end_next)
-        pl.semaphore_wait(barrier, 4)
+        pl.semaphore_wait(barrier, 5)
 
     @pl.when(jnp.logical_not(at_end))
     def _():
         greet(mid_outer)
         greet(mid_other)
-        pl.semaphore_wait(barrier, 5)
+        pl.semaphore_wait(barrier, 6)
 
     def col_slot(j, half, index):
         before = sum(2 * parts[i].count for i in col_parts if i < j)
@@ -310,15 +311,12 @@
         for target in range(2):
             col_own_copy(j, half, index, target).wait()
             col_copy(j, half, index, target).wait_recv()
-            total = own[j][target, half, index].astype(F32)
-            total += mate_in[j][target, half, index].astype(F32)
-            mate_in[j][target, half, index] = total.astype(BF)
+            mate_in[j][target, half, index] = mate_in[j][target, half, index] + own[j][target, half, index]
         x_copy(j, half, index).start()
 
     def take_x(j, half, index):
         x_copy(j, half, index).wait_recv()
-        total = far_in[j][half, index].astype(F32) + mate_in[j][group, half, index].astype(F32)
-        far_in[j][half, index] = total.astype(BF)
+        far_in[j][half, index] = far_in[j][half, index] + mate_in[j][group, half, index]
 
     def row_copy(j, index):
         slot = parts[j].base + index
@@ -367,7 +365,7 @@
         else:
             own_copy(j, index).wait()
             mine = own[j][index % SLOTS]
-        near[j][index] = (near[j][index].astype(F32) + mine.astype(F32)).astype(BF)
+        near[j][index] = near[j][index] + mine
 
         @pl.when(at_end)
         def _():
@@ -375,12 +373,12 @@
 
     def take_far(j, index):
         back_copy(j, index).wait_recv()
-        far[j][index] = (far[j][index].astype(F32) + near[j][index].astype(F32)).astype(BF)
+        far[j][index] = far[j][index] + near[j][index]
         mid_copy(j, index).start()
 
     def take_wide(j, index):
         mid_copy(j, index).wait_recv()
-        wide[j][index] = (wide[j][index].astype(F32) + far[j][index].astype(F32)).astype(BF)
+        wide[j][index] = wide[j][index] + far[j][index]
         back_copy(j, index).start()
         out_copy(j, index, wide).start()
 
@@ -409,8 +407,26 @@
     small_load = pltpu.make_async_copy(small_ref, small_sum.at[0], small_local.at[0])
     small_store = pltpu.make_async_copy(small_sum.at[5], small_out, small_local.at[1])
 
+    span, width = mine_ref.shape[0] // 4, mine_ref.shape[1] // 2
+    member = 2 * row + side
+    dealt = []
+    for index, (to_row, to_side, where) in enumerate(
+        [(1 - row, side, other_row), (1 - row, 1 - side, cross), (row, 1 - side, mate), (row, side, None)]
+    ):
+        for high in range(2):
+            piece = 7 - member if high else member
+            first = pl.multiple_of(to_side * 2 * span + high * span, span)
+            source = mine_ref.at[pl.ds(first, span), pl.ds((0 if index >= 2 else 1) * width, width)]
+            target = dealt_ref.at[pl.ds(pl.multiple_of(piece * span, span), span), :]
+            if where is None:
+                dealt.append(pltpu.make_async_copy(source, target, deal_local.at[high]))
+            else:
+                dealt.append(remote(source, target, deal_send.at[index, high], deal_recv.at[index, high], where))
+
     total = sum(part.count for part in parts)
     small_load.start()
+    for copy in dealt[4:]:
+        copy.start()
     for j in col_parts:
         for half in (1, 0):
             for index in range(parts[j].count):
@@ -435,8 +451,13 @@
 
         @pl.when(jnp.logical_not(at_end))
         def _():
-            each(step - 1, take_far)
-            each(step - 2, take_wide)
+            each(step - FAR_LAG, take_far)
+            each(step - WIDE_LAG, take_wide)
+
+        @pl.when(step == total - AHEAD)
+        def _():
+            for copy in dealt[:4]:
+                copy.start()
 
         for place, piece in enumerate(pieces):
             @pl.when(step == place + 1)
@@ -486,6 +507,8 @@
     for copy in plane_hops:
         copy.wait_send()
     small_store.wait()
+    for copy in dealt:
+        copy.wait()
     for j, half, index in pieces:
         for target in range(2):
             col_copy(j, half, index, target).wait_send()
@@ -509,7 +532,7 @@
             each(step, finish_mid)
 
 
-def reduce_all(planes, grads, small):
+def reduce_all(planes, grads, small, mine):
     parts, base = [], 0
     for grad, axis, rows in grads:
         height, width = grad.shape[-2:]
@@ -527,9 +550,12 @@
     return pl.pallas_call(
         functools.partial(reduce_kernel, parts, planes),
         out_shape=[jax.ShapeDtypeStruct((n * r, c), BF) for n, r, c in shapes]
-        + [jax.ShapeDtypeStruct(small.shape, F32)],
-        in_specs=[anywhere] * (len(parts) + 1),
-        out_specs=[anywhere] * (len(parts) + 1),
+        + [
+            jax.ShapeDtypeStruct(small.shape, F32),
+            jax.ShapeDtypeStruct((2 * mine.shape[0], mine.shape[1] // 2), BF),
+        ],
+        in_specs=[anywhere] * (len(parts) + 2),
+        out_specs=[anywhere] * (len(parts) + 2),
         scratch_shapes=[pltpu.VMEM(shape, BF) for _ in range(3) for shape in shapes]
         + [pltpu.VMEM(shape, BF) for shape in own_shapes]
         + [pltpu.VMEM((2, *shape), BF) for shape in col_shapes]
@@ -537,12 +563,13 @@
         + [dma((base,)) for _ in range(8)]
         + [dma((2, pieces)), dma((2, pieces)), dma((2, pieces)), dma((pieces,)), dma((pieces,))]
         + [dma((2,)), dma((5,)), dma((5,))]
-        + [pltpu.VMEM((5, *small.shape), F32), pltpu.VMEM((6, *small.shape), F32)],
+        + [pltpu.VMEM((5, *small.shape), F32), pltpu.VMEM((6, *small.shape), F32)]
+        + [dma((3, 2)), dma((3, 2)), dma((2,))],
         compiler_params=pltpu.CompilerParams(
             collective_id=0, has_side_effects=True, vmem_limit_bytes=60 * 1024 * 1024
         ),
         name="reduce_grads",
-    )(*[grad for grad, _, _ in grads], small)
+    )(*[grad for grad, _, _ in grads], small, mine)
 
 
 TILE = 256
@@ -1426,6 +1453,159 @@
     )(tokens, w_project, w_out, gains, w_gate, w_up, cosine, sine, query_gain, key_gain)
 
 
+def back_kernel(*refs):
+    query, d_out, logs_ref, delta_ref, pair, raw, key_raw, cos_ref, sin_ref, query_gain, key_gain = refs[:11]
+    d_project, query_gain_out, key_gain_out = refs[11:14]
+    key_n, value_n, d_key, d_value, both_t, staged, come, gain_sum, send_sem, recv_sem = refs[14:]
+    row, side = lax.axis_index("row"), lax.axis_index("side")
+    others = [
+        (2 * (1 - row) + side, {"row": 1 - row}),
+        (2 * (1 - row) + 1 - side, {"row": 1 - row, "side": 1 - side}),
+        (2 * row + 1 - side, {"side": 1 - side}),
+    ]
+    member = 2 * row + side
+    pieces = 8
+    span = query.shape[2] // 4
+    rows = REP * span
+    kv_rows = key_raw.shape[0]
+    half = HD // 2
+
+    barrier = pltpu.get_barrier_semaphore()
+    for _, where in others:
+        pl.semaphore_signal(barrier, 1, device_id=where, device_id_type=pl.DeviceIdType.MESH)
+    pl.semaphore_wait(barrier, 3)
+
+    def sent(index, head):
+        return pltpu.make_async_remote_copy(
+            staged.at[index, head],
+            come.at[index, head],
+            send_sem.at[index, head],
+            recv_sem.at[index, head],
+            device_id=others[index][1],
+            device_id_type=pl.DeviceIdType.MESH,
+        )
+
+    def starts(who):
+        return [who, pieces - 1 - who, pieces + who, 2 * pieces - 1 - who]
+
+    def through_norm(values, gain, cosine, sine, d_turned):
+        first, second = d_turned[:half], d_turned[half:]
+        d_scaled = jnp.concatenate([first * cosine + second * sine, second * cosine - first * sine], axis=0)
+        inverse = lax.rsqrt(jnp.mean(values * values, axis=0, keepdims=True) + EPSILON)
+        d_normed = d_scaled * gain
+        mean = jnp.mean(values * d_normed, axis=0, keepdims=True)
+        return inverse * d_normed - values * inverse**3 * mean, d_scaled * values * inverse
+
+    gain_sum[...] = jnp.zeros_like(gain_sum)
+    scale = 1.0 / math.sqrt(HD)
+
+    @pl.loop(0, KVH)
+    def _(head):
+        key_rows = pl.ds(pl.multiple_of(head * HD, HD), HD)
+        value_rows = pl.ds(pl.multiple_of(kv_rows + head * HD, HD), HD)
+        key_n[...] = pair[key_rows, :].T
+        value_n[...] = pair[value_rows, :].T
+        d_key[...] = jnp.zeros_like(d_key)
+        d_value[...] = jnp.zeros_like(d_value)
+        for index, start in enumerate(starts(member)):
+            cut = slice(index * span, (index + 1) * span)
+
+            def beside(ref):
+                return jnp.concatenate([ref[head * REP + rep, :, cut] for rep in range(REP)], axis=1)
+
+            query_here, d_out_here = beside(query), beside(d_out)
+            query_t, d_out_t = query_here.T, d_out_here.T
+            logs = jnp.concatenate([logs_ref[head, rep : rep + 1, cut] for rep in range(REP)], axis=1)
+            delta = jnp.concatenate([delta_ref[head, rep : rep + 1, cut] for rep in range(REP)], axis=1)
+            first_query = start * span
+            full, last = tiles_of(first_query)
+
+            def tile(where, accum, masked):
+                first_key = pl.multiple_of(where * KEYS, KEYS)
+                here = pl.ds(first_key, KEYS)
+                probs = jnp.exp(dot(key_n[here, :], query_here) - logs)
+                if masked:
+                    probs = jnp.where(allowed(first_query, first_key, span, rows), probs, 0.0)
+                d_probs = dot(value_n[here, :], d_out_here)
+                d_scores = (probs * (d_probs - delta)).astype(BF)
+                d_value[here, :] += dot(probs.astype(BF), d_out_t)
+                d_key[here, :] += dot(d_scores, query_t)
+                return accum + dot(pair[key_rows, here], d_scores)
+
+            accum = tile(last, jnp.zeros((HD, rows), F32), True)
+            accum = lax.fori_loop(0, full, lambda where, total: tile(where, total, False), accum)
+            cosine = jnp.concatenate([cos_ref[:, cut]] * REP, axis=1)
+            sine = jnp.concatenate([sin_ref[:, cut]] * REP, axis=1)
+            d_raw, part = through_norm(beside(raw), query_gain[...], cosine, sine, accum * scale)
+            gain_sum[0] += part
+            for rep in range(REP):
+                which = head * REP + rep
+                place = pl.ds(pl.multiple_of(which % KVH * HD, HD), HD)
+                d_project[which // KVH, place, cut] = d_raw[:, rep * span : (rep + 1) * span].astype(BF)
+        both_t[:HD, :] = d_key[...].T.astype(BF)
+        both_t[HD:, :] = d_value[...].T.astype(BF)
+        for index, who in enumerate([who for who, _ in others] + [member]):
+            for number, start in enumerate(starts(who)):
+                part = both_t[:, pl.ds(pl.multiple_of(start * span, span), span)]
+                staged[index, head, :, number * span : (number + 1) * span] = part
+            if index < 3:
+                sent(index, head).start()
+
+    cosine, sine = cos_ref[...], sin_ref[...]
+    width = kv_rows // 4
+    for head in range(KVH):
+        total = staged[3, head].astype(F32)
+        for index in range(3):
+            sent(index, head).wait_recv()
+            total += come[index, head].astype(F32)
+        values = key_raw[head * HD : (head + 1) * HD, :].astype(F32)
+        d_raw, part = through_norm(values, key_gain[...], cosine, sine, total[:HD])
+        gain_sum[1] += part
+        for offset, result in ((0, d_raw.astype(BF)), (width, total[HD:].astype(BF))):
+            first = head * HD
+            while first < (head + 1) * HD:
+                col, inside = first // width, first % width
+                size = min(width - inside, (head + 1) * HD - first)
+                place = d_project.shape[1] - 2 * width + offset + inside
+                d_project[col, place : place + size, :] = result[first - head * HD : first - head * HD + size]
+                first += size
+    query_gain_out[...] = jnp.sum(gain_sum[0], axis=1, keepdims=True)
+    key_gain_out[...] = jnp.sum(gain_sum[1], axis=1, keepdims=True)
+    for head in range(KVH):
+        for index in range(3):
+            sent(index, head).wait_send()
+
+
+def back(query, d_out, logs, delta, pair, raw, key_raw, cosine, sine, query_gain, key_gain):
+    mine = query.shape[2]
+    inside = pl.BlockSpec(memory_space=pltpu.VMEM)
+    dma = pltpu.SemaphoreType.DMA
+    shape = jax.ShapeDtypeStruct
+    columns = (QH + 2 * KVH) * HD // 4
+    return pl.pallas_call(
+        back_kernel,
+        out_shape=[shape((4, columns, mine), BF), shape((HD, 1), F32), shape((HD, 1), F32)],
+        in_specs=[inside] * 11,
+        out_specs=[inside] * 3,
+        scratch_shapes=[
+            pltpu.VMEM((GROUP, HD), BF),
+            pltpu.VMEM((GROUP, HD), BF),
+            pltpu.VMEM((GROUP, HD), F32),
+            pltpu.VMEM((GROUP, HD), F32),
+            pltpu.VMEM((2 * HD, GROUP), BF),
+            pltpu.VMEM((4, KVH, 2 * HD, mine), BF),
+            pltpu.VMEM((3, KVH, 2 * HD, mine), BF),
+            pltpu.VMEM((2, HD, mine), F32),
+            dma((3, KVH)),
+            dma((3, KVH)),
+        ],
+        compiler_params=pltpu.CompilerParams(
+            collective_id=4, has_side_effects=True, vmem_limit_bytes=48 * 1024 * 1024
+        ),
+        name="attend_back",
+    )(query, d_out, logs, delta, pair, raw, key_raw, cosine, sine, query_gain, key_gain)
+
+
 def body(
     tokens,
     norm1_gain,
@@ -1546,20 +1726,10 @@
         states = states.astype(F32)
         inverse_one, inverse_two = rms(states), rms(hidden)
         gain_one, gain_two = gains[:, 0].reshape(D), gains[:, 1].reshape(D)
-        key_sent = key_sent.reshape(KVH, HD, mine)
-        query_use = query_use.reshape(KVH, REP, HD, mine)
         mixed_f = mixed_f.reshape(KVH, REP, HD, mine)
-        pair = pair.reshape(2, KVH, HD, GROUP)
-        key_t, value_t = pair[0], pair[1]
         mixed = mixed_f.reshape(QH * HD, mine).astype(BF)
         w_project = w_project.reshape(cols, D, -1)
         ffn_weights = [w_gate, gate_other, w_up, up_other, w_down]
-        query_back = jax.vjp(
-            lambda raw, gain: prepare(raw, gain, cosine, sine), query_raw, query_gain
-        )[1]
-        key_back = jax.vjp(
-            lambda raw, gain: prepare(raw, gain, cosine, sine), key_sent.astype(F32), key_gain
-        )[1]
     else:
         states = to_members(tokens).astype(F32)
         gain_one = gather_rows(norm1_gain, 0)
@@ -1641,44 +1811,53 @@
     d_mixed = dot(w_out_all, d_hidden_low, ((1,), (1,))).astype(BF)
     d_mixed = d_mixed.reshape(KVH, REP, HD, mine)
     delta = jnp.sum(d_mixed.astype(F32) * mixed_f, axis=2)
-    d_query, d_key_n, d_value_n = attend_back(
-        first_tokens, query_use, d_mixed, logs, delta, key_t, value_t
-    )
-    d_pair = dealt(jnp.stack([d_key_n, d_value_n])).astype(BF)
-    d_pair = lax.psum_scatter(d_pair, ("row", "side"), scatter_dimension=0, tiled=True)[0]
-    d_pair = d_pair.astype(F32).transpose(0, 1, 3, 2)
-    d_query_raw, query_gain_part = query_back(d_query.reshape(QH, HD, mine) * scale)
-    d_key_raw, key_gain_part = key_back(d_pair[0])
-    d_projected = jnp.concatenate(
-        [
-            d_query_raw.reshape(cols, q_width, mine),
-            d_key_raw.reshape(cols, k_width, mine),
-            d_pair[1].reshape(cols, k_width, mine),
-        ],
-        axis=1,
-    ).astype(BF)
+    if fast:
+        d_projected, query_gain_part, key_gain_part = back(
+            query_use, d_mixed.reshape(QH, HD, mine), logs, delta, pair, query_raw, key_sent,
+            cosine, sine, query_gain[:, None], key_gain[:, None],
+        )
+        query_gain_part, key_gain_part = query_gain_part[:, 0], key_gain_part[:, 0]
+    else:
+        d_query, d_key_n, d_value_n = attend_back(
+            first_tokens, query_use, d_mixed, logs, delta, key_t, value_t
+        )
+        d_pair = dealt(jnp.stack([d_key_n, d_value_n])).astype(BF)
+        d_pair = lax.psum_scatter(d_pair, ("row", "side"), scatter_dimension=0, tiled=True)[0]
+        d_pair = d_pair.astype(F32).transpose(0, 1, 3, 2)
+        d_query_raw, query_gain_part = query_back(d_query.reshape(QH, HD, mine) * scale)
+        d_key_raw, key_gain_part = key_back(d_pair[0])
+        d_projected = jnp.concatenate(
+            [
+                d_query_raw.reshape(cols, q_width, mine),
+                d_key_raw.reshape(cols, k_width, mine),
+                d_pair[1].reshape(cols, k_width, mine),
+            ],
+            axis=1,
+        ).astype(BF)
     d_normed_one = dot(d_projected, w_project, ((0, 1), (0, 2)))
     grad_input = d_hidden + norm_back(states, inverse_one, gain_one, d_normed_one)
     norm_one_part = jnp.sum(d_normed_one * states * inverse_one, axis=0)
-    grad_input = from_members(grad_input)
 
     grad_project = lax.dot_general(
         d_projected, normed_one, (((2,), (0,)), ((), ())), preferred_element_type=F32
     )
-    grad_project = grad_project.astype(BF).transpose(0, 2, 1)
+    grad_project = grad_project.astype(BF)
     grad_out = grad_out.reshape(cols, q_width, D)
     norm_one_part = jnp.roll(norm_one_part.reshape(rows, width), row_index, 0).reshape(D)
     norm_two_part = jnp.roll(norm_two_part.reshape(rows, width), row_index, 0).reshape(D)
     small = jnp.concatenate([norm_one_part, norm_two_part, query_gain_part, key_gain_part])
-    if rows == 2 and cols == 4 and lax.axis_size("dp") == 4:
+    if fast and lax.axis_size("dp") == 4:
         padded = jnp.pad(small, (0, SMALL * 128 - small.shape[0])).reshape(SMALL, 128)
-        grad_down, grad_gate_up, grad_out, grad_project, small = reduce_all(
+        grad_down, grad_gate_up, grad_out, grad_project, small, grad_input = reduce_all(
             4,
-            [(grad_down, 1, 128), (grad_gate_up, 0, 64), (grad_out, 1, 160), (grad_project, 0, 512)],
+            [(grad_down, 1, 128), (grad_gate_up, 0, 64), (grad_out, 1, 160), (grad_project, 1, 240)],
             padded,
-        )
+            grad_input.astype(BF),
+        )
+        grad_input = grad_input.astype(F32)
         small = small.reshape(-1)[: 2 * D + 2 * HD]
     else:
+        grad_input = from_members(grad_input)
         small = lax.psum(small, ("dp", "row", "group", "side"))
         col_axes = ("group", "side")
         grad_project = lax.psum_scatter(grad_project, col_axes, scatter_dimension=0, tiled=True)
@@ -1686,10 +1865,10 @@
         grad_down = sum_planes(scatter_rows(grad_down, 1), 2)
         grad_gate_up = sum_planes(scatter_rows(grad_gate_up, 0), 4)
         grad_out = sum_planes(scatter_rows(grad_out[0], 1), 1)
-        grad_project = sum_planes(scatter_rows(grad_project[0], 0), 2)
+        grad_project = sum_planes(scatter_rows(grad_project[0], 1), 2)
     grad_norm1 = lax.dynamic_slice_in_dim(small, row_index * width, width, 0)
     grad_norm2 = lax.dynamic_slice_in_dim(small, D + row_index * width, width, 0)
-    grad_project = grad_project.astype(F32)
+    grad_project = grad_project.astype(F32).T
     return (
         block_out,
         grad_input,

time: 915 us -> 808 us (0.88)
  local copies, waits for them, and re-layouts: 70.1 us -> 14 us
  other arithmetic: 55.8 us -> 39 us
  between operations: 15.9 us -> 2.09 us
    convert_element_type x3 -> x0, local copies, waits for them, and re-layouts: 20.6 us -> none  [the longest x1 11.3 us: body(): grad_project = grad_project.astype(BF).transpose(0, 2, 1)]
    pallas_call x1, Pallas kernels: 272 us -> 253 us  [reduce_all(): pl.pallas_call(functools.partial(reduce_kernel, parts, planes), out_shape...]
    pallas_call x1, Pallas kernels: 38.9 us -> 52 us  [back(): pl.pallas_call(back_kernel, out_shape=[shape((4, columns, mine), BF), sha...]
    unnamed x75 -> x76, local copies, waits for them, and re-layouts: 16.6 us -> 6.44 us
    reshape x2 -> x0, local copies, waits for them, and re-layouts: 10.1 us -> none  [from_members(): parts = block.reshape(cores, 2, span, rows, width).transpose(3, 0, 1, 2, 4)]
  transfers between devices with their start and end apart: 2 -> 0, of which waited for: 0 -> 0; matrix products, arithmetic and copies ran while one was open for 11% -> 0% of each run, Pallas kernels for 30% -> 0%
where the time goes in v5:
time: 808 us; the launch traced here: 799 us
  Pallas kernels  677 us (84%)
  matrix products  66.4 us (8%)
  other arithmetic  39 us (5%)
  local copies, waits for them, and re-layouts  14 us (2%)
    pallas_call x1, Pallas kernels, reduce_all(): pl.pallas_call(functools.partial(reduce_kernel, parts, planes), out_shape...  253 us
    pallas_call x2, Pallas kernels, spread(): pl.pallas_call(functools.partial(spread_kernel, forward, dealt is not Non...  222 us
    pallas_call x1, Pallas kernels, front(): pl.pallas_call(front_kernel, out_shape=[shape((mine, depth), BF), shape((...  150 us
    dot_general x5, matrix products, dot(): lax.dot_general(left, right, (dims, ((), ())), preferred_element_type=F32)  58.3 us
    pallas_call x1, Pallas kernels, back(): pl.pallas_call(back_kernel, out_shape=[shape((4, columns, mine), BF), sha...  52 us

profile of v5, /device:TPU:0, one launch (start us, length us, event | category | flops | bytes accessed | tf_op | source)
XLA Modules:
  0.0 798.8 jit_solution(14081278556337609414)
XLA Ops:
  2.5 1.4 copy.51.refs_8_.refs_9_
  3.8 1.4 copy.52.refs_9_.refs_10_
  5.2 1.4 copy.48
  8.8 1.3 pad_maximum_fusion.refs_1_
  10.7 150.3 %front.1 = (bf16[512,2048]{1,0:T(8,128)(2,1)}, bf16[512,2048]{1,0:T(8,128)(2,1)}, f32[20,64,512]{2,1,0:T(8,128)}, bf16[20,64,512]{2,1,0:T(8,128)(2,1)}, bf16[320...) custom-call(bf16[1024,1024]{1,0:T(8,128)(2,1)} %refs_0_.1, ...), custom_call_target="tpu_custom_call" | custom-call | tf_op jit(solution)/shard_map/front/pallas_call | solution.py:1408
  161.1 118.1 %feed_forward.1 = (bf16[8,256,2048]{2,1,0:T(8,128)(2,1)}, bf16[8,256,1280]{2,1,0:T(8,128)(2,1)}, bf16[8,256,1280]{2,1,0:T(8,128)(2,1)}, bf16[8,256,1280]{2,1,0:T...) custom-call(bf16[512,2048]{1,0:T(8,128)(2,1)} %get-tuple-element.50.refs_0_, ...), custom_call_target="tpu_custom_call" | custom-call | tf_op jit(solution)/shard_map/feed_forward/pallas_call | solution.py:1014
  279.9 7.8 fusion.16
  287.6 103.8 %feed_forward_back.1 = (bf16[8,256,2048]{2,1,0:T(8,128)(2,1)}, bf16[8,256,2560]{2,1,0:T(8,128)(2,1)}, f32[2,256,2048]{2,1,0:T(8,128)}, bf16[1024,1024]{1,0:T(8,128)(2,1)}) custom-call(bf16[512,2048]{1,0:T(8,128)(2,1)} %get-tuple-element.89.refs_0_, bf16[1024,1280]{1,0:T(8,128)(2,1)} %refs_1_.3, bf16[1024,1280]{1,0:T(8,128)(2,1)} %get-tuple-element.51.refs_2_, ...), custom_call_target="tpu_custom_call" | custom-call | tf_op jit(solution)/shard_map/feed_forward_back/pallas_call | solution.py:1014
  391.6 5.1 fusion.13
  398.1 3.7 fusion.10
  401.9 4.5 convert_multiply_fusion.4
  406.4 2.1 reduce_sum.65.refs_3_
  408.6 52.0 %attend_back.1 = (bf16[4,480,512]{2,1,0:T(8,128)(2,1)S(1)}, f32[64,1]{1,0:T(8,128)S(1)}, f32[64,1]{1,0:T(8,128)S(1)}) custom-call(bf16[20,64,512]{2,1,0:T(8,128)(2,1)S(1)} %copy-done, bf16[20,64,512]{2,1,0:T(8,128)(2,1)S(1)} %bitcast.76, f32[5,4,512]{2,1,0:T(4,128)S(1)} %copy-done.6, f32[5,4,512]{2,1,0:T(4,128)S(1)} %reduce_sum.65.refs_3_, ...), custom_call_target="tpu_custom_call" | custom-call | tf_op jit(solution)/shard_map/attend_back/pallas_call | solution.py:1585
  460.6 8.5 %fusion.8 = (f32[512]{0:T(512)S(1)}, f32[2048]{0:T(1024)S(1)}, f32[512,2048,1]{1,0,2:T(8,128)S(1)}) fusion(bf16[512,2048]{1,0:T(8,128)(2,1)S(1)} %copy-done.16, f32[2048]{0:T(1024)S(1)} %bitcast.83, f32[512]{0:T(512)S(1)} %get-tuple-element.106, bf16[4,480,512]{2,1,0:T(8,128)(2,1)S(1)} %get-tuple-element.72, bf16[4,2048,480]{2,1,0:T(8,128)(2,1)} %bitcast.95), kind=kOutput, calls=%fused_computation.16 | convolution fusion | flops 4033869312 | bytes 16142336 | tf_op jit(solution)/shard_map/dot_general | solution.py:29
  469.2 2.6 fusion.6.refs_5_
  472.8 8.1 %convolution_convert_fusion.1.refs_3_ = bf16[4,480,2048]{2,1,0:T(8,128)(2,1)} fusion(bf16[4,480,512]{2,1,0:T(8,128)(2,1)S(1)} %copy-done.8, bf16[512,2048]{1,0:T(8,128)(2,1)} %get-tuple-element.73), kind=kOutput, calls=%fused_computation.7 | convolution fusion | flops 4030464000 | bytes 11927552 | tf_op jit(solution)/shard_map/dot_general | solution.py:1841
  480.9 4.8 convolution_convert_fusion
  485.7 25.9 %bitcast_convert_fusion.refs_1_ = bf16[2048,2560]{1,0:T(8,128)(2,1)} fusion(bf16[8,256,2048]{2,1,0:T(8,128)(2,1)} %get-tuple-element.61, bf16[8,256,2560]{2,1,0:T(8,128)(2,1)S(1)} %bitcast.92), kind=kOutput, calls=%fused_computation | convolution fusion | flops 21480079360 | bytes 29360128 | tf_op jit(solution)/shard_map/dot_general | solution.py:29
  511.7 14.6 %bitcast_convert_fusion.1.refs_0_ = bf16[1280,2048]{1,0:T(8,128)(2,1)} fusion(bf16[8,256,1280]{2,1,0:T(8,128)(2,1)} %get-tuple-element.59, bf16[8,256,2048]{2,1,0:T(8,128)(2,1)S(1)} %bitcast.94), kind=kOutput, calls=%fused_computation.1 | convolution fusion | flops 10740039680 | bytes 18874368 | tf_op jit(solution)/shard_map/dot_general | solution.py:29
  526.2 253.2 %reduce_grads.1 = (bf16[1280,1024]{1,0:T(8,128)(2,1)}, bf16[1024,2560]{1,0:T(8,128)(2,1)}, bf16[320,1024]{1,0:T(8,128)(2,1)}, bf16[480,1024]{1,0:T(8,128)(2,1)},...) custom-call(bf16[1280,2048]{1,0:T(8,128)(2,1)} %bitcast_convert_fusion.1.refs_0_, ...), custom_call_target="tpu_custom_call" | custom-call | tf_op jit(solution)/shard_map/reduce_grads/pallas_call | solution.py:550
  779.4 7.6 slice_convert_fusion
  787.0 3.0 convert_element_type.92
  790.0 2.5 convert_element_type.88
  797.2 1.3 copy.69
  (102 shorter events, 11.8 us)
Async XLA Ops:
  0.6 9.5 %copy-start.25 = (f32[1024]{0:T(1024)S(1)}, f32[1024]{0:T(1024)}, u32[]{:S(2)}) copy-start(f32[1024]{0:T(1024)} %param.18) | copy-start | bytes 12292
  0.7 9.5 %copy-start.24 = (f32[1024]{0:T(1024)S(1)}, f32[1024]{0:T(1024)}, u32[]{:S(2)}) copy-start(f32[1024]{0:T(1024)} %param.25) | copy-start | bytes 12292
  287.6 103.9 %copy-start.23 = (f32[2,2,1024]{2,1,0:T(2,128)S(1)}, f32[2,2,1024]{2,1,0:T(2,128)}, u32[]{:S(2)}) copy-start(f32[2,2,1024]{2,1,0:T(2,128)} %get-tuple-element.64) | copy-start | bytes 49156
  287.6 103.9 %copy-start.15 = (bf16[512,2048]{1,0:T(8,128)(2,1)S(1)}, bf16[512,2048]{1,0:T(8,128)(2,1)}, u32[]{:S(2)}) copy-start(bf16[512,2048]{1,0:T(8,128)(2,1)} %get-tuple-element.75) | copy-start | bytes 6291460
  391.5 5.9 copy-start.10
  391.5 6.5 copy-start.14
  391.6 10.2 %slice-start.5 = ((s8[5242880]{0:T(1024)(128)(4,1)}), s8[4194304]{0:T(1024)(128)(4,1)S(1)}, s32[]{:S(2)}) async-start(s8[5242880]{0:T(1024)(128)(4,1)} %bitcast.96), calls=%async_computation.5 | async-start | bytes 8388608
  401.8 6.7 copy-start
  401.8 6.7 copy-start.1
  401.8 6.7 copy-start.2
  401.8 6.7 copy-start.3
  401.9 6.7 copy-start.4
  401.9 6.7 copy-start.5
  401.9 6.7 copy-start.6
  408.6 52.0 %copy-start.16 = (bf16[512,2048]{1,0:T(8,128)(2,1)S(1)}, bf16[512,2048]{1,0:T(8,128)(2,1)}, u32[]{:S(2)}) copy-start(bf16[512,2048]{1,0:T(8,128)(2,1)} %get-tuple-element.75) | copy-start | bytes 6291460
  460.6 8.6 %copy-start.7 = (bf16[4,480,512]{2,1,0:T(8,128)(2,1)}, bf16[4,480,512]{2,1,0:T(8,128)(2,1)S(1)}, u32[]{:S(2)}) copy-start(bf16[4,480,512]{2,1,0:T(8,128)(2,1)S(1)} %get-tuple-element.72) | copy-start | bytes 5898244
  460.6 8.6 %copy-start.12 = (f32[512,2048]{1,0:T(8,128)S(1)}, f32[512,2048]{1,0:T(8,128)}, u32[]{:S(2)}) copy-start(f32[512,2048]{1,0:T(8,128)} %copy-done.11) | copy-start | bytes 12582916
  472.8 8.2 %copy-start.13 = (f32[512,2048]{1,0:T(8,128)S(1)}, f32[512,2048]{1,0:T(8,128)}, u32[]{:S(2)}) copy-start(f32[512,2048]{1,0:T(8,128)} %copy-done.11) | copy-start | bytes 12582916
  472.8 8.2 %copy-start.27 = (f32[1280,512]{1,0:T(8,128)S(1)}, f32[1280,512]{1,0:T(8,128)}, u32[]{:S(2)}) copy-start(f32[1280,512]{1,0:T(8,128)} %get-tuple-element.63) | copy-start | bytes 7864324
  472.8 12.9 %slice-start = ((s8[10485760]{0:T(1024)(128)(4,1)}), s8[4194304]{0:T(1024)(128)(4,1)S(1)}, s32[]{:S(2)}) async-start(s8[10485760]{0:T(1024)(128)(4,1)} %bitcast.91), calls=%async_computation | async-start | bytes 8388608
  472.8 12.9 %slice-start.1 = ((s8[10485760]{0:T(1024)(128)(4,1)}), s8[4194304]{0:T(1024)(128)(4,1)S(1)}, s32[]{:S(2)}) async-start(s8[10485760]{0:T(1024)(128)(4,1)} %bitcast.91), calls=%async_computation.1 | async-start | bytes 8388608
  480.9 30.7 %slice-start.3 = ((s8[8388608]{0:T(1024)(128)(4,1)}), s8[4194304]{0:T(1024)(128)(4,1)S(1)}, s32[]{:S(2)}) async-start(s8[8388608]{0:T(1024)(128)(4,1)} %bitcast.93), calls=%async_computation.3 | async-start | bytes 8388608
  485.7 25.9 %slice-start.4 = ((s8[8388608]{0:T(1024)(128)(4,1)}), s8[4194304]{0:T(1024)(128)(4,1)S(1)}, s32[]{:S(2)}) async-start(s8[8388608]{0:T(1024)(128)(4,1)} %bitcast.93), calls=%async_computation.4 | async-start | bytes 8388608
  779.4 7.6 copy-start.17
  (11 other events, 41.6 us)

commit v6 on v5

--- a/solution.py
+++ b/solution.py
@@ -231,15 +231,19 @@
         del refs[:number]
         return taken
 
-    grads = take(count)
+    col_parts = [j for j in range(count) if parts[j].col]
+    normed_ref, d_gate_up_ref, act_ref, d_low_ref = take(4)
+    grads = dict(zip(col_parts, take(len(col_parts))))
     (small_ref, mine_ref) = take(2)
     outs = take(count)
     (small_out, dealt_ref) = take(2)
-    near, far, wide, own = take(count), take(count), take(count), take(count)
-    col_parts = [j for j in range(count) if parts[j].col]
+    near, far, own = take(count), take(count), take(count)
+    made = [j for j in range(count) if not parts[j].col]
+    leaving = dict(zip(made, take(len(made))))
     mate_in = dict(zip(col_parts, take(len(col_parts))))
     far_in = dict(zip(col_parts, take(len(col_parts))))
-    own_sem, out_sem, row_send, row_recv, in_send, far_recv, mid_send, wide_recv = take(8)
+    right, left, left_t, right_sem, left_sem, free_sem = take(6)
+    out_sem, row_send, row_recv, in_send, far_recv, mid_send, wide_recv = take(7)
     col_own, col_send, col_recv, x_send, x_recv, small_local, small_send, small_recv = take(8)
     small_in, small_sum, deal_send, deal_recv, deal_local = take(5)
     plane, row = lax.axis_index("dp"), lax.axis_index("row")
@@ -318,9 +322,97 @@
         x_copy(j, half, index).wait_recv()
         far_in[j][half, index] = far_in[j][half, index] + mate_in[j][group, half, index]
 
+    half_depth = normed_ref.shape[1] // 2
+    gate_up, down = made
+    units = parts[gate_up].count // 2
+
+    def left_copies(unit, of_down):
+        if of_down:
+            source = act_ref.at[:, pl.ds(pl.multiple_of(unit * 256, 256), 256)]
+            slot = (units + unit) % 2
+            return [pltpu.make_async_copy(source, left.at[slot], left_sem.at[slot, 0])]
+        slot = unit % 2
+        copies = []
+        for half in range(2):
+            first = pl.multiple_of(half * half_depth + unit * 128, 128)
+            target = left.at[slot, :, pl.ds(half * 128, 128)]
+            copies.append(
+                pltpu.make_async_copy(normed_ref.at[:, pl.ds(first, 128)], target, left_sem.at[slot, half])
+            )
+        return copies
+
+    d_low_load = pltpu.make_async_copy(d_low_ref, right.at[:, pl.ds(0, d_low_ref.shape[1])], right_sem.at[1])
+    d_gate_up_load = pltpu.make_async_copy(d_gate_up_ref, right, right_sem.at[0])
+
+    def start_unit(j, unit):
+        of_down = j == down
+        part = parts[j]
+        for copy in left_copies(unit, of_down):
+            copy.wait()
+
+        @pl.when(unit + 1 < part.count // 2)
+        def _():
+            for copy in left_copies(unit + 1, of_down):
+                copy.start()
+
+        if not of_down:
+            @pl.when(unit + 1 == units)
+            def _():
+                for copy in left_copies(0, True):
+                    copy.start()
+
+        @pl.when(unit == 0)
+        def _():
+            (d_low_load if of_down else d_gate_up_load).wait()
+
+        for chunk in range(2):
+            index = 2 * unit + chunk
+
+            @pl.when(index >= SLOTS)
+            def _(index=index):
+                row_copy(j, jnp.maximum(index - SLOTS, 0)).wait_send()
+
+        slot = ((units + unit) if of_down else unit) % 2
+
+        @pl.loop(0, left.shape[1] // 256)
+        def _(block):
+            here = pl.ds(pl.multiple_of(block * 256, 256), 256)
+            left_t[:, here] = left[slot, here, :].T
+
+    def tile(j, unit, number, targets):
+        rows = parts[j].rows
+        where = pl.ds(pl.multiple_of(number * 256, 256), 256)
+        product = dot(left_t[...], right[:, where]).astype(BF)
+        for place, (target, chunk, first_tile) in enumerate(targets):
+            to = pl.ds(pl.multiple_of((number - first_tile) * 256, 256), 256)
+            target[j][(2 * unit + chunk) % SLOTS, :, to] = product[place * rows : (place + 1) * rows]
+
+    def make(j, unit, second):
+        part = parts[j]
+        if not second:
+            start_unit(j, unit)
+        if j == down:
+            tiles = part.cols // 256
+            first, target = (0, own) if second else (tiles, leaving)
+            targets = [(target, 0, first), (target, 1, first)]
+            pl.loop(first, first + tiles)(lambda number: tile(j, unit, number, targets))
+        else:
+            tiles = part.cols // 256
+            targets = [(own, 0, 0), (own, 1, 0), (leaving, 0, 0), (leaving, 1, 0)]
+            bounds = (tiles // 2, tiles) if second else (0, tiles // 2)
+            pl.loop(*bounds)(lambda number: tile(j, unit, number, targets))
+        if second and j != down:
+            @pl.when(unit + 1 == units)
+            def _():
+                d_low_load.start()
+
+        if second != (j == down):
+            for chunk in range(2):
+                row_copy(j, 2 * unit + chunk).start()
+
     def row_copy(j, index):
         slot = parts[j].base + index
-        source = far_in[j].at[1, index] if parts[j].col else parts[j].cut(grads[j], index, 1)
+        source = far_in[j].at[1, index] if parts[j].col else leaving[j].at[index % SLOTS]
         return remote(source, near[j].at[index], row_send.at[slot], row_recv.at[slot], other_row)
 
     def in_copy(j, index):
@@ -329,22 +421,16 @@
 
     def mid_copy(j, index):
         slot = parts[j].base + index
-        return remote(far[j].at[index], wide[j].at[index], mid_send.at[slot], wide_recv.at[slot], mid_other)
+        return remote(far[j].at[index], near[j].at[index], mid_send.at[slot], wide_recv.at[slot], mid_other)
 
     def back_copy(j, index):
         slot = parts[j].base + index
-        return remote(wide[j].at[index], far[j].at[index], in_send.at[slot], far_recv.at[slot], mid_outer)
+        return remote(near[j].at[index], far[j].at[index], in_send.at[slot], far_recv.at[slot], mid_outer)
 
     def out_copy(j, index, source):
         slot = parts[j].base + index
         return pltpu.make_async_copy(source[j].at[index], parts[j].cut(outs[j], index, 0), out_sem.at[slot])
 
-    def own_copy(j, index):
-        slot = parts[j].base + index
-        return pltpu.make_async_copy(
-            parts[j].cut(grads[j], index, 0), own[j].at[index % SLOTS], own_sem.at[slot]
-        )
-
     def each(step, action):
         for j, part in enumerate(parts):
             index = step - part.base
@@ -354,17 +440,20 @@
                 action(j, index)
 
     def send_row(j, index):
-        if not parts[j].col:
-            own_copy(j, index).start()
-        row_copy(j, index).start()
+        if parts[j].col:
+            row_copy(j, index).start()
+        else:
+            @pl.when(index % 2 == 0)
+            def _():
+                make(j, index // 2, False)
+
+            @pl.when(index % 2 == 1)
+            def _():
+                make(j, index // 2, True)
 
     def take_row(j, index):
         row_copy(j, index).wait_recv()
-        if parts[j].col:
-            mine = far_in[j][0, index]
-        else:
-            own_copy(j, index).wait()
-            mine = own[j][index % SLOTS]
+        mine = far_in[j][0, index] if parts[j].col else own[j][index % SLOTS]
         near[j][index] = near[j][index] + mine
 
         @pl.when(at_end)
@@ -374,28 +463,35 @@
     def take_far(j, index):
         back_copy(j, index).wait_recv()
         far[j][index] = far[j][index] + near[j][index]
+        pl.semaphore_signal(free_sem, 1, device_id=mid_other, device_id_type=pl.DeviceIdType.MESH)
+        pl.semaphore_wait(free_sem, 1)
         mid_copy(j, index).start()
 
     def take_wide(j, index):
         mid_copy(j, index).wait_recv()
-        wide[j][index] = wide[j][index] + far[j][index]
+        near[j][index] = near[j][index] + far[j][index]
         back_copy(j, index).start()
-        out_copy(j, index, wide).start()
+        out_copy(j, index, near).start()
 
     def take_back(j, index):
         in_copy(j, index).wait_recv()
         out_copy(j, index, far).start()
 
+    def row_sent(j, index):
+        @pl.when(jnp.logical_or(parts[j].col, index >= parts[j].count - SLOTS))
+        def _():
+            row_copy(j, index).wait_send()
+
     def finish_end(j, index):
-        row_copy(j, index).wait_send()
+        row_sent(j, index)
         in_copy(j, index).wait_send()
         out_copy(j, index, far).wait()
 
     def finish_mid(j, index):
-        row_copy(j, index).wait_send()
+        row_sent(j, index)
         mid_copy(j, index).wait_send()
         back_copy(j, index).wait_send()
-        out_copy(j, index, wide).wait()
+        out_copy(j, index, near).wait()
 
     def small_copy(stage, source, where):
         return remote(small_sum.at[source], small_in.at[stage], small_send.at[stage], small_recv.at[stage], where)
@@ -424,6 +520,9 @@
                 dealt.append(remote(source, target, deal_send.at[index, high], deal_recv.at[index, high], where))
 
     total = sum(part.count for part in parts)
+    for copy in left_copies(0, False):
+        copy.start()
+    d_gate_up_load.start()
     small_load.start()
     for copy in dealt[4:]:
         copy.start()
@@ -532,21 +631,24 @@
             each(step, finish_mid)
 
 
-def reduce_all(planes, grads, small, mine):
-    parts, base = [], 0
-    for grad, axis, rows in grads:
-        height, width = grad.shape[-2:]
-        height, width = (height // 2, width) if axis == 0 else (height, width // 2)
-        parts.append(Part(axis, rows, width, height // rows, base, grad.ndim == 3))
-        base += height // rows
+def reduce_all(planes, normed, d_gate_up, act, d_low, grad_out, grad_project, small, mine):
+    depth, width = normed.shape[1], act.shape[1]
+    parts = [Part(0, 64, d_gate_up.shape[1], depth // 128, 0, False)]
+    for rows, height, col in ((grad_out.shape[1] // 2, grad_out.shape[1], True),
+                              (grad_project.shape[1] // 2, grad_project.shape[1], True), (128, width, False)):
+        parts.append(Part(1, rows, depth // 2, height // rows, parts[-1].base + parts[-1].count, col))
+    base = parts[-1].base + parts[-1].count
     shapes = [(part.count, part.rows, part.cols) for part in parts]
     col_shapes = [(2, *shape) for part, shape in zip(parts, shapes) if part.col]
+    made_shapes = [(SLOTS, *shape[1:]) for part, shape in zip(parts, shapes) if not part.col]
     pieces = sum(shape[1] * 2 for shape in col_shapes)
     own_shapes = [
         (2, 2, *shape) if part.col else (SLOTS, *shape[1:]) for part, shape in zip(parts, shapes)
     ]
     anywhere = pl.BlockSpec(memory_space=pl.ANY)
     dma = pltpu.SemaphoreType.DMA
+    tokens = normed.shape[0]
+    inputs = (normed, d_gate_up, act, d_low, grad_out, grad_project, small, mine)
     return pl.pallas_call(
         functools.partial(reduce_kernel, parts, planes),
         out_shape=[jax.ShapeDtypeStruct((n * r, c), BF) for n, r, c in shapes]
@@ -554,13 +656,21 @@
             jax.ShapeDtypeStruct(small.shape, F32),
             jax.ShapeDtypeStruct((2 * mine.shape[0], mine.shape[1] // 2), BF),
         ],
-        in_specs=[anywhere] * (len(parts) + 2),
+        in_specs=[anywhere] * len(inputs),
         out_specs=[anywhere] * (len(parts) + 2),
-        scratch_shapes=[pltpu.VMEM(shape, BF) for _ in range(3) for shape in shapes]
-        + [pltpu.VMEM(shape, BF) for shape in own_shapes]
+        scratch_shapes=[pltpu.VMEM(shape, BF) for _ in range(2) for shape in shapes]
+        + [pltpu.VMEM(shape, BF) for shape in own_shapes + made_shapes]
         + [pltpu.VMEM((2, *shape), BF) for shape in col_shapes]
         + [pltpu.VMEM(shape, BF) for shape in col_shapes]
-        + [dma((base,)) for _ in range(8)]
+        + [
+            pltpu.VMEM((tokens, d_gate_up.shape[1]), BF),
+            pltpu.VMEM((2, tokens, 256), BF),
+            pltpu.VMEM((256, tokens), BF),
+            dma((2,)),
+            dma((2, 2)),
+            pltpu.SemaphoreType.REGULAR,
+        ]
+        + [dma((base,)) for _ in range(7)]
         + [dma((2, pieces)), dma((2, pieces)), dma((2, pieces)), dma((pieces,)), dma((pieces,))]
         + [dma((2,)), dma((5,)), dma((5,))]
         + [pltpu.VMEM((5, *small.shape), F32), pltpu.VMEM((6, *small.shape), F32)]
@@ -569,7 +679,7 @@
             collective_id=0, has_side_effects=True, vmem_limit_bytes=60 * 1024 * 1024
         ),
         name="reduce_grads",
-    )(*[grad for grad, _, _ in grads], small, mine)
+    )(*inputs)
 
 
 TILE = 256
@@ -844,7 +954,8 @@
         far_sum[index] = total.astype(BF)
         back_copy(index).start()
 
-    if forward and fast:
+    split = forward and fast
+    if split:
         down_saved = pltpu.make_async_copy(w_down.at[:, pl.ds(half, half)], down_out, weight_sem.at[5])
     for copy in fetches(0):
         copy.start()
@@ -889,32 +1000,39 @@
         def _():
             second_loads()
 
-        if forward and fast:
-            @pl.when(step < 4)
+        if split:
+            @pl.when(step < 6)
             def _():
                 second_half(step, 0, half // TILE)
 
             for index in range(4):
-                @pl.when(step == min(index + 1, 3))
+                @pl.when(step == index + 1)
                 def _(index=index):
                     down_chunks[index][0].wait_recv()
                     down_chunks[index][1].start()
 
-            @pl.when(step == 3)
+            @pl.when(step == 5)
             def _():
                 for _, over_planes in down_chunks:
                     over_planes.wait_recv()
                 down_saved.start()
-
-                @pl.loop(0, 4)
-                def _(early):
-                    second_half(early, half // TILE)
-
-                sum_copy(0).start()
-
-            @pl.when(step >= 4)
+                pl.loop(4, 6)(lambda early: second_half(early, half // TILE))
+                part_copy(0).start()
+                part_copy(1).start()
+
+            @pl.when(step >= 6)
             def _():
                 second_half(step)
+                part_copy(jnp.maximum(step - 4, 0)).start()
+
+            @pl.when(step == 6)
+            def _():
+                finish_far(0)
+                finish_far(1)
+
+            @pl.when(step == 7)
+            def _():
+                finish_far(2)
         else:
             second_half(step)
         for copy in saves(step):
@@ -924,19 +1042,26 @@
         def _():
             x_copy(2 + step // 2).start()
 
-        @pl.when((step == 3) if forward and fast else ((step >= 2) & (step < 4)))
-        def _():
-            sum_copy(jnp.clip(step - 2, 0, 1)).start()
-
-        @pl.when(step >= 4)
-        def _():
-            part_copy(jnp.maximum(step - 4, 0)).start()
-
-        @pl.when(step >= 5)
-        def _():
-            finish_far(jnp.maximum(step - 5, 0))
-
+        if not split:
+            @pl.when((step >= 2) & (step < 4))
+            def _():
+                sum_copy(jnp.clip(step - 2, 0, 1)).start()
+
+            @pl.when(step >= 4)
+            def _():
+                part_copy(jnp.maximum(step - 4, 0)).start()
+
+            @pl.when(step >= 5)
+            def _():
+                finish_far(jnp.maximum(step - 5, 0))
+
+    if split:
+        pl.loop(2, 4)(lambda early: second_half(early, half // TILE))
+        sum_copy(0).start()
+        sum_copy(1).start()
     finish_far(3)
+    if split:
+        pl.loop(0, 2)(lambda early: second_half(early, half // TILE))
     for index in range(2):
         sum_copy(index).wait_recv()
         kept[index] = kept[index] + from_mate[index].astype(F32)
@@ -1209,7 +1334,6 @@
     project.first()
     for copy in sent_tokens:
         copy.start()
-    output.first()
     chunks[0][0].start()
     for copy in own_copies:
         copy.wait()
@@ -1255,6 +1379,7 @@
 
     project.plane_in()
     project.far_in(0)
+    output.to_row.start()
     project_col(me)
     project.mate_in(0, 3)
     project_col(2 * group + 1 - side)
@@ -1292,9 +1417,9 @@
         passed.append(remote(place, place, pair_send.at[2, index], pair_recv.at[2, index], mate))
     for copy in to_row + to_mate:
         copy.start()
+    output.to_far[0].start()
+    output.to_mate[0].start()
     chunks[1][0].start()
-    output.row_in()
-    output.far_in(0)
 
     @pl.loop(0, raw.shape[0])
     def _(head):
@@ -1304,15 +1429,15 @@
     for index in range(4):
         to_row[index].wait_recv()
         passed[index].start()
+    output.row_in()
     chunks[2][0].start()
-    output.plane_in()
     pass_on(0)
     for index in range(4):
         to_mate[index].wait_recv()
         passed[index].wait_recv()
     chunks[3][0].start()
-    output.far_in(1)
-    output.far_in(2)
+    output.plane_in()
+    output.far_in(0)
 
     firsts = [member, pieces - 1 - member, pieces + member, 2 * pieces - 1 - member]
     rows = REP * span
@@ -1345,6 +1470,11 @@
                 part = slice(rep * span, (rep + 1) * span)
                 mixed_t[pl.ds(pl.multiple_of((head * REP + rep) * HD, HD), HD), cut] = result[:, part]
                 logs[head, rep : rep + 1, cut] = log[:, part]
+
+        @pl.when(head == 2)
+        def _():
+            output.far_in(1)
+            output.far_in(2)
 
         for number, index in ((1, 1), (3, 2)):
             @pl.when(head == number)
@@ -1801,8 +1931,7 @@
         block_out = from_members(result.astype(BF))
     d_normed = d_normed.reshape(mine, D)
     d_low, normed_all = d_low.reshape(-1, D), normed_all.reshape(-1, D)
-    grad_down = dot(activated.reshape(-1, ff), d_low, ((0,), (0,))).astype(BF)
-    grad_gate_up = dot(normed_all, d_gate_up.reshape(-1, 2 * ff), ((0,), (0,))).astype(BF)
+    activated, d_gate_up = activated.reshape(-1, ff), d_gate_up.reshape(-1, 2 * ff)
 
     norm_two_part = jnp.sum(d_normed * hidden * inverse_two, axis=0)
     d_hidden = d_result + norm_back(hidden, inverse_two, gain_two, d_normed)
@@ -1848,11 +1977,8 @@
     small = jnp.concatenate([norm_one_part, norm_two_part, query_gain_part, key_gain_part])
     if fast and lax.axis_size("dp") == 4:
         padded = jnp.pad(small, (0, SMALL * 128 - small.shape[0])).reshape(SMALL, 128)
-        grad_down, grad_gate_up, grad_out, grad_project, small, grad_input = reduce_all(
-            4,
-            [(grad_down, 1, 128), (grad_gate_up, 0, 64), (grad_out, 1, 160), (grad_project, 1, 240)],
-            padded,
-            grad_input.astype(BF),
+        grad_gate_up, grad_out, grad_project, grad_down, small, grad_input = reduce_all(
+            4, normed_all, d_gate_up, activated, d_low, grad_out, grad_project, padded, grad_input.astype(BF)
         )
         grad_input = grad_input.astype(F32)
         small = small.reshape(-1)[: 2 * D + 2 * HD]
@@ -1862,6 +1988,8 @@
         col_axes = ("group", "side")
         grad_project = lax.psum_scatter(grad_project, col_axes, scatter_dimension=0, tiled=True)
         grad_out = lax.psum_scatter(grad_out, col_axes, scatter_dimension=0, tiled=True)
+        grad_down = dot(activated, d_low, ((0,), (0,))).astype(BF)
+        grad_gate_up = dot(normed_all, d_gate_up, ((0,), (0,))).astype(BF)
         grad_down = sum_planes(scatter_rows(grad_down, 1), 2)
         grad_gate_up = sum_planes(scatter_rows(grad_gate_up, 0), 4)
         grad_out = sum_planes(scatter_rows(grad_out[0], 1), 1)

time: 808 us -> 754 us (0.933)
  matrix products: 66.4 us -> 25.9 us
  Pallas kernels: 677 us -> 665 us
    dot_general x5 -> x3, matrix products: 58.3 us -> 17.8 us  [dot(): lax.dot_general(left, right, (dims, ((), ())), preferred_element_type=F32)]
    pallas_call x2, Pallas kernels: 222 us -> 209 us  [spread(): pl.pallas_call(functools.partial(spread_kernel, forward, dealt is not Non...]
    pallas_call x1, Pallas kernels: 253 us -> 263 us  [reduce_all(): pl.pallas_call(functools.partial(reduce_kernel, parts, planes), out_shape...]
    pallas_call x1, Pallas kernels: 150 us -> 141 us  [front(): pl.pallas_call(front_kernel, out_shape=[shape((mine, depth), BF), shape((...]
where the time goes in v6:
time: 754 us; the launch traced here: 746 us
  Pallas kernels  665 us (88%)
  other arithmetic  39 us (5%)
  matrix products  25.9 us (3%)
  local copies, waits for them, and re-layouts  13.9 us (2%)
    pallas_call x1, Pallas kernels, reduce_all(): pl.pallas_call(functools.partial(reduce_kernel, parts, planes), out_shape...  263 us
    pallas_call x2, Pallas kernels, spread(): pl.pallas_call(functools.partial(spread_kernel, forward, dealt is not Non...  209 us
    pallas_call x1, Pallas kernels, front(): pl.pallas_call(front_kernel, out_shape=[shape((mine, depth), BF), shape((...  141 us
    pallas_call x1, Pallas kernels, back(): pl.pallas_call(back_kernel, out_shape=[shape((4, columns, mine), BF), sha...  51.8 us
    dot_general x3, matrix products, dot(): lax.dot_general(left, right, (dims, ((), ())), preferred_element_type=F32)  17.8 us

profile of v6, /device:TPU:0, one launch (start us, length us, event | category | flops | bytes accessed | tf_op | source)
XLA Modules:
  0.0 745.8 jit_solution(13384578991742115514)
XLA Ops:
  2.5 1.4 copy.47.refs_8_.refs_9_
  3.8 1.4 copy.48.refs_9_.refs_10_
  5.2 1.4 copy.44
  8.8 1.3 pad_maximum_fusion.refs_1_
  10.7 141.0 %front.1 = (bf16[512,2048]{1,0:T(8,128)(2,1)}, bf16[512,2048]{1,0:T(8,128)(2,1)}, f32[20,64,512]{2,1,0:T(8,128)}, bf16[20,64,512]{2,1,0:T(8,128)(2,1)}, bf16[320...) custom-call(bf16[1024,1024]{1,0:T(8,128)(2,1)} %refs_0_.1, ...), custom_call_target="tpu_custom_call" | custom-call | tf_op jit(solution)/shard_map/front/pallas_call | solution.py:1538
  151.7 104.7 %feed_forward.1 = (bf16[8,256,2048]{2,1,0:T(8,128)(2,1)}, bf16[8,256,1280]{2,1,0:T(8,128)(2,1)}, bf16[8,256,1280]{2,1,0:T(8,128)(2,1)}, bf16[8,256,1280]{2,1,0:T...) custom-call(bf16[512,2048]{1,0:T(8,128)(2,1)} %get-tuple-element.50.refs_0_, ...), custom_call_target="tpu_custom_call" | custom-call | tf_op jit(solution)/shard_map/feed_forward/pallas_call | solution.py:1139
  257.2 7.8 %fusion.16 = (bf16[512,2048]{1,0:T(8,128)(2,1)}, bf16[512,2048]{1,0:T(8,128)(2,1)}, f32[512]{0:T(512)S(1)}) fusion(f32[512,2048]{1,0:T(8,128)} %get-tuple-element.49, f32[2,256,2048]{2,1,0:T(8,128)} %get-tuple-element.53, bf16[512,2048]{1,0:T(8,128)(2,1)} %get-tuple-element.54, f32[]{:T(128)} %bitcast), kind=kLoop, calls=%fused_computation.34 | loop fusion | flops 8388096 | bytes 14682116 | tf_op jit(solution)/shard_map/convert_element_type | solution.py:1927
  264.9 104.1 %feed_forward_back.1 = (bf16[8,256,2048]{2,1,0:T(8,128)(2,1)}, bf16[8,256,2560]{2,1,0:T(8,128)(2,1)}, f32[2,256,2048]{2,1,0:T(8,128)}, bf16[1024,1024]{1,0:T(8,128)(2,1)}) custom-call(bf16[512,2048]{1,0:T(8,128)(2,1)} %get-tuple-element.89.refs_0_, bf16[1024,1280]{1,0:T(8,128)(2,1)} %refs_1_.3, bf16[1024,1280]{1,0:T(8,128)(2,1)} %get-tuple-element.51.refs_2_, ...), custom_call_target="tpu_custom_call" | custom-call | tf_op jit(solution)/shard_map/feed_forward_back/pallas_call | solution.py:1139
  369.2 5.1 fusion.13
  375.7 3.7 fusion.10
  379.5 4.5 convert_multiply_fusion.4
  384.0 2.1 reduce_sum.65.refs_3_
  386.2 51.8 %attend_back.1 = (bf16[4,480,512]{2,1,0:T(8,128)(2,1)S(1)}, f32[64,1]{1,0:T(8,128)S(1)}, f32[64,1]{1,0:T(8,128)S(1)}) custom-call(bf16[20,64,512]{2,1,0:T(8,128)(2,1)S(1)} %copy-done, bf16[20,64,512]{2,1,0:T(8,128)(2,1)S(1)} %bitcast.72, f32[5,4,512]{2,1,0:T(4,128)S(1)} %copy-done.6, f32[5,4,512]{2,1,0:T(4,128)S(1)} %reduce_sum.65.refs_3_, ...), custom_call_target="tpu_custom_call" | custom-call | tf_op jit(solution)/shard_map/attend_back/pallas_call | solution.py:1715
  438.1 8.5 %fusion.8 = (f32[512]{0:T(512)S(1)}, f32[2048]{0:T(1024)S(1)}, f32[512,2048,1]{1,0,2:T(8,128)S(1)}) fusion(bf16[512,2048]{1,0:T(8,128)(2,1)S(1)} %copy-done.16, f32[2048]{0:T(1024)S(1)} %bitcast.83, f32[512]{0:T(512)S(1)} %get-tuple-element.106, bf16[4,480,512]{2,1,0:T(8,128)(2,1)S(1)} %get-tuple-element.72, bf16[4,2048,480]{2,1,0:T(8,128)(2,1)} %bitcast.91), kind=kOutput, calls=%fused_computation.14 | convolution fusion | flops 4033869312 | bytes 16142336 | tf_op jit(solution)/shard_map/dot_general | solution.py:29
  446.6 2.6 fusion.6.refs_7_
  450.2 8.1 %convolution_convert_fusion.1.refs_5_ = bf16[4,480,2048]{2,1,0:T(8,128)(2,1)} fusion(bf16[4,480,512]{2,1,0:T(8,128)(2,1)S(1)} %copy-done.8, bf16[512,2048]{1,0:T(8,128)(2,1)} %get-tuple-element.73), kind=kOutput, calls=%fused_computation.5 | convolution fusion | flops 4030464000 | bytes 11927552 | tf_op jit(solution)/shard_map/dot_general | solution.py:1970
  458.3 4.8 convolution_convert_fusion
  463.1 263.1 %reduce_grads.1 = (bf16[1024,2560]{1,0:T(8,128)(2,1)}, bf16[320,1024]{1,0:T(8,128)(2,1)}, bf16[480,1024]{1,0:T(8,128)(2,1)}, bf16[1280,1024]{1,0:T(8,128)(2,1)},...) custom-call(bf16[2048,2048]{1,0:T(8,128)(2,1)} %bitcast.74, bf16[2048,2560]{1,0:T(8,128)(2,1)} %bitcast.73, ...), custom_call_target="tpu_custom_call" | custom-call | tf_op jit(solution)/shard_map/reduce_grads/pallas_call | solution.py:652
  726.3 7.6 %slice_convert_fusion = (f32[1024,1280]{1,0:T(8,128)}, f32[1024,1280]{1,0:T(8,128)}) fusion(bf16[1024,2560]{1,0:T(8,128)(2,1)} %get-tuple-element.82), kind=kLoop, calls=%fused_computation.29 | loop fusion | flops 2621440 | bytes 15728640 | tf_op jit(solution)/shard_map/convert_element_type | solution.py:2012
  733.8 3.0 convert_element_type.84
  736.9 2.5 convert_element_type.80
  739.6 1.1 slice.44
  741.6 1.2 convert_element_type.81
  744.1 1.3 copy.61
  (88 shorter events, 9.4 us)
Async XLA Ops:
  0.6 9.5 %copy-start.25 = (f32[1024]{0:T(1024)S(1)}, f32[1024]{0:T(1024)}, u32[]{:S(2)}) copy-start(f32[1024]{0:T(1024)} %param.18) | copy-start | bytes 12292
  0.7 9.5 %copy-start.24 = (f32[1024]{0:T(1024)S(1)}, f32[1024]{0:T(1024)}, u32[]{:S(2)}) copy-start(f32[1024]{0:T(1024)} %param.25) | copy-start | bytes 12292
  264.9 104.2 %copy-start.23 = (f32[2,2,1024]{2,1,0:T(2,128)S(1)}, f32[2,2,1024]{2,1,0:T(2,128)}, u32[]{:S(2)}) copy-start(f32[2,2,1024]{2,1,0:T(2,128)} %get-tuple-element.64) | copy-start | bytes 49156
  264.9 104.2 %copy-start.15 = (bf16[512,2048]{1,0:T(8,128)(2,1)S(1)}, bf16[512,2048]{1,0:T(8,128)(2,1)}, u32[]{:S(2)}) copy-start(bf16[512,2048]{1,0:T(8,128)(2,1)} %get-tuple-element.75) | copy-start | bytes 6291460
  369.1 5.2 copy-start.9
  369.2 5.9 copy-start.10
  369.2 6.5 copy-start.14
  369.2 10.2 %slice-start = ((s8[5242880]{0:T(1024)(128)(4,1)}), s8[4194304]{0:T(1024)(128)(4,1)S(1)}, s32[]{:S(2)}) async-start(s8[5242880]{0:T(1024)(128)(4,1)} %bitcast.92), calls=%async_computation | async-start | bytes 8388608
  375.7 3.7 copy-start.26
  379.4 4.6 copy-start.11
  379.4 6.7 copy-start
  379.4 6.7 copy-start.1
  379.5 6.7 copy-start.2
  379.5 6.7 copy-start.3
  379.5 6.7 copy-start.4
  379.5 6.7 copy-start.5
  379.5 6.7 copy-start.6
  386.2 51.9 %copy-start.16 = (bf16[512,2048]{1,0:T(8,128)(2,1)S(1)}, bf16[512,2048]{1,0:T(8,128)(2,1)}, u32[]{:S(2)}) copy-start(bf16[512,2048]{1,0:T(8,128)(2,1)} %get-tuple-element.75) | copy-start | bytes 6291460
  438.0 8.6 %copy-start.7 = (bf16[4,480,512]{2,1,0:T(8,128)(2,1)}, bf16[4,480,512]{2,1,0:T(8,128)(2,1)S(1)}, u32[]{:S(2)}) copy-start(bf16[4,480,512]{2,1,0:T(8,128)(2,1)S(1)} %get-tuple-element.72) | copy-start | bytes 5898244
  438.1 8.6 %copy-start.12 = (f32[512,2048]{1,0:T(8,128)S(1)}, f32[512,2048]{1,0:T(8,128)}, u32[]{:S(2)}) copy-start(f32[512,2048]{1,0:T(8,128)} %copy-done.11) | copy-start | bytes 12582916
  450.2 8.1 %copy-start.13 = (f32[512,2048]{1,0:T(8,128)S(1)}, f32[512,2048]{1,0:T(8,128)}, u32[]{:S(2)}) copy-start(f32[512,2048]{1,0:T(8,128)} %copy-done.11) | copy-start | bytes 12582916
  450.2 8.1 %copy-start.27 = (f32[1280,512]{1,0:T(8,128)S(1)}, f32[1280,512]{1,0:T(8,128)}, u32[]{:S(2)}) copy-start(f32[1280,512]{1,0:T(8,128)} %get-tuple-element.63) | copy-start | bytes 7864324
  726.2 7.6 %copy-start.17 = (bf16[1280,1024]{1,0:T(8,128)(2,1)S(1)}, bf16[1280,1024]{1,0:T(8,128)(2,1)}, u32[]{:S(2)}) copy-start(bf16[1280,1024]{1,0:T(8,128)(2,1)} %get-tuple-element.83) | copy-start | bytes 7864324
  739.4 4.7 copy-start.19
  (6 other events, 18.6 us)

commit v7 on v6

--- a/solution.py
+++ b/solution.py
@@ -686,43 +686,27 @@
 STEPS = 8
 
 
-def spread_kernel(forward, fast, *refs):
-    refs = list(refs)
-
-    def take(number):
-        taken = refs[:number]
-        del refs[:number]
-        return taken
-
-    (mine_ref,) = take(1)
-    weights = take(5 if forward and fast else 6)
-    if not forward:
-        gate_ref, up_ref = take(2)
-    dealt_in = take(1) if fast else None
+def spread_kernel(forward, *refs):
     if forward:
-        all_ref, gate_ref, up_ref, act_ref, out_ref = take(5)
-        if fast:
-            (down_out,) = take(1)
+        mine_ref, *weights = refs[:7]
+        all_ref, gate_ref, up_ref, act_ref, out_ref = refs[7:12]
+        rest = refs[12:]
     else:
-        all_ref, d_gate_up_ref, out_ref = take(3)
-    dealt_out = take(1) if fast else None
-    block, w_gate, w_up, w_down, kept, to_mate, from_mate, far_part, to_far, from_mate_far, far_sum, from_far = take(12)
+        mine_ref, *weights = refs[:7]
+        gate_ref, up_ref = refs[7:9]
+        all_ref, d_gate_up_ref, out_ref = refs[9:12]
+        rest = refs[12:]
+    block, w_gate, w_up, w_down, kept, to_mate, from_mate, far_part, to_far, from_mate_far, far_sum, from_far = rest[:12]
     (
         weight_sem, block_sem, out_sem, mate_send, mate_recv, x_send, x_recv, pass_send, pass_recv,
         sum_send, sum_recv, part_send, part_recv, back_send, back_recv,
-    ) = take(15)
-    deal_send, deal_recv, deal_local, row_send, row_recv, plane_send, plane_recv = take(7)
-    stage = refs
+    ) = rest[12:27]
+    stage = rest[27:]
     tokens, depth = mine_ref.shape
     quarter = tokens // 4
     width = w_gate.shape[1]
-    half = depth // 2
-    row = lax.axis_index("row")
     group, side = lax.axis_index("group"), lax.axis_index("side")
     mate, far = {"side": 1 - side}, {"group": 1 - group}
-    other_row, cross = {"row": 1 - row}, {"row": 1 - row, "side": 1 - side}
-    parity = lax.axis_index("dp") % 2
-    next_plane = {"dp": lax.axis_index("dp") + 1 - 2 * parity}
 
     def remote(source, target, send, recv, where):
         return pltpu.make_async_remote_copy(
@@ -730,48 +714,10 @@
         )
 
     barrier = pltpu.get_barrier_semaphore()
-    greeted = [mate, far]
-    if fast:
-        greeted += [other_row, cross] + ([next_plane] if forward else [])
-    for where in greeted:
+    for where in (mate, far):
         pl.semaphore_signal(barrier, 1, device_id=where, device_id_type=pl.DeviceIdType.MESH)
 
-    dealt_own, dealt_sent, down_chunks = [], [], []
-    if fast:
-        span = tokens // 4
-        member = 2 * row + side
-        for index, (to_row, to_side, where) in enumerate(
-            [(1 - row, side, other_row), (1 - row, 1 - side, cross), (row, 1 - side, mate), (row, side, None)]
-        ):
-            slot = 0 if index >= 2 else 1
-            there = 2 * to_row + to_side
-            for high in range(2):
-                piece = 7 - there if high else there
-                if not forward:
-                    piece = 7 - member if high else member
-                whole = pl.ds(pl.multiple_of(piece * span, span), span), slice(None)
-                of_side = side if forward else to_side
-                first = pl.multiple_of(of_side * 2 * span + high * span, span)
-                part = pl.ds(first, span), pl.ds(slot * half, half)
-                source = dealt_in[0].at[whole] if forward else dealt_in[0].at[part]
-                target = dealt_out[0].at[part] if forward else dealt_out[0].at[whole]
-                if where is None:
-                    dealt_own.append(pltpu.make_async_copy(source, target, deal_local.at[high]))
-                else:
-                    sems = deal_send.at[index, high], deal_recv.at[index, high]
-                    dealt_sent.append(remote(source, target, *sems, where))
-        if forward:
-            rows = width // 8
-            for index in range(4):
-                here = pl.ds(pl.multiple_of((4 * parity + index) * rows, 16), rows)
-                place = w_down.at[here, pl.ds(half, half)]
-                down_chunks.append(
-                    (
-                        remote(weights[4].at[here, :], place, row_send.at[index], row_recv.at[index], other_row),
-                        remote(place, place, plane_send.at[index], plane_recv.at[index], next_plane),
-                    )
-                )
-
+    half = depth // 2
     loads = []
     for index, (source, target) in enumerate(
         [
@@ -780,8 +726,8 @@
             (weights[2], w_up.at[pl.ds(0, half), :]),
             (weights[3], w_up.at[pl.ds(half, half), :]),
             (weights[4], w_down.at[:, pl.ds(0, half)]),
+            (weights[5], w_down.at[:, pl.ds(half, half)]),
         ]
-        + ([] if forward and fast else [(weights[5], w_down.at[:, pl.ds(half, half)])])
     ):
         loads.append(pltpu.make_async_copy(source, target, weight_sem.at[index]))
     order = loads if forward else loads[4:] + loads[:4]
@@ -795,9 +741,7 @@
         copy.start()
     for copy in order:
         copy.start()
-    pl.semaphore_wait(barrier, len(greeted))
-    for over_row, over_planes in down_chunks:
-        over_row.start()
+    pl.semaphore_wait(barrier, 2)
 
     def piece(index):
         return mine_ref.at[pl.ds(index * quarter, quarter), :]
@@ -838,8 +782,6 @@
     for index in range(4):
         mate_copy(index).start()
     x_copy(1).start()
-    for copy in dealt_sent + dealt_own:
-        copy.start()
     for copy in mine_copies:
         copy.wait()
 
@@ -868,7 +810,7 @@
             return [
                 pltpu.make_async_copy(stage_gate.at[slot], gate_ref.at[step], out_sem.at[1, step]),
                 pltpu.make_async_copy(stage_up.at[slot], up_ref.at[step], out_sem.at[2, step]),
-                pltpu.make_async_copy(stage_act.at[step], act_ref.at[step], out_sem.at[3, step]),
+                pltpu.make_async_copy(stage_act.at[slot], act_ref.at[step], out_sem.at[3, step]),
             ]
 
         def fetches(step):
@@ -892,13 +834,15 @@
                 up = dot(block[step], w_up[:, where])
                 stage_gate[slot, :, where] = gate.astype(BF)
                 stage_up[slot, :, where] = up.astype(BF)
-                stage_act[step, :, where] = (gate * up / (1.0 + jnp.exp(-gate))).astype(BF)
-
-        def second_half(step, first=0, last=depth // TILE):
-            @pl.loop(first, last)
+                stage_act[slot, :, where] = (gate * up / (1.0 + jnp.exp(-gate))).astype(BF)
+
+        def second_half(step):
+            slot = step % 2
+
+            @pl.loop(0, depth // TILE)
             def _(tile):
                 where = pl.ds(pl.multiple_of(tile * TILE, TILE), TILE)
-                emit(step, where, dot(stage_act[step], w_down[:, where]))
+                emit(step, where, dot(stage_act[slot], w_down[:, where]))
 
     else:
         stage_gate, stage_up, stage_d, fetch_sem = stage
@@ -954,9 +898,6 @@
         far_sum[index] = total.astype(BF)
         back_copy(index).start()
 
-    split = forward and fast
-    if split:
-        down_saved = pltpu.make_async_copy(w_down.at[:, pl.ds(half, half)], down_out, weight_sem.at[5])
     for copy in fetches(0):
         copy.start()
 
@@ -1000,41 +941,7 @@
         def _():
             second_loads()
 
-        if split:
-            @pl.when(step < 6)
-            def _():
-                second_half(step, 0, half // TILE)
-
-            for index in range(4):
-                @pl.when(step == index + 1)
-                def _(index=index):
-                    down_chunks[index][0].wait_recv()
-                    down_chunks[index][1].start()
-
-            @pl.when(step == 5)
-            def _():
-                for _, over_planes in down_chunks:
-                    over_planes.wait_recv()
-                down_saved.start()
-                pl.loop(4, 6)(lambda early: second_half(early, half // TILE))
-                part_copy(0).start()
-                part_copy(1).start()
-
-            @pl.when(step >= 6)
-            def _():
-                second_half(step)
-                part_copy(jnp.maximum(step - 4, 0)).start()
-
-            @pl.when(step == 6)
-            def _():
-                finish_far(0)
-                finish_far(1)
-
-            @pl.when(step == 7)
-            def _():
-                finish_far(2)
-        else:
-            second_half(step)
+        second_half(step)
         for copy in saves(step):
             copy.start()
 
@@ -1042,26 +949,19 @@
         def _():
             x_copy(2 + step // 2).start()
 
-        if not split:
-            @pl.when((step >= 2) & (step < 4))
-            def _():
-                sum_copy(jnp.clip(step - 2, 0, 1)).start()
-
-            @pl.when(step >= 4)
-            def _():
-                part_copy(jnp.maximum(step - 4, 0)).start()
-
-            @pl.when(step >= 5)
-            def _():
-                finish_far(jnp.maximum(step - 5, 0))
-
-    if split:
-        pl.loop(2, 4)(lambda early: second_half(early, half // TILE))
-        sum_copy(0).start()
-        sum_copy(1).start()
+        @pl.when((step >= 2) & (step < 4))
+        def _():
+            sum_copy(jnp.clip(step - 2, 0, 1)).start()
+
+        @pl.when(step >= 4)
+        def _():
+            part_copy(jnp.maximum(step - 4, 0)).start()
+
+        @pl.when(step >= 5)
+        def _():
+            finish_far(jnp.maximum(step - 5, 0))
+
     finish_far(3)
-    if split:
-        pl.loop(0, 2)(lambda early: second_half(early, half // TILE))
     for index in range(2):
         sum_copy(index).wait_recv()
         kept[index] = kept[index] + from_mate[index].astype(F32)
@@ -1074,15 +974,8 @@
             copy = pltpu.make_async_copy(kept.at[index // 2], out_ref.at[index // 2], block_sem.at[index // 2])
             copy.start()
             results.append(copy)
-    for copy in results + dealt_own:
+    for copy in results:
         copy.wait()
-    for copy in dealt_sent:
-        copy.wait()
-    for over_row, over_planes in down_chunks:
-        over_row.wait_send()
-        over_planes.wait_send()
-    if forward and fast:
-        down_saved.wait()
 
     @pl.loop(0, STEPS)
     def _(step):
@@ -1107,7 +1000,7 @@
             sum_copy(jnp.minimum(step, 1)).wait_send()
 
 
-def spread(forward, mine, weights, kept=(), dealt=None):
+def spread(forward, mine, weights, *kept):
     tokens, depth = mine.shape
     quarter, double = tokens // 4, tokens // 2
     width = weights[0].shape[1]
@@ -1117,29 +1010,19 @@
     out = jax.ShapeDtypeStruct((2, double, depth), F32)
     if forward:
         outs = [whole, wide, wide, wide, out]
-        if dealt is not None:
-            outs.append(jax.ShapeDtypeStruct((width, depth // 2), BF))
-            outs.append(jax.ShapeDtypeStruct((tokens, depth), BF))
-        stage = [
-            pltpu.VMEM((2, double, width), BF),
-            pltpu.VMEM((2, double, width), BF),
-            pltpu.VMEM((STEPS, double, width), BF),
-        ]
+        stage = [pltpu.VMEM((2, double, width), BF) for _ in range(3)]
     else:
         outs = [whole, jax.ShapeDtypeStruct((STEPS, double, 2 * width), BF), out]
-        if dealt is not None:
-            outs.append(jax.ShapeDtypeStruct((2 * tokens, depth // 2), BF))
         stage = [
             pltpu.VMEM((2, double, width), BF),
             pltpu.VMEM((2, double, width), BF),
             pltpu.VMEM((2, double, 2 * width), BF),
             pltpu.SemaphoreType.DMA((2, STEPS)),
         ]
-    inputs = [mine, *weights, *kept] + ([] if dealt is None else [dealt])
-    return pl.pallas_call(
-        functools.partial(spread_kernel, forward, dealt is not None),
+    result = pl.pallas_call(
+        functools.partial(spread_kernel, forward),
         out_shape=outs,
-        in_specs=[anywhere] * len(inputs),
+        in_specs=[anywhere] * (7 + len(kept)),
         out_specs=[anywhere] * len(outs),
         scratch_shapes=[
             pltpu.VMEM((STEPS, double, depth), BF),
@@ -1161,16 +1044,513 @@
         + [pltpu.SemaphoreType.DMA((4,)) for _ in range(6)]
         + [pltpu.SemaphoreType.DMA((2,)) for _ in range(2)]
         + [pltpu.SemaphoreType.DMA((4,)) for _ in range(4)]
-        + [pltpu.SemaphoreType.DMA((3, 2)), pltpu.SemaphoreType.DMA((3, 2)), pltpu.SemaphoreType.DMA((2,))]
-        + [pltpu.SemaphoreType.DMA((4,)) for _ in range(4)]
         + stage,
         compiler_params=pltpu.CompilerParams(
-            collective_id=1 if forward else 2,
+            collective_id=5 if forward else 2,
             has_side_effects=True,
             vmem_limit_bytes=60 * 1024 * 1024,
         ),
-        name="feed_forward" if forward else "feed_forward_back",
-    )(*inputs)
+        name="spread" if forward else "spread_back",
+    )(mine, *weights, *kept)
+    return result
+
+
+def feed_kernel(*refs):
+    refs = list(refs)
+
+    def take(number):
+        taken = refs[:number]
+        del refs[:number]
+        return taken
+
+    mine_ref, *weights = take(6)
+    teacher_ref, hidden_ref, scale_ref = take(3)
+    all_ref, gate_ref, up_ref, act_ref, target_ref = take(5)
+    all_low_ref, d_gate_up_ref, d_result_ref, out_ref, block_out_ref = take(5)
+    block, w_gate, w_up, w_down, kept, to_mate, from_mate, far_part, to_far, from_mate_far, far_sum, from_far = take(12)
+    stage_gate, stage_up, stage_act = take(3)
+    weight_sem, block_sem, out_sem, fetch_sem, result_sem = take(5)
+    mate_send, mate_recv, x_send, x_recv, pass_send, pass_recv, sum_send, sum_recv = take(8)
+    part_send, part_recv, back_send, back_recv = take(4)
+    deal_send, deal_recv, deal_local, row_send, row_recv, plane_send, plane_recv = take(7)
+    tokens, depth = mine_ref.shape
+    quarter = tokens // 4
+    width = w_gate.shape[1]
+    half = depth // 2
+    row = lax.axis_index("row")
+    group, side = lax.axis_index("group"), lax.axis_index("side")
+    mate, far = {"side": 1 - side}, {"group": 1 - group}
+    other_row, cross = {"row": 1 - row}, {"row": 1 - row, "side": 1 - side}
+    parity = lax.axis_index("dp") % 2
+    next_plane = {"dp": lax.axis_index("dp") + 1 - 2 * parity}
+    member = 2 * row + side
+
+    def remote(source, target, send, recv, where):
+        return pltpu.make_async_remote_copy(
+            source, target, send, recv, device_id=where, device_id_type=pl.DeviceIdType.MESH
+        )
+
+    def local(source, target, sem):
+        return pltpu.make_async_copy(source, target, sem)
+
+    barrier = pltpu.get_barrier_semaphore()
+    greeted = [mate, far, other_row, cross, next_plane]
+    for where in greeted:
+        pl.semaphore_signal(barrier, 1, device_id=where, device_id_type=pl.DeviceIdType.MESH)
+
+    mine_copies = [
+        local(mine_ref.at[pl.ds(i * 2 * quarter, 2 * quarter), :], block.at[i], block_sem.at[i]) for i in range(2)
+    ]
+    loads = [
+        local(weights[0], w_gate.at[pl.ds(0, half), :], weight_sem.at[0]),
+        local(weights[1], w_gate.at[pl.ds(half, half), :], weight_sem.at[1]),
+        local(weights[2], w_up.at[pl.ds(0, half), :], weight_sem.at[2]),
+        local(weights[3], w_up.at[pl.ds(half, half), :], weight_sem.at[3]),
+        local(weights[4], w_down.at[:, pl.ds(0, half)], weight_sem.at[4]),
+    ]
+    for copy in mine_copies + loads:
+        copy.start()
+
+    down_chunks = []
+    rows = width // 8
+    for index in range(4):
+        here = pl.ds(pl.multiple_of((4 * parity + index) * rows, 16), rows)
+        place = w_down.at[here, pl.ds(half, half)]
+        down_chunks.append(
+            (
+                remote(weights[4].at[here, :], place, row_send.at[index], row_recv.at[index], other_row),
+                remote(place, place, plane_send.at[index], plane_recv.at[index], next_plane),
+            )
+        )
+
+    def deals(outward):
+        sent, own = [], []
+        for index, (to_row, to_side, where) in enumerate(
+            [(1 - row, side, other_row), (1 - row, 1 - side, cross), (row, 1 - side, mate), (row, side, None)]
+        ):
+            slot = 0 if index >= 2 else 1
+            there = 2 * to_row + to_side if outward == 0 else member
+            for high in range(2):
+                piece = 7 - there if high else there
+                whole = pl.ds(pl.multiple_of(piece * quarter, quarter), quarter), slice(None)
+                columns = pl.ds(slot * half, half)
+                if outward == 0:
+                    first = pl.multiple_of(side * 2 * quarter + high * quarter, quarter)
+                    source, target = teacher_ref.at[whole], target_ref.at[pl.ds(first, quarter), columns]
+                else:
+                    source = to_mate.at[to_side, pl.ds(high * quarter, quarter), columns]
+                    target = block_out_ref.at[whole]
+                if where is None:
+                    own.append(local(source, target, deal_local.at[outward, high]))
+                else:
+                    sems = deal_send.at[outward, index, high], deal_recv.at[outward, index, high]
+                    sent.append(remote(source, target, *sems, where))
+        return sent, own
+
+    teacher_sent, teacher_own = deals(0)
+    result_sent, result_own = deals(1)
+
+    def piece(phase, index):
+        if phase == 0:
+            return mine_ref.at[pl.ds(index * quarter, quarter), :]
+        return block.at[index // 2, pl.ds(index % 2 * quarter, quarter), :]
+
+    def mate_copy(phase, index):
+        target = block.at[2 + index // 2, pl.ds(index % 2 * quarter, quarter), :]
+        return remote(piece(phase, index), target, mate_send.at[phase, index], mate_recv.at[phase, index], mate)
+
+    def x_copy(phase, index):
+        target = block.at[4 + index, pl.ds(0, quarter), :]
+        return remote(piece(phase, index), target, x_send.at[phase, index], x_recv.at[phase, index], far)
+
+    def pass_copy(phase, index):
+        return remote(
+            block.at[4 + index, pl.ds(0, quarter), :],
+            block.at[4 + index, pl.ds(quarter, quarter), :],
+            pass_send.at[phase, index],
+            pass_recv.at[phase, index],
+            mate,
+        )
+
+    def sum_copy(phase, index):
+        return remote(
+            to_mate.at[index], from_mate.at[index], sum_send.at[phase, index], sum_recv.at[phase, index], mate
+        )
+
+    def part_copy(phase, index):
+        return remote(
+            to_far.at[index], from_mate_far.at[index], part_send.at[phase, index], part_recv.at[phase, index], mate
+        )
+
+    def back_copy(phase, index):
+        return remote(
+            far_sum.at[index], from_far.at[index], back_send.at[phase, index], back_recv.at[phase, index], far
+        )
+
+    def all_copy(phase, step):
+        return local(block.at[step], (all_ref, all_low_ref)[phase].at[step], out_sem.at[4 * phase, step])
+
+    def saves(step):
+        return [
+            local(stage_gate.at[step % 2], gate_ref.at[step], out_sem.at[1, step]),
+            local(stage_up.at[step % 2], up_ref.at[step], out_sem.at[2, step]),
+            local(stage_act.at[step], act_ref.at[step], out_sem.at[3, step]),
+        ]
+
+    def back_saves(step):
+        slot = 2 * (step % 2)
+        return [
+            local(stage_act.at[slot + i], d_gate_up_ref.at[step, :, pl.ds(i * width, width)], out_sem.at[5 + i, step])
+            for i in range(2)
+        ]
+
+    def fetches(step):
+        return [
+            local(gate_ref.at[step], stage_gate.at[step % 2], fetch_sem.at[0, step]),
+            local(up_ref.at[step], stage_up.at[step % 2], fetch_sem.at[1, step]),
+        ]
+
+    def emit(step, where, part):
+        @pl.when(step < 2)
+        def _():
+            kept[jnp.minimum(step, 1), :, where] = part
+
+        @pl.when((step >= 2) & (step < 4))
+        def _():
+            to_mate[jnp.clip(step - 2, 0, 1), :, where] = part.astype(BF)
+
+        @pl.when(step >= 4)
+        def _():
+            far_part[jnp.maximum(step - 4, 0), :, where] = part[:quarter]
+            to_far[jnp.maximum(step - 4, 0), :, where] = part[quarter:].astype(BF)
+
+    def tiles(first, last, action):
+        @pl.loop(first, last)
+        def _(tile):
+            action(pl.ds(pl.multiple_of(tile * TILE, TILE), TILE), pl.multiple_of(tile * TILE, TILE))
+
+    def multiply_in(step):
+        slot = step % 2
+
+        def action(where, first):
+            gate = dot(block[step], w_gate[:, where])
+            up = dot(block[step], w_up[:, where])
+            stage_gate[slot, :, where] = gate.astype(BF)
+            stage_up[slot, :, where] = up.astype(BF)
+            stage_act[step, :, where] = (gate * up / (1.0 + jnp.exp(-gate))).astype(BF)
+
+        tiles(0, width // TILE, action)
+
+    def multiply_out(step, first=0, last=depth // TILE):
+        tiles(first, last, lambda where, _: emit(step, where, dot(stage_act[step], w_down[:, where])))
+
+    def multiply_back_in(step):
+        slot = step % 2
+
+        def action(where, first):
+            d_act = dot(block[step], w_down[where, :], ((1,), (1,)))
+            gate = stage_gate[slot, :, where].astype(F32)
+            up = stage_up[slot, :, where].astype(F32)
+            sig = 1.0 / (1.0 + jnp.exp(-gate))
+            d_gate = d_act * up * sig * (1.0 + gate * (1.0 - sig))
+            stage_act[2 * slot, :, where] = d_gate.astype(BF)
+            stage_act[2 * slot + 1, :, where] = (d_act * gate * sig).astype(BF)
+
+        tiles(0, width // TILE, action)
+
+    def multiply_back_out(step):
+        slot = 2 * (step % 2)
+
+        def action(where, first):
+            part = dot(stage_act[slot], w_gate[where, :], ((1,), (1,)))
+            part += dot(stage_act[slot + 1], w_up[where, :], ((1,), (1,)))
+            emit(step, where, part)
+
+        tiles(0, depth // TILE, action)
+
+    def finish_far(phase, index):
+        part_copy(phase, index).wait_recv()
+        total = far_part[index] + from_mate_far[index].astype(F32)
+        far_sum[index] = total.astype(BF)
+        if phase == 0:
+            all_copy(0, 4 + index).wait()
+            pass_copy(0, index).wait_send()
+        back_copy(phase, index).start()
+
+    def arrive(phase, step):
+        @pl.when((step == 2) | (step == 3))
+        def _():
+            index = jnp.clip(2 * (step - 2), 0, 2)
+            mate_copy(phase, index).wait_recv()
+            mate_copy(phase, index + 1).wait_recv()
+
+        @pl.when(step >= 4)
+        def _():
+            index = jnp.maximum(step - 4, 0)
+            x_copy(phase, index).wait_recv()
+            pass_copy(phase, index).start()
+            pass_copy(phase, index).wait_recv()
+
+        all_copy(phase, step).start()
+
+    pl.semaphore_wait(barrier, len(greeted))
+    for over_row, _ in down_chunks:
+        over_row.start()
+    x_copy(0, 0).start()
+    for index in range(4):
+        mate_copy(0, index).start()
+    x_copy(0, 1).start()
+    for copy in teacher_sent + teacher_own:
+        copy.start()
+    for copy in mine_copies:
+        copy.wait()
+
+    @pl.loop(0, STEPS)
+    def _(step):
+        @pl.when(step == 7)
+        def _():
+            finish_far(0, 2)
+
+        arrive(0, step)
+
+        @pl.when(step == 0)
+        def _():
+            for copy in loads:
+                copy.wait()
+
+        @pl.when(step >= 2)
+        def _():
+            for copy in saves(jnp.maximum(step - 2, 0)):
+                copy.wait()
+
+        multiply_in(step)
+
+        @pl.when(step < 6)
+        def _():
+            multiply_out(step, 0, half // TILE)
+
+        for index in range(4):
+            @pl.when(step == index + 1)
+            def _(index=index):
+                down_chunks[index][0].wait_recv()
+                down_chunks[index][1].start()
+
+        @pl.when(step == 5)
+        def _():
+            for _, over_planes in down_chunks:
+                over_planes.wait_recv()
+            pl.loop(4, 6)(lambda early: multiply_out(early, half // TILE))
+            part_copy(0, 0).start()
+            part_copy(0, 1).start()
+            pl.loop(2, 4)(lambda early: multiply_out(early, half // TILE))
+            for index in range(2):
+                all_copy(0, 2 + index).wait()
+                sum_copy(0, index).start()
+            finish_far(0, 0)
+            finish_far(0, 1)
+            pl.loop(0, 2)(lambda early: multiply_out(early, half // TILE))
+
+        @pl.when(step >= 6)
+        def _():
+            multiply_out(step)
+            part_copy(0, jnp.maximum(step - 4, 0)).start()
+
+        for copy in saves(step):
+            copy.start()
+
+        @pl.when((step == 1) | (step == 3))
+        def _():
+            x_copy(0, 2 + step // 2).start()
+
+    for copy in teacher_own:
+        copy.wait()
+    for copy in teacher_sent:
+        copy.wait_recv()
+    result_loads = []
+    for index in range(4):
+        if index == 3:
+            finish_far(0, 3)
+        part_copy(0, index).wait_send()
+        here = pl.ds(index * quarter, quarter)
+        result_loads.append(
+            [
+                local(target_ref.at[here, :], to_far.at[index], result_sem.at[0, index]),
+                local(hidden_ref.at[here, :], far_part.at[index], result_sem.at[1, index]),
+            ]
+        )
+        for copy in result_loads[-1]:
+            copy.start()
+    for index in range(2):
+        all_copy(0, index).wait()
+        sum_copy(0, index).wait()
+    for step in (STEPS - 2, STEPS - 1):
+        for copy in saves(step):
+            copy.wait()
+    for copy in fetches(0):
+        copy.start()
+    scale = scale_ref[0]
+    d_result_saves = []
+    for index in range(4):
+        back_copy(0, index).wait_recv()
+        for copy in result_loads[index]:
+            copy.wait()
+        here = pl.ds(index % 2 * quarter, quarter)
+
+        def action(where, first):
+            total = kept[index // 2, here, where] + from_mate[index // 2, here, where].astype(F32)
+            total = total + from_far[index, :, where].astype(F32)
+            result = far_part[index, :, where] + total
+            d_result = scale * (result - to_far[index, :, where].astype(F32))
+            to_mate[index // 2, here, where] = result.astype(BF)
+            kept[index // 2, here, where] = d_result
+            block[index // 2, here, where] = d_result.astype(BF)
+
+        tiles(0, depth // TILE, action)
+        x_copy(1, index).start()
+        mate_copy(1, index).start()
+        if index % 2:
+            copy = local(kept.at[index // 2], d_result_ref.at[index // 2], block_sem.at[index // 2])
+            copy.start()
+            d_result_saves.append(copy)
+    for copy in result_sent + result_own:
+        copy.start()
+    for index in range(4):
+        mate_copy(0, index).wait_send()
+        x_copy(0, index).wait_send()
+        back_copy(0, index).wait_send()
+
+    @pl.loop(0, STEPS)
+    def _(step):
+        @pl.when(step >= 5)
+        def _():
+            finish_far(1, jnp.maximum(step - 5, 0))
+
+        arrive(1, step)
+        for copy in fetches(step):
+            copy.wait()
+
+        @pl.when(step < STEPS - 1)
+        def _():
+            for copy in fetches(jnp.minimum(step + 1, STEPS - 1)):
+                copy.start()
+
+        @pl.when(step >= 2)
+        def _():
+            for copy in back_saves(jnp.maximum(step - 2, 0)):
+                copy.wait()
+
+        multiply_back_in(step)
+
+        @pl.when(step == 0)
+        def _():
+            for copy in d_result_saves:
+                copy.wait()
+
+        @pl.when(step == 2)
+        def _():
+            for copy in result_own:
+                copy.wait()
+            for copy in result_sent:
+                copy.wait_send()
+
+        multiply_back_out(step)
+        for copy in back_saves(step):
+            copy.start()
+
+        @pl.when((step >= 2) & (step < 4))
+        def _():
+            sum_copy(1, jnp.clip(step - 2, 0, 1)).start()
+
+        @pl.when(step >= 4)
+        def _():
+            part_copy(1, jnp.maximum(step - 4, 0)).start()
+
+    finish_far(1, 3)
+    for index in range(2):
+        sum_copy(1, index).wait_recv()
+        kept[index] = kept[index] + from_mate[index].astype(F32)
+    results = []
+    for index in range(4):
+        back_copy(1, index).wait_recv()
+        here = pl.ds(index % 2 * quarter, quarter)
+        kept[index // 2, here, :] = kept[index // 2, here, :] + from_far[index].astype(F32)
+        if index % 2:
+            results.append(local(kept.at[index // 2], out_ref.at[index // 2], block_sem.at[index // 2]))
+            results[-1].start()
+    for copy in results:
+        copy.wait()
+    for copy in result_sent:
+        copy.wait_recv()
+    for copy in teacher_sent:
+        copy.wait_send()
+    for over_row, over_planes in down_chunks:
+        over_row.wait_send()
+        over_planes.wait_send()
+
+    @pl.loop(0, STEPS)
+    def _(step):
+        all_copy(1, step).wait()
+
+        @pl.when(step >= STEPS - 2)
+        def _():
+            for copy in back_saves(step):
+                copy.wait()
+
+        @pl.when(step < 4)
+        def _():
+            index = jnp.minimum(step, 3)
+            for copy in (mate_copy, x_copy, pass_copy, part_copy, back_copy):
+                copy(1, index).wait_send()
+
+        @pl.when(step < 2)
+        def _():
+            sum_copy(1, jnp.minimum(step, 1)).wait_send()
+
+
+def feed(mine, weights, teacher, hidden, scale):
+    tokens, depth = mine.shape
+    quarter, double = tokens // 4, tokens // 2
+    width = weights[0].shape[1]
+    anywhere = pl.BlockSpec(memory_space=pl.ANY)
+    shape = jax.ShapeDtypeStruct
+    wide, whole = shape((STEPS, double, width), BF), shape((STEPS, double, depth), BF)
+    own = shape((2, double, depth), F32)
+    outs = [
+        whole, wide, wide, wide, shape((tokens, depth), BF),
+        whole, shape((STEPS, double, 2 * width), BF), own, own, shape((2 * tokens, depth // 2), BF),
+    ]
+    dma = pltpu.SemaphoreType.DMA
+    return pl.pallas_call(
+        feed_kernel,
+        out_shape=outs,
+        in_specs=[anywhere] * 8 + [pl.BlockSpec(memory_space=pltpu.SMEM)],
+        out_specs=[anywhere] * len(outs),
+        scratch_shapes=[
+            pltpu.VMEM((STEPS, double, depth), BF),
+            pltpu.VMEM((depth, width), BF),
+            pltpu.VMEM((depth, width), BF),
+            pltpu.VMEM((width, depth), BF),
+            pltpu.VMEM((2, double, depth), F32),
+            pltpu.VMEM((2, double, depth), BF),
+            pltpu.VMEM((2, double, depth), BF),
+            pltpu.VMEM((4, quarter, depth), F32),
+            pltpu.VMEM((4, quarter, depth), BF),
+            pltpu.VMEM((4, quarter, depth), BF),
+            pltpu.VMEM((4, quarter, depth), BF),
+            pltpu.VMEM((4, quarter, depth), BF),
+            pltpu.VMEM((2, double, width), BF),
+            pltpu.VMEM((2, double, width), BF),
+            pltpu.VMEM((STEPS, double, width), BF),
+            dma((5,)), dma((2,)), dma((7, STEPS)), dma((2, STEPS)), dma((2, 4)),
+            dma((2, 4)), dma((2, 4)), dma((2, 4)), dma((2, 4)), dma((2, 4)), dma((2, 4)), dma((2, 2)), dma((2, 2)),
+            dma((2, 4)), dma((2, 4)), dma((2, 4)), dma((2, 4)),
+            dma((2, 3, 2)), dma((2, 3, 2)), dma((2, 2)), dma((4,)), dma((4,)), dma((4,)), dma((4,)),
+        ],
+        compiler_params=pltpu.CompilerParams(
+            collective_id=1, has_side_effects=True, vmem_limit_bytes=60 * 1024 * 1024
+        ),
+        name="feed_forward",
+    )(mine, *weights, teacher, hidden, scale)
 
 
 def front_kernel(*refs):
@@ -1908,26 +2288,18 @@
         inverse_two = rms(hidden)
         normed_two = (hidden * inverse_two * gain_two).astype(BF)
 
+    total_tokens = shard * cols * lax.axis_size("dp")
+    loss_scale = total_tokens / token_count[0].astype(F32)
     if fast:
-        normed_all, gate, up, activated, ffn_out, down_other, target = spread(
-            True, normed_two, ffn_weights, dealt=teacher
-        )
-        ffn_weights.append(down_other)
+        normed_all, _, _, activated, _, d_low, d_gate_up, d_result, d_normed, block_out = feed(
+            normed_two, ffn_weights, teacher, hidden, loss_scale[None]
+        )
+        d_result = d_result.reshape(mine, D)
     else:
         normed_all, gate, up, activated, ffn_out = spread(True, normed_two, ffn_weights)
-        target = to_members(teacher)
-    ffn_out = ffn_out.reshape(mine, D)
-    result = hidden + ffn_out
-
-    total_tokens = shard * cols * lax.axis_size("dp")
-    loss_scale = total_tokens / token_count[0].astype(F32)
-    d_result = loss_scale * (result - target.astype(F32))
-    if fast:
-        d_low, d_gate_up, d_normed, block_out = spread(
-            False, d_result.astype(BF), ffn_weights, (gate, up), result.astype(BF)
-        )
-    else:
-        d_low, d_gate_up, d_normed = spread(False, d_result.astype(BF), ffn_weights, (gate, up))
+        result = hidden + ffn_out.reshape(mine, D)
+        d_result = loss_scale * (result - to_members(teacher).astype(F32))
+        d_low, d_gate_up, d_normed = spread(False, d_result.astype(BF), ffn_weights, gate, up)
         block_out = from_members(result.astype(BF))
     d_normed = d_normed.reshape(mine, D)
     d_low, normed_all = d_low.reshape(-1, D), normed_all.reshape(-1, D)

time: 754 us -> 732 us (0.971)
  Pallas kernels: 665 us -> 646 us
  other arithmetic: 39 us -> 30.2 us
    pallas_call x2 -> x1, Pallas kernels: 209 us -> 190 us  [feed(): pl.pallas_call(feed_kernel, out_shape=outs, in_specs=[anywhere] * 8 + [pl...]
    convert_element_type x1 -> x0, other arithmetic: 7.78 us -> none  [body(): result.astype(BF)]
where the time goes in v7:
time: 732 us; the launch traced here: 722 us
  Pallas kernels  646 us (88%)
  other arithmetic  30.2 us (4%)
  matrix products  30.2 us (4%)
  local copies, waits for them, and re-layouts  14 us (2%)
    pallas_call x1, Pallas kernels, reduce_all(): pl.pallas_call(functools.partial(reduce_kernel, parts, planes), out_shape...  263 us
    pallas_call x1, Pallas kernels, feed(): pl.pallas_call(feed_kernel, out_shape=outs, in_specs=[anywhere] * 8 + [pl...  190 us
    pallas_call x1, Pallas kernels, front(): pl.pallas_call(front_kernel, out_shape=[shape((mine, depth), BF), shape((...  141 us
    pallas_call x1, Pallas kernels, back(): pl.pallas_call(back_kernel, out_shape=[shape((4, columns, mine), BF), sha...  51.7 us
    dot_general x3, matrix products, dot(): lax.dot_general(left, right, (dims, ((), ())), preferred_element_type=F32)  22.1 us

profile of v7, /device:TPU:0, one launch (start us, length us, event | category | flops | bytes accessed | tf_op | source)
XLA Modules:
  0.0 722.4 jit_solution(13220307162856764281)
XLA Ops:
  2.5 1.4 copy.47.refs_8_.refs_9_
  3.8 1.4 copy.48.refs_9_.refs_10_
  5.2 1.4 copy.44
  7.7 1.1 copy.46
  8.8 1.3 pad_maximum_fusion.refs_1_
  10.7 141.0 %front.1 = (bf16[512,2048]{1,0:T(8,128)(2,1)}, bf16[512,2048]{1,0:T(8,128)(2,1)}, f32[20,64,512]{2,1,0:T(8,128)}, bf16[20,64,512]{2,1,0:T(8,128)(2,1)}, bf16[320...) custom-call(bf16[1024,1024]{1,0:T(8,128)(2,1)} %refs_0_.1, ...), custom_call_target="tpu_custom_call" | custom-call | tf_op jit(solution)/shard_map/front/pallas_call | solution.py:1918
  152.4 189.9 %feed_forward.1 = (bf16[8,256,2048]{2,1,0:T(8,128)(2,1)}, bf16[8,256,1280]{2,1,0:T(8,128)(2,1)}, bf16[8,256,1280]{2,1,0:T(8,128)(2,1)}, bf16[8,256,1280]{2,1,0:T...) custom-call(bf16[512,2048]{1,0:T(8,128)(2,1)} %get-tuple-element.45., ...), custom_call_target="tpu_custom_call" | custom-call | tf_op jit(solution)/shard_map/feed_forward/pallas_call | solution.py:1523
  342.4 2.7 multiply_reduce_fusion
  345.8 4.0 fusion.13
  350.5 1.1 fusion.10
  351.7 8.7 %convert_multiply_fusion.4 = (f32[1280,512]{1,0:T(8,128)}, bf16[1280,512]{1,0:T(8,128)(2,1)S(1)}) fusion(f32[1280,512]{1,0:T(8,128)} %get-tuple-element.54, bf16[1280,2048]{1,0:T(8,128)(2,1)} %get-tuple-element.59, f32[512,2048]{1,0:T(8,128)S(1)} %fusion.10), kind=kOutput, calls=%fused_computation.28 | convolution fusion | flops 2687369216 | bytes 15990784 | tf_op jit(solution)/shard_map/dot_general | solution.py:29
  360.4 2.1 reduce_sum.65.refs_3_
  362.6 51.7 %attend_back.1 = (bf16[4,480,512]{2,1,0:T(8,128)(2,1)S(1)}, f32[64,1]{1,0:T(8,128)S(1)}, f32[64,1]{1,0:T(8,128)S(1)}) custom-call(bf16[20,64,512]{2,1,0:T(8,128)(2,1)S(1)} %copy-done, bf16[20,64,512]{2,1,0:T(8,128)(2,1)S(1)} %bitcast.65, f32[5,4,512]{2,1,0:T(4,128)S(1)} %copy-done.6, f32[5,4,512]{2,1,0:T(4,128)S(1)} %reduce_sum.65.refs_3_, ...), custom_call_target="tpu_custom_call" | custom-call | tf_op jit(solution)/shard_map/attend_back/pallas_call | solution.py:2095
  414.4 8.8 %fusion.8 = (f32[512]{0:T(512)S(1)}, f32[2048]{0:T(1024)S(1)}, f32[512,2048,1]{1,0,2:T(8,128)S(1)}) fusion(bf16[512,2048]{1,0:T(8,128)(2,1)S(1)} %copy-done.15, f32[2048]{0:T(1024)S(1)} %bitcast.76, f32[512]{0:T(512)S(1)} %get-tuple-element.95, bf16[4,480,512]{2,1,0:T(8,128)(2,1)S(1)} %get-tuple-element.64, bf16[4,2048,480]{2,1,0:T(8,128)(2,1)} %bitcast.84), kind=kOutput, calls=%fused_computation.14 | convolution fusion | flops 4033869312 | bytes 16142336 | tf_op jit(solution)/shard_map/dot_general | solution.py:29
  423.3 2.6 fusion.6.refs_7_
  426.8 8.1 %convolution_convert_fusion.1.refs_5_ = bf16[4,480,2048]{2,1,0:T(8,128)(2,1)} fusion(bf16[4,480,512]{2,1,0:T(8,128)(2,1)S(1)} %copy-done.8, bf16[512,2048]{1,0:T(8,128)(2,1)} %get-tuple-element.65), kind=kOutput, calls=%fused_computation.5 | convolution fusion | flops 4030464000 | bytes 11927552 | tf_op jit(solution)/shard_map/dot_general | solution.py:2342
  434.9 4.6 convolution_convert_fusion
  439.5 263.2 %reduce_grads.1 = (bf16[1024,2560]{1,0:T(8,128)(2,1)}, bf16[320,1024]{1,0:T(8,128)(2,1)}, bf16[480,1024]{1,0:T(8,128)(2,1)}, bf16[1280,1024]{1,0:T(8,128)(2,1)},...) custom-call(bf16[2048,2048]{1,0:T(8,128)(2,1)} %bitcast.67, bf16[2048,2560]{1,0:T(8,128)(2,1)} %bitcast.66, ...), custom_call_target="tpu_custom_call" | custom-call | tf_op jit(solution)/shard_map/reduce_grads/pallas_call | solution.py:652
  702.7 7.6 %slice_convert_fusion = (f32[1024,1280]{1,0:T(8,128)}, f32[1024,1280]{1,0:T(8,128)}) fusion(bf16[1024,2560]{1,0:T(8,128)(2,1)} %get-tuple-element.74), kind=kLoop, calls=%fused_computation.26 | loop fusion | flops 2621440 | bytes 15728640 | tf_op jit(solution)/shard_map/convert_element_type | solution.py:2384
  710.3 3.0 convert_element_type.72
  713.3 2.5 convert_element_type.68
  716.1 1.2 slice.44
  718.2 1.2 convert_element_type.69
  720.6 1.3 copy.61
  (80 shorter events, 8.4 us)
Async XLA Ops:
  0.6 9.5 %copy-start.25 = (f32[1024]{0:T(1024)S(1)}, f32[1024]{0:T(1024)}, u32[]{:S(2)}) copy-start(f32[1024]{0:T(1024)} %param.18) | copy-start | bytes 12292
  0.7 9.5 %copy-start.24 = (f32[1024]{0:T(1024)S(1)}, f32[1024]{0:T(1024)}, u32[]{:S(2)}) copy-start(f32[1024]{0:T(1024)} %param.25) | copy-start | bytes 12292
  152.4 189.9 %copy-start.23 = (f32[2,2,1024]{2,1,0:T(2,128)S(1)}, f32[2,2,1024]{2,1,0:T(2,128)}, u32[]{:S(2)}) copy-start(f32[2,2,1024]{2,1,0:T(2,128)} %get-tuple-element.56) | copy-start | bytes 49156
  152.4 192.6 %copy-start.14 = (bf16[512,2048]{1,0:T(8,128)(2,1)S(1)}, bf16[512,2048]{1,0:T(8,128)(2,1)}, u32[]{:S(2)}) copy-start(bf16[512,2048]{1,0:T(8,128)(2,1)} %get-tuple-element.67) | copy-start | bytes 6291460
  342.3 3.5 copy-start.9
  345.8 4.0 copy-start.13
  345.8 4.7 copy-start.16
  351.6 8.8 %copy-start.10 = (f32[512,2048]{1,0:T(8,128)}, f32[512,2048]{1,0:T(8,128)S(1)}, u32[]{:S(2)}) copy-start(f32[512,2048]{1,0:T(8,128)S(1)} %fusion.10) | copy-start | bytes 12582916
  351.7 10.9 %copy-start = (bf16[20,64,512]{2,1,0:T(8,128)(2,1)S(1)}, bf16[20,64,512]{2,1,0:T(8,128)(2,1)}, u32[]{:S(2)}) copy-start(bf16[20,64,512]{2,1,0:T(8,128)(2,1)} %get-tuple-element.58.refs_0_) | copy-start | bytes 3932164
  351.7 10.9 %copy-start.1 = (f32[32,512]{1,0:T(8,128)S(1)}, f32[32,512]{1,0:T(8,128)}, u32[]{:S(2)}) copy-start(f32[32,512]{1,0:T(8,128)} %get-tuple-element.92.refs_7_.refs_8_) | copy-start | bytes 196612
  351.7 10.9 %copy-start.2 = (f32[32,512]{1,0:T(8,128)S(1)}, f32[32,512]{1,0:T(8,128)}, u32[]{:S(2)}) copy-start(f32[32,512]{1,0:T(8,128)} %get-tuple-element.93.refs_6_.refs_7_) | copy-start | bytes 196612
  351.7 10.9 %copy-start.3 = (bf16[320,512]{1,0:T(8,128)(2,1)S(1)}, bf16[320,512]{1,0:T(8,128)(2,1)}, u32[]{:S(2)}) copy-start(bf16[320,512]{1,0:T(8,128)(2,1)} %get-tuple-element.63.refs_6_) | copy-start | bytes 983044
  351.7 10.9 %copy-start.4 = (f32[64,1]{1,0:T(8,128)S(1)}, f32[64,1]{1,0:T(8,128)}, u32[]{:S(2)}) copy-start(f32[64,1]{1,0:T(8,128)} %copy.47.refs_8_.refs_9_) | copy-start | bytes 772
  351.7 10.9 %copy-start.5 = (f32[64,1]{1,0:T(8,128)S(1)}, f32[64,1]{1,0:T(8,128)}, u32[]{:S(2)}) copy-start(f32[64,1]{1,0:T(8,128)} %copy.48.refs_9_.refs_10_) | copy-start | bytes 772
  351.7 10.9 %copy-start.6 = (f32[5,4,512]{2,1,0:T(4,128)S(1)}, f32[5,4,512]{2,1,0:T(4,128)}, u32[]{:S(2)}) copy-start(f32[5,4,512]{2,1,0:T(4,128)} %get-tuple-element.60.refs_2_) | copy-start | bytes 122884
  362.6 51.7 %copy-start.15 = (bf16[512,2048]{1,0:T(8,128)(2,1)S(1)}, bf16[512,2048]{1,0:T(8,128)(2,1)}, u32[]{:S(2)}) copy-start(bf16[512,2048]{1,0:T(8,128)(2,1)} %get-tuple-element.67) | copy-start | bytes 6291460
  414.3 8.9 %copy-start.7 = (bf16[4,480,512]{2,1,0:T(8,128)(2,1)}, bf16[4,480,512]{2,1,0:T(8,128)(2,1)S(1)}, u32[]{:S(2)}) copy-start(bf16[4,480,512]{2,1,0:T(8,128)(2,1)S(1)} %get-tuple-element.64) | copy-start | bytes 5898244
  414.4 8.9 %copy-start.11 = (f32[512,2048]{1,0:T(8,128)S(1)}, f32[512,2048]{1,0:T(8,128)}, u32[]{:S(2)}) copy-start(f32[512,2048]{1,0:T(8,128)} %copy-done.10) | copy-start | bytes 12582916
  423.2 3.6 copy-start.8
  426.8 8.1 %copy-start.12 = (f32[512,2048]{1,0:T(8,128)S(1)}, f32[512,2048]{1,0:T(8,128)}, u32[]{:S(2)}) copy-start(f32[512,2048]{1,0:T(8,128)} %copy-done.10) | copy-start | bytes 12582916
  426.8 8.1 %copy-start.26 = (f32[1280,512]{1,0:T(8,128)S(1)}, f32[1280,512]{1,0:T(8,128)}, u32[]{:S(2)}) copy-start(f32[1280,512]{1,0:T(8,128)} %get-tuple-element.54) | copy-start | bytes 7864324
  702.7 7.6 %copy-start.17 = (bf16[1280,1024]{1,0:T(8,128)(2,1)S(1)}, bf16[1280,1024]{1,0:T(8,128)(2,1)}, u32[]{:S(2)}) copy-start(bf16[1280,1024]{1,0:T(8,128)(2,1)} %get-tuple-element.75) | copy-start | bytes 7864324
  715.8 3.6 copy-start.22
  715.8 4.8 copy-start.19
  (3 other events, 7.9 us)

commit v8 on v7

--- a/solution.py
+++ b/solution.py
@@ -1842,7 +1842,11 @@
                 return accum + dot(value, expo.astype(BF))
 
             accum = tile(last, jnp.zeros((HD + 16, rows), F32), True)
-            accum = lax.fori_loop(0, full, lambda where, total: tile(where, total, False), accum)
+            least = (0, PROMPT // KEYS // 2, PROMPT // KEYS, PROMPT // KEYS)[index]
+            for where in range(least):
+                accum = tile(where, accum, False)
+            if index < 2:
+                accum = lax.fori_loop(least, full, lambda where, total: tile(where, total, False), accum)
             total = accum[HD : HD + 1]
             result = accum[:HD] / total
             log = jnp.log(total)
@@ -2043,7 +2047,11 @@
                 return accum + dot(pair[key_rows, here], d_scores)
 
             accum = tile(last, jnp.zeros((HD, rows), F32), True)
-            accum = lax.fori_loop(0, full, lambda where, total: tile(where, total, False), accum)
+            least = (0, PROMPT // KEYS // 2, PROMPT // KEYS, PROMPT // KEYS)[index]
+            for where in range(least):
+                accum = tile(where, accum, False)
+            if index < 2:
+                accum = lax.fori_loop(least, full, lambda where, total: tile(where, total, False), accum)
             cosine = jnp.concatenate([cos_ref[:, cut]] * REP, axis=1)
             sine = jnp.concatenate([sin_ref[:, cut]] * REP, axis=1)
             d_raw, part = through_norm(beside(raw), query_gain[...], cosine, sine, accum * scale)
@@ -2307,7 +2315,7 @@
 
     norm_two_part = jnp.sum(d_normed * hidden * inverse_two, axis=0)
     d_hidden = d_result + norm_back(hidden, inverse_two, gain_two, d_normed)
-    d_hidden_low = d_hidden.astype(BF)
+    d_hidden, d_hidden_low = lax.optimization_barrier((d_hidden, d_hidden.astype(BF)))
     grad_out = dot(mixed, d_hidden_low, ((1,), (0,))).astype(BF)
     d_mixed = dot(w_out_all, d_hidden_low, ((1,), (1,))).astype(BF)
     d_mixed = d_mixed.reshape(KVH, REP, HD, mine)

time: 732 us -> 723 us (0.988)
  no operation moved by 1% of the time
where the time goes in v8:
time: 723 us; the launch traced here: 714 us
  Pallas kernels  639 us (88%)
  other arithmetic  32.3 us (4%)
  matrix products  26 us (4%)
  local copies, waits for them, and re-layouts  14.1 us (2%)
    pallas_call x1, Pallas kernels, reduce_all(): pl.pallas_call(functools.partial(reduce_kernel, parts, planes), out_shape...  263 us
    pallas_call x1, Pallas kernels, feed(): pl.pallas_call(feed_kernel, out_shape=outs, in_specs=[anywhere] * 8 + [pl...  190 us
    pallas_call x1, Pallas kernels, front(): pl.pallas_call(front_kernel, out_shape=[shape((mine, depth), BF), shape((...  141 us
    pallas_call x1, Pallas kernels, back(): pl.pallas_call(back_kernel, out_shape=[shape((4, columns, mine), BF), sha...  45.4 us
    dot_general x3, matrix products, dot(): lax.dot_general(left, right, (dims, ((), ())), preferred_element_type=F32)  17.6 us

profile of v8, /device:TPU:0, one launch (start us, length us, event | category | flops | bytes accessed | tf_op | source)
XLA Modules:
  0.0 713.8 jit_solution(11270704424083507604)
XLA Ops:
  2.5 1.4 copy.47.refs_8_.refs_9_
  3.8 1.4 copy.48.refs_9_.refs_10_
  5.2 1.4 copy.44
  7.7 1.1 copy.46
  8.8 1.3 pad_maximum_fusion.refs_1_
  10.7 141.0 %front.1 = (bf16[512,2048]{1,0:T(8,128)(2,1)}, bf16[512,2048]{1,0:T(8,128)(2,1)}, f32[20,64,512]{2,1,0:T(8,128)}, bf16[20,64,512]{2,1,0:T(8,128)(2,1)}, bf16[320...) custom-call(bf16[1024,1024]{1,0:T(8,128)(2,1)} %refs_0_.1, ...), custom_call_target="tpu_custom_call" | custom-call | tf_op jit(solution)/shard_map/front/pallas_call | solution.py:1922
  152.4 189.7 %feed_forward.1 = (bf16[8,256,2048]{2,1,0:T(8,128)(2,1)}, bf16[8,256,1280]{2,1,0:T(8,128)(2,1)}, bf16[8,256,1280]{2,1,0:T(8,128)(2,1)}, bf16[8,256,1280]{2,1,0:T...) custom-call(bf16[512,2048]{1,0:T(8,128)(2,1)} %get-tuple-element.47., ...), custom_call_target="tpu_custom_call" | custom-call | tf_op jit(solution)/shard_map/feed_forward/pallas_call | solution.py:1523
  342.2 2.7 multiply_reduce_fusion
  345.6 4.0 fusion.13
  350.3 3.3 fusion.22
  353.7 4.5 convert_multiply_fusion.4
  358.2 2.1 reduce_sum.65.refs_3_
  360.4 45.4 %attend_back.1 = (bf16[4,480,512]{2,1,0:T(8,128)(2,1)S(1)}, f32[64,1]{1,0:T(8,128)S(1)}, f32[64,1]{1,0:T(8,128)S(1)}) custom-call(bf16[20,64,512]{2,1,0:T(8,128)(2,1)S(1)} %copy-done, bf16[20,64,512]{2,1,0:T(8,128)(2,1)S(1)} %bitcast.69, f32[5,4,512]{2,1,0:T(4,128)S(1)} %copy-done.6, f32[5,4,512]{2,1,0:T(4,128)S(1)} %reduce_sum.65.refs_3_, ...), custom_call_target="tpu_custom_call" | custom-call | tf_op jit(solution)/shard_map/attend_back/pallas_call | solution.py:2103
  405.9 8.5 %fusion.8 = (f32[512]{0:T(512)S(1)}, f32[2048]{0:T(1024)S(1)}, f32[512,2048,1]{1,0,2:T(8,128)S(1)}) fusion(bf16[512,2048]{1,0:T(8,128)(2,1)S(1)} %copy-done.13, f32[2048]{0:T(1024)S(1)} %bitcast.80, f32[512]{0:T(512)S(1)} %get-tuple-element.101, bf16[4,480,512]{2,1,0:T(8,128)(2,1)S(1)} %get-tuple-element.67, bf16[4,2048,480]{2,1,0:T(8,128)(2,1)} %bitcast.88), kind=kOutput, calls=%fused_computation.14 | convolution fusion | flops 4033869312 | bytes 16142336 | tf_op jit(solution)/shard_map/dot_general | solution.py:29
  414.4 2.6 fusion.6.refs_7_
  418.0 8.4 %convolution_convert_fusion.1.refs_5_ = bf16[4,480,2048]{2,1,0:T(8,128)(2,1)} fusion(bf16[4,480,512]{2,1,0:T(8,128)(2,1)S(1)} %copy-done.8, bf16[512,2048]{1,0:T(8,128)(2,1)} %get-tuple-element.68), kind=kOutput, calls=%fused_computation.5 | convolution fusion | flops 4030464000 | bytes 11927552 | tf_op jit(solution)/shard_map/dot_general | solution.py:2350
  426.4 4.6 convolution_convert_fusion
  431.0 263.2 %reduce_grads.1 = (bf16[1024,2560]{1,0:T(8,128)(2,1)}, bf16[320,1024]{1,0:T(8,128)(2,1)}, bf16[480,1024]{1,0:T(8,128)(2,1)}, bf16[1280,1024]{1,0:T(8,128)(2,1)},...) custom-call(bf16[2048,2048]{1,0:T(8,128)(2,1)} %bitcast.71, bf16[2048,2560]{1,0:T(8,128)(2,1)} %bitcast.70, ...), custom_call_target="tpu_custom_call" | custom-call | tf_op jit(solution)/shard_map/reduce_grads/pallas_call | solution.py:652
  694.2 7.6 %slice_convert_fusion = (f32[1024,1280]{1,0:T(8,128)}, f32[1024,1280]{1,0:T(8,128)}) fusion(bf16[1024,2560]{1,0:T(8,128)(2,1)} %get-tuple-element.78), kind=kLoop, calls=%fused_computation.26 | loop fusion | flops 2621440 | bytes 15728640 | tf_op jit(solution)/shard_map/convert_element_type | solution.py:2392
  701.8 3.0 convert_element_type.72
  704.8 2.5 convert_element_type.68
  707.5 1.2 slice.44
  709.6 1.2 convert_element_type.69
  712.1 1.3 copy.61
  (87 shorter events, 8.4 us)
Async XLA Ops:
  0.6 9.5 %copy-start.25 = (f32[1024]{0:T(1024)S(1)}, f32[1024]{0:T(1024)}, u32[]{:S(2)}) copy-start(f32[1024]{0:T(1024)} %param.18) | copy-start | bytes 12292
  0.7 9.5 %copy-start.24 = (f32[1024]{0:T(1024)S(1)}, f32[1024]{0:T(1024)}, u32[]{:S(2)}) copy-start(f32[1024]{0:T(1024)} %param.25) | copy-start | bytes 12292
  152.4 189.7 %copy-start.23 = (f32[2,2,1024]{2,1,0:T(2,128)S(1)}, f32[2,2,1024]{2,1,0:T(2,128)}, u32[]{:S(2)}) copy-start(f32[2,2,1024]{2,1,0:T(2,128)} %get-tuple-element.58) | copy-start | bytes 49156
  152.4 192.5 %copy-start.12 = (bf16[512,2048]{1,0:T(8,128)(2,1)S(1)}, bf16[512,2048]{1,0:T(8,128)(2,1)}, u32[]{:S(2)}) copy-start(bf16[512,2048]{1,0:T(8,128)(2,1)} %get-tuple-element.70) | copy-start | bytes 6291460
  345.6 4.0 copy-start.11
  345.6 4.7 copy-start.14
  345.6 8.0 %slice-start = ((s8[5242880]{0:T(1024)(128)(4,1)}), s8[4194304]{0:T(1024)(128)(4,1)S(1)}, s32[]{:S(2)}) async-start(s8[5242880]{0:T(1024)(128)(4,1)} %bitcast.89), calls=%async_computation | async-start | bytes 8388608
  353.6 4.6 copy-start.16
  353.6 6.7 copy-start
  353.6 6.7 copy-start.1
  353.6 6.7 copy-start.2
  353.7 6.7 copy-start.3
  353.7 6.7 copy-start.4
  353.7 6.7 copy-start.5
  353.7 6.7 copy-start.6
  360.4 45.4 %copy-start.13 = (bf16[512,2048]{1,0:T(8,128)(2,1)S(1)}, bf16[512,2048]{1,0:T(8,128)(2,1)}, u32[]{:S(2)}) copy-start(bf16[512,2048]{1,0:T(8,128)(2,1)} %get-tuple-element.70) | copy-start | bytes 6291460
  405.8 8.6 %copy-start.7 = (bf16[4,480,512]{2,1,0:T(8,128)(2,1)}, bf16[4,480,512]{2,1,0:T(8,128)(2,1)S(1)}, u32[]{:S(2)}) copy-start(bf16[4,480,512]{2,1,0:T(8,128)(2,1)S(1)} %get-tuple-element.67) | copy-start | bytes 5898244
  405.9 8.6 %copy-start.10 = (f32[512,2048]{1,0:T(8,128)S(1)}, f32[512,2048]{1,0:T(8,128)}, u32[]{:S(2)}) copy-start(f32[512,2048]{1,0:T(8,128)} %get-tuple-element.73) | copy-start | bytes 12582916
  414.4 3.6 copy-start.8
  418.0 8.4 %copy-start.17 = (bf16[512,2048]{1,0:T(8,128)(2,1)S(1)}, bf16[512,2048]{1,0:T(8,128)(2,1)}, u32[]{:S(2)}) copy-start(bf16[512,2048]{1,0:T(8,128)(2,1)} %copy-done.16) | copy-start | bytes 6291460
  418.0 8.4 %copy-start.27 = (f32[1280,512]{1,0:T(8,128)S(1)}, f32[1280,512]{1,0:T(8,128)}, u32[]{:S(2)}) copy-start(f32[1280,512]{1,0:T(8,128)} %get-tuple-element.56) | copy-start | bytes 7864324
  694.2 7.6 %copy-start.15 = (bf16[1280,1024]{1,0:T(8,128)(2,1)S(1)}, bf16[1280,1024]{1,0:T(8,128)(2,1)}, u32[]{:S(2)}) copy-start(bf16[1280,1024]{1,0:T(8,128)(2,1)} %get-tuple-element.79) | copy-start | bytes 7864324
  707.3 3.6 copy-start.22
  707.3 4.8 copy-start.19
  (6 other events, 17.9 us)

commit v9 on v8

--- a/solution.py
+++ b/solution.py
@@ -1714,6 +1714,7 @@
     project.first()
     for copy in sent_tokens:
         copy.start()
+    output.to_row.start()
     chunks[0][0].start()
     for copy in own_copies:
         copy.wait()
@@ -1759,7 +1760,6 @@
 
     project.plane_in()
     project.far_in(0)
-    output.to_row.start()
     project_col(me)
     project.mate_in(0, 3)
     project_col(2 * group + 1 - side)
@@ -1800,6 +1800,7 @@
     output.to_far[0].start()
     output.to_mate[0].start()
     chunks[1][0].start()
+    output.row_in()
 
     @pl.loop(0, raw.shape[0])
     def _(head):
@@ -1809,15 +1810,15 @@
     for index in range(4):
         to_row[index].wait_recv()
         passed[index].start()
-    output.row_in()
     chunks[2][0].start()
+    output.plane_in()
     pass_on(0)
     for index in range(4):
         to_mate[index].wait_recv()
         passed[index].wait_recv()
     chunks[3][0].start()
-    output.plane_in()
     output.far_in(0)
+    output.far_in(1)
 
     firsts = [member, pieces - 1 - member, pieces + member, 2 * pieces - 1 - member]
     rows = REP * span
@@ -1857,7 +1858,6 @@
 
         @pl.when(head == 2)
         def _():
-            output.far_in(1)
             output.far_in(2)
 
         for number, index in ((1, 1), (3, 2)):

time: 723 us -> 717 us (level)
  no operation moved by 1% of the time
where the time goes in v9:
time: 717 us; the launch traced here: 708 us
  Pallas kernels  633 us (88%)
  other arithmetic  32.3 us (5%)
  matrix products  26 us (4%)
  local copies, waits for them, and re-layouts  14.1 us (2%)
    pallas_call x1, Pallas kernels, reduce_all(): pl.pallas_call(functools.partial(reduce_kernel, parts, planes), out_shape...  263 us
    pallas_call x1, Pallas kernels, feed(): pl.pallas_call(feed_kernel, out_shape=outs, in_specs=[anywhere] * 8 + [pl...  189 us
    pallas_call x1, Pallas kernels, front(): pl.pallas_call(front_kernel, out_shape=[shape((mine, depth), BF), shape((...  134 us
    pallas_call x1, Pallas kernels, back(): pl.pallas_call(back_kernel, out_shape=[shape((4, columns, mine), BF), sha...  46.3 us
    dot_general x3, matrix products, dot(): lax.dot_general(left, right, (dims, ((), ())), preferred_element_type=F32)  17.6 us

profile of v9, /device:TPU:0, one launch (start us, length us, event | category | flops | bytes accessed | tf_op | source)
XLA Modules:
  0.0 707.7 jit_solution(254104034502488906)
XLA Ops:
  2.5 1.4 copy.47.refs_8_.refs_9_
  3.8 1.4 copy.48.refs_9_.refs_10_
  5.2 1.4 copy.44
  7.7 1.1 copy.46
  8.8 1.3 pad_maximum_fusion.refs_1_
  10.7 134.3 %front.1 = (bf16[512,2048]{1,0:T(8,128)(2,1)}, bf16[512,2048]{1,0:T(8,128)(2,1)}, f32[20,64,512]{2,1,0:T(8,128)}, bf16[20,64,512]{2,1,0:T(8,128)(2,1)}, bf16[320...) custom-call(bf16[1024,1024]{1,0:T(8,128)(2,1)} %refs_0_.1, ...), custom_call_target="tpu_custom_call" | custom-call | tf_op jit(solution)/shard_map/front/pallas_call | solution.py:1922
  145.7 189.3 %feed_forward.1 = (bf16[8,256,2048]{2,1,0:T(8,128)(2,1)}, bf16[8,256,1280]{2,1,0:T(8,128)(2,1)}, bf16[8,256,1280]{2,1,0:T(8,128)(2,1)}, bf16[8,256,1280]{2,1,0:T...) custom-call(bf16[512,2048]{1,0:T(8,128)(2,1)} %get-tuple-element.47., ...), custom_call_target="tpu_custom_call" | custom-call | tf_op jit(solution)/shard_map/feed_forward/pallas_call | solution.py:1523
  335.0 2.7 multiply_reduce_fusion
  338.5 4.0 fusion.13
  343.2 3.3 fusion.22
  346.6 4.5 convert_multiply_fusion.4
  351.1 2.1 reduce_sum.65.refs_3_
  353.3 46.3 %attend_back.1 = (bf16[4,480,512]{2,1,0:T(8,128)(2,1)S(1)}, f32[64,1]{1,0:T(8,128)S(1)}, f32[64,1]{1,0:T(8,128)S(1)}) custom-call(bf16[20,64,512]{2,1,0:T(8,128)(2,1)S(1)} %copy-done, bf16[20,64,512]{2,1,0:T(8,128)(2,1)S(1)} %bitcast.69, f32[5,4,512]{2,1,0:T(4,128)S(1)} %copy-done.6, f32[5,4,512]{2,1,0:T(4,128)S(1)} %reduce_sum.65.refs_3_, ...), custom_call_target="tpu_custom_call" | custom-call | tf_op jit(solution)/shard_map/attend_back/pallas_call | solution.py:2103
  399.7 8.5 %fusion.8 = (f32[512]{0:T(512)S(1)}, f32[2048]{0:T(1024)S(1)}, f32[512,2048,1]{1,0,2:T(8,128)S(1)}) fusion(bf16[512,2048]{1,0:T(8,128)(2,1)S(1)} %copy-done.13, f32[2048]{0:T(1024)S(1)} %bitcast.80, f32[512]{0:T(512)S(1)} %get-tuple-element.101, bf16[4,480,512]{2,1,0:T(8,128)(2,1)S(1)} %get-tuple-element.67, bf16[4,2048,480]{2,1,0:T(8,128)(2,1)} %bitcast.88), kind=kOutput, calls=%fused_computation.14 | convolution fusion | flops 4033869312 | bytes 16142336 | tf_op jit(solution)/shard_map/dot_general | solution.py:29
  408.2 2.6 fusion.6.refs_7_
  411.8 8.4 %convolution_convert_fusion.1.refs_5_ = bf16[4,480,2048]{2,1,0:T(8,128)(2,1)} fusion(bf16[4,480,512]{2,1,0:T(8,128)(2,1)S(1)} %copy-done.8, bf16[512,2048]{1,0:T(8,128)(2,1)} %get-tuple-element.68), kind=kOutput, calls=%fused_computation.5 | convolution fusion | flops 4030464000 | bytes 11927552 | tf_op jit(solution)/shard_map/dot_general | solution.py:2350
  420.2 4.6 convolution_convert_fusion
  424.8 263.2 %reduce_grads.1 = (bf16[1024,2560]{1,0:T(8,128)(2,1)}, bf16[320,1024]{1,0:T(8,128)(2,1)}, bf16[480,1024]{1,0:T(8,128)(2,1)}, bf16[1280,1024]{1,0:T(8,128)(2,1)},...) custom-call(bf16[2048,2048]{1,0:T(8,128)(2,1)} %bitcast.71, bf16[2048,2560]{1,0:T(8,128)(2,1)} %bitcast.70, ...), custom_call_target="tpu_custom_call" | custom-call | tf_op jit(solution)/shard_map/reduce_grads/pallas_call | solution.py:652
  688.0 7.6 %slice_convert_fusion = (f32[1024,1280]{1,0:T(8,128)}, f32[1024,1280]{1,0:T(8,128)}) fusion(bf16[1024,2560]{1,0:T(8,128)(2,1)} %get-tuple-element.78), kind=kLoop, calls=%fused_computation.26 | loop fusion | flops 2621440 | bytes 15728640 | tf_op jit(solution)/shard_map/convert_element_type | solution.py:2392
  695.6 3.0 convert_element_type.72
  698.6 2.5 convert_element_type.68
  701.3 1.2 slice.44
  703.4 1.2 convert_element_type.69
  705.9 1.3 copy.61
  (87 shorter events, 8.4 us)
Async XLA Ops:
  0.6 9.5 %copy-start.25 = (f32[1024]{0:T(1024)S(1)}, f32[1024]{0:T(1024)}, u32[]{:S(2)}) copy-start(f32[1024]{0:T(1024)} %param.18) | copy-start | bytes 12292
  0.7 9.5 %copy-start.24 = (f32[1024]{0:T(1024)S(1)}, f32[1024]{0:T(1024)}, u32[]{:S(2)}) copy-start(f32[1024]{0:T(1024)} %param.25) | copy-start | bytes 12292
  145.7 189.3 %copy-start.23 = (f32[2,2,1024]{2,1,0:T(2,128)S(1)}, f32[2,2,1024]{2,1,0:T(2,128)}, u32[]{:S(2)}) copy-start(f32[2,2,1024]{2,1,0:T(2,128)} %get-tuple-element.58) | copy-start | bytes 49156
  145.7 192.0 %copy-start.12 = (bf16[512,2048]{1,0:T(8,128)(2,1)S(1)}, bf16[512,2048]{1,0:T(8,128)(2,1)}, u32[]{:S(2)}) copy-start(bf16[512,2048]{1,0:T(8,128)(2,1)} %get-tuple-element.70) | copy-start | bytes 6291460
  338.5 4.0 copy-start.11
  338.5 4.7 copy-start.14
  338.5 8.0 %slice-start = ((s8[5242880]{0:T(1024)(128)(4,1)}), s8[4194304]{0:T(1024)(128)(4,1)S(1)}, s32[]{:S(2)}) async-start(s8[5242880]{0:T(1024)(128)(4,1)} %bitcast.89), calls=%async_computation | async-start | bytes 8388608
  346.5 4.6 copy-start.16
  346.5 6.7 copy-start
  346.5 6.7 copy-start.1
  346.5 6.7 copy-start.2
  346.5 6.7 copy-start.3
  346.5 6.7 copy-start.4
  346.5 6.7 copy-start.5
  346.5 6.7 copy-start.6
  353.3 46.4 %copy-start.13 = (bf16[512,2048]{1,0:T(8,128)(2,1)S(1)}, bf16[512,2048]{1,0:T(8,128)(2,1)}, u32[]{:S(2)}) copy-start(bf16[512,2048]{1,0:T(8,128)(2,1)} %get-tuple-element.70) | copy-start | bytes 6291460
  399.6 8.6 %copy-start.7 = (bf16[4,480,512]{2,1,0:T(8,128)(2,1)}, bf16[4,480,512]{2,1,0:T(8,128)(2,1)S(1)}, u32[]{:S(2)}) copy-start(bf16[4,480,512]{2,1,0:T(8,128)(2,1)S(1)} %get-tuple-element.67) | copy-start | bytes 5898244
  399.7 8.6 %copy-start.10 = (f32[512,2048]{1,0:T(8,128)S(1)}, f32[512,2048]{1,0:T(8,128)}, u32[]{:S(2)}) copy-start(f32[512,2048]{1,0:T(8,128)} %get-tuple-element.73) | copy-start | bytes 12582916
  408.2 3.6 copy-start.8
  411.8 8.4 %copy-start.17 = (bf16[512,2048]{1,0:T(8,128)(2,1)S(1)}, bf16[512,2048]{1,0:T(8,128)(2,1)}, u32[]{:S(2)}) copy-start(bf16[512,2048]{1,0:T(8,128)(2,1)} %copy-done.16) | copy-start | bytes 6291460
  411.8 8.4 %copy-start.27 = (f32[1280,512]{1,0:T(8,128)S(1)}, f32[1280,512]{1,0:T(8,128)}, u32[]{:S(2)}) copy-start(f32[1280,512]{1,0:T(8,128)} %get-tuple-element.56) | copy-start | bytes 7864324
  688.0 7.6 %copy-start.15 = (bf16[1280,1024]{1,0:T(8,128)(2,1)S(1)}, bf16[1280,1024]{1,0:T(8,128)(2,1)}, u32[]{:S(2)}) copy-start(bf16[1280,1024]{1,0:T(8,128)(2,1)} %get-tuple-element.79) | copy-start | bytes 7864324
  701.1 3.6 copy-start.22
  701.1 4.8 copy-start.19
  (6 other events, 17.9 us)
